TPU v7x, 128 devices: a whole 4x4x4 slice. The times are simulated.
128 devices in a mesh: gx: 8 (over y, core), gy: 16 (over z, x).
Axes of the slice: x: 4, y: 4, z: 4, core: 2. Of those that a mesh axis runs over, the one named last changes fastest.
Arguments:
- features: bfloat16 [128, 256, 96, 128], P('gx', 'gy'), may hold values from -160 to 160
- cotangent: bfloat16 [128, 256, 96, 128], P('gx', 'gy'), may hold values from -6 to 6
- weight: bfloat16 [27, 96, 96], replicated, may hold values from -0.125 to 0.125
- bn_gain: float32 [96], replicated, may hold values from 0.5 to 2
- bn_shift: float32 [96], replicated, may hold values from -3 to 3
- voxel_mask: int32 [128, 256, 128], P('gx', 'gy'), may hold values 0 or 1
- brick_live: int32 [8, 16, 8], P('gx', 'gy'), may hold values from 0 to 1, as said below
Outputs:
- input_grad: bfloat16 [128, 256, 96, 128], P('gx', 'gy')
- weight_grad: float32 [27, 96, 96], replicated
- gain_grad: float32 [96], replicated
- shift_grad: float32 [96], replicated
Inputs may be any that keep to these rules, and one draw needn't show every extreme that they name: `brick_live`: along gy, the two tiles of one gx index whose gy indices differ by 8 hold exactly 2 live bricks together. In every gx index, the tiles with gy index 0 and 1 hold 1 each, and so do those with gy index 8 and 9, whose live bricks stand at the same vertical positions. At least one tile with gy index 2 to 7 holds 2.
All inputs are finite; a program needn't handle non-finite values. No bound on the sum of `voxel_mask` on one device may be relied on, other than what follows from the above.
Results may differ from a plain program's by a relative error of at most 0.0049.
Values may be sent and summed in bfloat16 or wider, within the bound.
No kernel may reach another device: no remote copies, remote signals or barrier semaphores. Data moves between devices by JAX's collectives and lax.ppermute only.
A program may use at most 256 MiB of HBM per device.

v0:
```python
import jax
import jax.numpy as jnp
from jax import lax
from jax.sharding import PartitionSpec as P

BRICK = 16
MOST_LIVE = 2


def padded(cells, sides, width):
    for axis, dim in sides:
        count = lax.axis_size(axis)
        ends = count - 1
        head = lax.slice_in_dim(cells, 0, width, axis=dim)
        tail = lax.slice_in_dim(cells, cells.shape[dim] - width, cells.shape[dim], axis=dim)
        cells = jnp.concatenate(
            [
                lax.ppermute(tail, axis, [(i, (i + 1) % count) for i in range(ends)]),
                cells,
                lax.ppermute(head, axis, [((i + 1) % count, i) for i in range(ends)]),
            ],
            axis=dim,
        )
    return cells


def unfold(padded_brick, brick_edge):
    shifted = [
        padded_brick[
            off_x : off_x + brick_edge, off_y : off_y + brick_edge, :, off_z : off_z + brick_edge
        ]
        for off_x in range(3)
        for off_y in range(3)
        for off_z in range(3)
    ]
    stacked = jnp.stack(shifted, 0)
    return jnp.transpose(stacked, (1, 2, 4, 0, 3)).reshape(
        brick_edge**3, 27 * padded_brick.shape[2]
    )


def margin_bricks(values_tile, slot_ids, brick_edge):
    widened = padded(values_tile, (("gx", 0), ("gy", 1)), 1)
    widened = jnp.pad(widened, ((0, 0), (0, 0), (0, 0), (1, 1)))

    def extract(slot_index):
        return lax.dynamic_slice_in_dim(widened, slot_index * brick_edge, brick_edge + 2, 3)

    return jax.vmap(extract)(slot_ids)


def brick_rows(values_tile, slot_index, brick_edge):
    brick_piece = lax.dynamic_slice_in_dim(values_tile, slot_index * brick_edge, brick_edge, 3)
    return jnp.transpose(brick_piece, (0, 1, 3, 2)).reshape(brick_edge**3, values_tile.shape[2])


def brick_mask(mask_tile, slot_index, brick_edge):
    return lax.dynamic_slice_in_dim(mask_tile, slot_index * brick_edge, brick_edge, 2).reshape(
        brick_edge**3
    )


def place_bricks(tile_shape, bricks, slot_ids, slot_valid, brick_edge):
    assembled = jnp.zeros(tile_shape, bricks.dtype)
    for slot_index in range(bricks.shape[0]):
        brick_piece = jnp.where(
            slot_valid[slot_index], bricks[slot_index], jnp.zeros_like(bricks[slot_index])
        )
        brick_piece = jnp.transpose(
            brick_piece.reshape(brick_edge, brick_edge, brick_edge, tile_shape[2]), (0, 1, 3, 2)
        )
        assembled = lax.dynamic_update_slice_in_dim(
            assembled, brick_piece, slot_ids[slot_index] * brick_edge, 3
        )
    return assembled


def body(features, cotangent, weight, bn_gain, bn_shift, voxel_mask, brick_live):
    brick_edge = BRICK
    capacity = MOST_LIVE
    live_flags = brick_live[0, 0]
    live_count = jnp.sum(live_flags)
    slot_ids = jnp.argsort(1 - live_flags, stable=True)[:capacity]
    slot_valid = jnp.arange(capacity) < live_count
    column_live = jnp.repeat(live_flags, brick_edge)
    mask_tile = (voxel_mask * column_live[None, None, :]).astype(jnp.float32)
    masked = jnp.where(mask_tile[:, :, None, :] > 0, features, jnp.zeros_like(features))
    margins = margin_bricks(masked, slot_ids, brick_edge)
    grad_bricks = jax.vmap(lambda slot_index: brick_rows(cotangent, slot_index, brick_edge))(
        slot_ids
    )
    mask_bricks = jax.vmap(lambda slot_index: brick_mask(mask_tile, slot_index, brick_edge))(
        slot_ids
    ).astype(jnp.bfloat16)
    work_inputs, work_grads, work_masks = (margins, grad_bricks, mask_bricks)
    weight_rows = weight.reshape(27 * weight.shape[1], weight.shape[2])
    weight_back = jnp.transpose(weight[::-1], (0, 2, 1)).reshape(
        27 * weight.shape[1], weight.shape[2]
    )

    def forward_one(padded_brick):
        return jnp.dot(
            unfold(padded_brick, brick_edge), weight_rows, preferred_element_type=jnp.float32
        )

    preact = lax.map(forward_one, work_inputs)
    mask_values = work_masks.astype(jnp.float32)[:, :, None]
    sum_pre, sum_sq, voxels = lax.psum(
        (
            jnp.sum(mask_values * preact, axis=(0, 1)),
            jnp.sum(mask_values * preact * preact, axis=(0, 1)),
            jnp.sum(mask_tile),
        ),
        ("gx", "gy"),
    )
    bn_mean = sum_pre / voxels
    bn_var = sum_sq / voxels - bn_mean * bn_mean
    inv_std = lax.rsqrt(bn_var + 1e-05)
    normed = (preact - bn_mean) * inv_std
    zed = bn_gain * normed + bn_shift
    sigma = jax.nn.sigmoid(zed)
    grad_z = mask_values * work_grads.astype(jnp.float32) * (sigma * (1.0 + zed * (1.0 - sigma)))
    sum_grad, sum_cross = lax.psum(
        (jnp.sum(grad_z, axis=(0, 1)), jnp.sum(grad_z * normed, axis=(0, 1))), ("gx", "gy")
    )
    grad_pre = (
        mask_values * bn_gain * inv_std * (grad_z - sum_grad / voxels - normed * sum_cross / voxels)
    ).astype(jnp.bfloat16)

    def weight_step(running, inputs_pair):
        padded_brick, grad_block = inputs_pair
        columns = unfold(padded_brick, brick_edge)
        term = lax.dot_general(
            columns, grad_block, (((0,), (0,)), ((), ())), preferred_element_type=jnp.float32
        )
        return (running + term, None)

    weight_local, unused = lax.scan(
        weight_step, jnp.zeros(weight_rows.shape, jnp.float32), (work_inputs, grad_pre)
    )
    grad_tile = place_bricks(features.shape, grad_pre, slot_ids, slot_valid, brick_edge)
    back_margins = margin_bricks(grad_tile, slot_ids, brick_edge)

    def backward_one(padded_brick):
        product = jnp.dot(
            unfold(padded_brick, brick_edge), weight_back, preferred_element_type=jnp.float32
        )
        return product.astype(jnp.bfloat16)

    input_work = lax.map(backward_one, back_margins)
    input_tile = place_bricks(features.shape, input_work, slot_ids, slot_valid, brick_edge)
    input_grad = jnp.where(mask_tile[:, :, None, :] > 0, input_tile, jnp.zeros_like(input_tile))
    weight_total = lax.psum(weight_local, ("gx", "gy"))
    scale = 1.0 / jnp.sqrt(voxels)
    weight_grad = (weight_total * scale).reshape(weight.shape)
    return (input_grad, weight_grad, sum_cross * scale, sum_grad * scale)


def solution(mesh):
    return jax.shard_map(
        body,
        mesh=mesh,
        in_specs=(
            P("gx", "gy", None, None),
            P("gx", "gy", None, None),
            P(),
            P(),
            P(),
            P("gx", "gy", None),
            P("gx", "gy", None),
        ),
        out_specs=(P("gx", "gy", None, None), P(), P(), P()),
        check_vma=False,
    )
```

profile of v0, /device:TPU:15, one launch (start us, length us, event | category | flops | bytes accessed | tf_op | source)
XLA Modules:
  0.0 1597.2 jit_solution(15725336460455798865)
XLA Ops:
  29.1 11.7 copy.59
  70.3 19.8 %fusion.97 = bf16[18,18,96,130]{3,2,1,0:T(8,128)(2,1)} fusion(bf16[18,1,96,128]{3,2,1,0:T(8,128)(2,1)S(1)} %collective-permute-done.3, bf16[18,1,96,128]{3,2,1,0:T(8,128)(2,1)S(1)} %collective-permute-done.2, bf16[1,16,96,128]{3,2,1,0:T(8,128)(2,1)S(1)} %collective-permute-done.1, bf16[16,16,96,128]{3,2,1,0:T(8,128)(2,1)} %copy-done.3, ...), kind=kLoop, calls=%fused_computation.196 | loop fusion | flops 72783360 | bytes 16049664 | tf_op jit(solution)/shard_map/concatenate | solution.py:16
  92.5 40.3 %while.35 = (s32[]{:T(128)}, bf16[18,18,96,130]{3,2,1,0:T(8,128)(2,1)}, s32[2,4]{1,0:T(2,128)S(1)}, bf16[2,18,18,96,18]{3,4,2,1,0:T(8,128)(2,1)}, s32[]{:T(128)}) while((s32[]{:T(128)}, bf16[18,18,96,130]{3,2,1,0:T(8,128)(2,1)}, s32[2,4]{1,0:T(2,128)S(1)}, bf16[2,18,18,96,18]{3,4,2,1,0:T(8,128)(2,1)}, s32[]{:T(128)}) %tuple.99), condition=%wide.while_cond, body=%wide.while_body.sunk | while | flops 2 | bytes 7589997 | solution.py:47
  133.3 239.0 %while.33 = (s32[]{:T(128)}, f32[2,4096,96]{1,2,0:T(8,128)}, bf16[2,18,18,96,18]{3,4,2,1,0:T(8,128)(2,1)}, bf16[2592,96]{1,0:T(8,128)(2,1)S(1)}, s32[]{:T(128)}) while((s32[]{:T(128)}, f32[2,4096,96]{1,2,0:T(8,128)}, bf16[2,18,18,96,18]{3,4,2,1,0:T(8,128)(2,1)}, bf16[2592,96]{1,0:T(8,128)(2,1)S(1)}, s32[]{:T(128)}) %tuple.118), condition=%wide.region_3.4_spmd, body=%wide.region_2.3_spmd.sunk | while | flops 2038431744 | bytes 252560976 | solution.py:106
  158.5 26.5 %copy.83 = bf16[16,16,16,27,96]{4,3,2,1,0:T(8,128)(2,1)} copy(bf16[16,16,16,27,96]{4,2,1,0,3:T(8,128)(2,1)} %bitcast.588) | data formatting | bytes 42467328 | tf_op jit(solution)/shard_map/while/body/eval_jaxpr/transpose | solution.py:37
  185.0 54.7 %reshape.157 = bf16[4096,2592]{1,0:T(8,128)(2,1)} reshape(bf16[16,16,16,27,96]{4,3,2,1,0:T(8,128)(2,1)} %copy.83) | data formatting | bytes 42467328 | tf_op jit(solution)/shard_map/while/body/eval_jaxpr/reshape | solution.py:37
  239.8 12.9 fusion.237
  277.8 26.5 %copy.83 = bf16[16,16,16,27,96]{4,3,2,1,0:T(8,128)(2,1)} copy(bf16[16,16,16,27,96]{4,2,1,0,3:T(8,128)(2,1)} %bitcast.588) | data formatting | bytes 42467328 | tf_op jit(solution)/shard_map/while/body/eval_jaxpr/transpose | solution.py:37
  304.3 54.7 %reshape.157 = bf16[4096,2592]{1,0:T(8,128)(2,1)} reshape(bf16[16,16,16,27,96]{4,3,2,1,0:T(8,128)(2,1)} %copy.83) | data formatting | bytes 42467328 | tf_op jit(solution)/shard_map/while/body/eval_jaxpr/reshape | solution.py:37
  359.0 12.9 fusion.237
  381.2 63.7 %all-reduce.4 = (f32[96]{0:T(128)S(1)}, f32[]{:T(128)}, f32[96]{0:T(128)S(1)}) all-reduce(f32[96]{0:T(128)S(1)} %get-tuple-element.143, f32[]{:T(128)} %get-tuple-element.194, f32[96]{0:T(128)S(1)} %get-tuple-element.142), channel_id=1, replica_groups=mesh['gx'=8,'gy'=16] {'gx','gy'}, use_global_device_ids=true, to_apply=%region_9.10 | all-reduce | flops 193 | bytes 1544 | tf_op jit(solution)/shard_map/psum | solution.py:108
  453.7 62.6 %all-reduce.3 = (f32[96]{0:T(128)S(1)}, f32[96]{0:T(128)S(1)}) all-reduce(f32[96]{0:T(128)S(1)} %get-tuple-element.145, f32[96]{0:T(128)S(1)} %get-tuple-element.144), channel_id=1, replica_groups=mesh['gx'=8,'gy'=16] {'gx','gy'}, use_global_device_ids=true, to_apply=%region_13.14 | all-reduce | flops 192 | bytes 1536 | tf_op jit(solution)/shard_map/psum | solution.py:123
  542.9 81.5 %dynamic_update_slice.20 = bf16[16,16,96,128]{3,2,1,0:T(8,128)(2,1)} dynamic-update-slice(bf16[16,16,96,128]{3,2,1,0:T(8,128)(2,1)} %broadcast.67.clone, bf16[16,16,96,16]{3,2,1,0:T(8,128)(2,1)} %copy.62, s32[]{:T(128)} %constant.15.clone.1, s32[]{:T(128)} %constant.15.clone.1, s32[]{:T(128)} %constant.15.clone.1, s32[]{:T(128)S(6)} %select_n.67) | dynamic-update-slice | bytes 1572868 | tf_op jit(solution)/shard_map/dynamic_update_slice | solution.py:72
  624.4 81.5 %dynamic_update_slice.21 = bf16[16,16,96,128]{3,2,1,0:T(8,128)(2,1)} dynamic-update-slice(bf16[16,16,96,128]{3,2,1,0:T(8,128)(2,1)} %dynamic_update_slice.20, bf16[16,16,96,16]{3,2,1,0:T(8,128)(2,1)} %copy.63, s32[]{:T(128)} %constant.15.clone.1, s32[]{:T(128)} %constant.15.clone.1, s32[]{:T(128)} %constant.15.clone.1, s32[]{:T(128)S(6)} %select_n.71) | dynamic-update-slice | bytes 1572868 | tf_op jit(solution)/shard_map/dynamic_update_slice | solution.py:72
  713.3 234.0 %while.37 = (s32[]{:T(128)}, f32[2592,96]{0,1:T(8,128)}, bf16[2,18,18,96,18]{3,4,2,1,0:T(8,128)(2,1)}, bf16[2,4096,96]{2,1,0:T(8,128)(2,1)S(1)}, s32[]{:T(128)}, /*index=5*/s32[]{:T(128)}) while((s32[]{:T(128)}, f32[2592,96]{0,1:T(8,128)}, bf16[2,18,18,96,18]{3,4,2,1,0:T(8,128)(2,1)}, bf16[2,4096,96]{2,1,0:T(8,128)(2,1)S(1)}, ...), condition=%wide.region_17.18_spmd.clone, body=%wide.region_16.17_spmd.clone.sunk | while | flops 2038929408 | bytes 252742768 | solution.py:138
  738.6 26.5 %copy.87 = bf16[16,16,16,27,96]{4,3,2,1,0:T(8,128)(2,1)} copy(bf16[16,16,16,27,96]{4,2,1,0,3:T(8,128)(2,1)} %bitcast.589) | data formatting | bytes 42467328 | tf_op jit(solution)/shard_map/while/body/eval_jaxpr/transpose | solution.py:37
  765.1 54.7 %reshape.159 = bf16[4096,2592]{1,0:T(8,128)(2,1)} reshape(bf16[16,16,16,27,96]{4,3,2,1,0:T(8,128)(2,1)} %copy.87) | data formatting | bytes 42467328 | tf_op jit(solution)/shard_map/while/body/eval_jaxpr/reshape | solution.py:37
  855.2 26.5 %copy.87 = bf16[16,16,16,27,96]{4,3,2,1,0:T(8,128)(2,1)} copy(bf16[16,16,16,27,96]{4,2,1,0,3:T(8,128)(2,1)} %bitcast.589) | data formatting | bytes 42467328 | tf_op jit(solution)/shard_map/while/body/eval_jaxpr/transpose | solution.py:37
  881.7 54.7 %reshape.159 = bf16[4096,2592]{1,0:T(8,128)(2,1)} reshape(bf16[16,16,16,27,96]{4,3,2,1,0:T(8,128)(2,1)} %copy.87) | data formatting | bytes 42467328 | tf_op jit(solution)/shard_map/while/body/eval_jaxpr/reshape | solution.py:37
  936.4 10.5 convolution_add_fusion.2
  954.9 139.6 %all-reduce.7.cloned.1.call-done = f32[2592,96]{0,1:T(8,128)} async-done(((f32[2592,96]{0,1:T(8,128)}), f32[2592,96]{0,1:T(8,128)}) %all-reduce.7.cloned.1.call-update) | async-done | bytes 995344 | tf_op jit(solution)/shard_map/psum | solution.py:153
  1097.3 21.2 %select_maximum_fusion = bf16[18,18,96,130]{3,2,1,0:T(8,128)(2,1)} fusion(bf16[18,1,96,128]{3,2,1,0:T(8,128)(2,1)S(1)} %collective-permute-done.7, bf16[18,1,96,128]{3,2,1,0:T(8,128)(2,1)S(1)} %collective-permute-done.6, bf16[1,16,96,128]{3,2,1,0:T(8,128)(2,1)} %collective-permute-done.5, bf16[16,16,96,128]{3,2,1,0:T(8,128)(2,1)} %dynamic_update_slice.21, ...), kind=kLoop, calls=%fused_computation.185 | loop fusion | flops 72783360 | bytes 16049664 | tf_op jit(solution)/shard_map/concatenate | solution.py:16
  1121.0 40.2 %while.36 = (s32[]{:T(128)}, bf16[18,18,96,130]{3,2,1,0:T(8,128)(2,1)}, s32[2,4]{1,0:T(2,128)S(1)}, bf16[2,18,18,96,18]{3,4,2,1,0:T(8,128)(2,1)}, s32[]{:T(128)}) while((s32[]{:T(128)}, bf16[18,18,96,130]{3,2,1,0:T(8,128)(2,1)}, s32[2,4]{1,0:T(2,128)S(1)}, bf16[2,18,18,96,18]{3,4,2,1,0:T(8,128)(2,1)}, s32[]{:T(128)}) %tuple.120), condition=%wide.while_cond.1, body=%wide.while_body.1.sunk | while | flops 2 | bytes 7589997 | solution.py:47
  1161.2 239.4 %while.34 = (s32[]{:T(128)}, bf16[2,4096,96]{1,2,0:T(8,128)(2,1)}, bf16[2,18,18,96,18]{3,4,2,1,0:T(8,128)(2,1)}, bf16[2592,96]{1,0:T(8,128)(2,1)S(1)}, s32[]{:T(128)}) while((s32[]{:T(128)}, bf16[2,4096,96]{1,2,0:T(8,128)(2,1)}, bf16[2,18,18,96,18]{3,4,2,1,0:T(8,128)(2,1)}, bf16[2592,96]{1,0:T(8,128)(2,1)S(1)}, s32[]{:T(128)}) %tuple.117), condition=%wide.region_15.16_spmd, body=%wide.region_14.15_spmd.sunk | while | flops 2038824960 | bytes 263736464 | solution.py:150
  1186.4 26.5 %copy.84 = bf16[16,16,16,27,96]{4,3,2,1,0:T(8,128)(2,1)} copy(bf16[16,16,16,27,96]{4,2,1,0,3:T(8,128)(2,1)} %bitcast.590) | data formatting | bytes 42467328 | tf_op jit(solution)/shard_map/while/body/eval_jaxpr/transpose | solution.py:37
  1212.9 54.9 %reshape.158 = bf16[4096,2592]{1,0:T(8,128)(2,1)} reshape(bf16[16,16,16,27,96]{4,3,2,1,0:T(8,128)(2,1)} %copy.84) | data formatting | bytes 42467328 | tf_op jit(solution)/shard_map/while/body/eval_jaxpr/reshape | solution.py:37
  1267.8 11.9 fusion.267
  1306.0 26.5 %copy.84 = bf16[16,16,16,27,96]{4,3,2,1,0:T(8,128)(2,1)} copy(bf16[16,16,16,27,96]{4,2,1,0,3:T(8,128)(2,1)} %bitcast.590) | data formatting | bytes 42467328 | tf_op jit(solution)/shard_map/while/body/eval_jaxpr/transpose | solution.py:37
  1332.5 54.9 %reshape.158 = bf16[4096,2592]{1,0:T(8,128)(2,1)} reshape(bf16[16,16,16,27,96]{4,3,2,1,0:T(8,128)(2,1)} %copy.84) | data formatting | bytes 42467328 | tf_op jit(solution)/shard_map/while/body/eval_jaxpr/reshape | solution.py:37
  1387.3 11.9 fusion.267
  1421.1 81.5 %dynamic_update_slice.22 = bf16[16,16,96,128]{3,2,1,0:T(8,128)(2,1)} dynamic-update-slice(bf16[16,16,96,128]{3,2,1,0:T(8,128)(2,1)} %broadcast.67, bf16[16,16,96,16]{3,2,1,0:T(8,128)(2,1)} %copy.67, s32[]{:T(128)} %constant.15.clone.1, s32[]{:T(128)} %constant.15.clone.1, s32[]{:T(128)} %constant.15.clone.1, s32[]{:T(128)S(6)} %select_n.67) | dynamic-update-slice | bytes 1572868 | tf_op jit(solution)/shard_map/dynamic_update_slice | solution.py:72
  1502.6 81.5 %dynamic_update_slice.23 = bf16[16,16,96,128]{3,2,1,0:T(8,128)(2,1)} dynamic-update-slice(bf16[16,16,96,128]{3,2,1,0:T(8,128)(2,1)} %dynamic_update_slice.22, bf16[16,16,96,16]{3,2,1,0:T(8,128)(2,1)} %copy.69, s32[]{:T(128)} %constant.15.clone.1, s32[]{:T(128)} %constant.15.clone.1, s32[]{:T(128)} %constant.15.clone.1, s32[]{:T(128)S(6)} %select_n.71) | dynamic-update-slice | bytes 1572868 | tf_op jit(solution)/shard_map/dynamic_update_slice | solution.py:72
  (310 shorter events, 385.1 us)
Async XLA Ops:
  7.2 1087.4 %all-reduce.7.cloned.1.call-start = ((), (), s32[]{:S(2)}) async-start(), calls=%async_computation | async-start | bytes 2064384 | tf_op jit(solution)/shard_map/psum | solution.py:153
  9.6 12.5 copy-start.11
  12.9 2.7 copy-start.3
  16.4 34.3 %collective-permute-start = (bf16[1,16,96,128]{3,2,1,0:T(8,128)(2,1)}, bf16[1,16,96,128]{3,2,1,0:T(8,128)(2,1)S(1)}, u32[]{:S(2)}, u32[]{:S(2)}) collective-permute-start(bf16[1,16,96,128]{3,2,1,0:T(8,128)(2,1)} %get-tuple-element.204), channel_id=1, source_target_pairs={{0,16},{16,32},{32,48},{48,64},{64,80},{80,96},{96,112},{1,17},{17... | collective-permute-start | bytes 1179656 | tf_op jit(solution)/shard_map/ppermute | solution.py:18
  20.2 30.5 %collective-permute-start.1 = (bf16[1,16,96,128]{3,2,1,0:T(8,128)(2,1)S(1)}, bf16[1,16,96,128]{3,2,1,0:T(8,128)(2,1)S(1)}, u32[]{:S(2)}, u32[]{:S(2)}) collective-permute-start(bf16[1,16,96,128]{3,2,1,0:T(8,128)(2,1)S(1)} %get-tuple-element.205), channel_id=1, source_target_pairs={{16,0},{32,16},{48,32},{64,48},{80,64},{96,80},{112,96},{17,1},{33... | collective-permute-start | bytes 1179656 | tf_op jit(solution)/shard_map/ppermute | solution.py:20
  52.0 13.1 collective-permute-start.2
  55.4 14.9 collective-permute-start.3
  92.5 40.3 %copy-start.4 = (bf16[27,96,96]{2,1,0:T(8,128)(2,1)S(1)}, bf16[27,96,96]{2,1,0:T(8,128)(2,1)}, u32[]{:S(2)}) copy-start(bf16[27,96,96]{2,1,0:T(8,128)(2,1)} %param.15) | copy-start | bytes 1492996
  132.7 244.7 %copy-start.10 = (f32[2,4096]{1,0:T(2,128)S(1)}, f32[2,4096]{1,0:T(2,128)}, u32[]{:S(2)}) copy-start(f32[2,4096]{1,0:T(2,128)} %reshape.129) | copy-start | bytes 98308
  132.7 313.5 %copy-start.13 = (f32[96]{0:T(128)S(1)}, f32[96]{0:T(128)}, u32[]{:S(2)}) copy-start(f32[96]{0:T(128)} %param.16) | copy-start | bytes 1156
  132.8 313.5 %copy-start.16 = (f32[96]{0:T(128)S(1)}, f32[96]{0:T(128)}, u32[]{:S(2)}) copy-start(f32[96]{0:T(128)} %param.17) | copy-start | bytes 1156
  149.2 9.3 copy-start
  268.4 9.3 copy-start
  516.3 189.6 %copy-start.17 = (f32[96]{0:T(128)}, f32[96]{0:T(128)S(1)}, u32[]{:S(2)}) copy-start(f32[96]{0:T(128)S(1)} %get-tuple-element.186) | copy-start | bytes 1156
  522.9 1.4 copy-start.6
  526.9 186.4 %copy-start.7 = (bf16[2,4096,96]{2,1,0:T(8,128)(2,1)S(1)}, bf16[2,4096,96]{2,1,0:T(8,128)(2,1)}, u32[]{:S(2)}) copy-start(bf16[2,4096,96]{2,1,0:T(8,128)(2,1)} %copy-done.6) | copy-start | bytes 4718596
  708.0 240.3 %collective-permute-start.4 = (bf16[1,16,96,128]{3,2,1,0:T(8,128)(2,1)}, bf16[1,16,96,128]{3,2,1,0:T(8,128)(2,1)}, u32[]{:S(2)}, u32[]{:S(2)}) collective-permute-start(bf16[1,16,96,128]{3,2,1,0:T(8,128)(2,1)} %get-tuple-element.202), channel_id=1, source_target_pairs={{0,16},{16,32},{32,48},{48,64},{64,80},{80,96},{96,112},{1,17},{17... | collective-permute-start | bytes 1179656 | tf_op jit(solution)/shard_map/ppermute | solution.py:18
  711.4 237.0 %collective-permute-start.5 = (bf16[1,16,96,128]{3,2,1,0:T(8,128)(2,1)}, bf16[1,16,96,128]{3,2,1,0:T(8,128)(2,1)}, u32[]{:S(2)}, u32[]{:S(2)}) collective-permute-start(bf16[1,16,96,128]{3,2,1,0:T(8,128)(2,1)} %get-tuple-element.203), channel_id=1, source_target_pairs={{16,0},{32,16},{48,32},{64,48},{80,64},{96,80},{112,96},{17,1},{33... | collective-permute-start | bytes 1179656 | tf_op jit(solution)/shard_map/ppermute | solution.py:20
  713.3 234.1 %copy-start.5 = (bf16[27,96,96]{2,1,0:T(8,128)(2,1)S(1)}, bf16[27,96,96]{2,1,0:T(8,128)(2,1)}, u32[]{:S(2)}) copy-start(bf16[27,96,96]{2,1,0:T(8,128)(2,1)} %param.15) | copy-start | bytes 1492996
  713.3 234.5 %copy-start.18 = (f32[96]{0:T(128)S(1)}, f32[96]{0:T(128)}, u32[]{:S(2)}) copy-start(f32[96]{0:T(128)} %copy-done.17) | copy-start | bytes 1156
  729.3 9.3 copy-start.1
  845.8 9.3 copy-start.1
  947.4 173.6 %copy-start.15 = (s32[2,4]{1,0:T(2,128)S(1)}, s32[2,4]{1,0:T(2,128)}, u32[]{:S(2)}) copy-start(s32[2,4]{1,0:T(2,128)} %copy-done.14) | copy-start | bytes 100
  949.6 147.7 %collective-permute-start.6 = (bf16[18,1,96,128]{3,2,1,0:T(8,128)(2,1)S(1)}, bf16[18,1,96,128]{3,2,1,0:T(8,128)(2,1)S(1)}, u32[]{:S(2)}, u32[]{:S(2)}) collective-permute-start(bf16[18,1,96,128]{3,2,1,0:T(8,128)(2,1)S(1)} %get-tuple-element.198), channel_id=1, source_target_pairs={{0,1},{1,2},{2,3},{3,4},{4,5},{5,6},{6,7},{7,8},{8,9},{9,10},{10,1... | collective-permute-start | bytes 1327112 | tf_op jit(solution)/shard_map/ppermute | solution.py:18
  951.5 145.8 %collective-permute-start.7 = (bf16[18,1,96,128]{3,2,1,0:T(8,128)(2,1)S(1)}, bf16[18,1,96,128]{3,2,1,0:T(8,128)(2,1)S(1)}, u32[]{:S(2)}, u32[]{:S(2)}) collective-permute-start(bf16[18,1,96,128]{3,2,1,0:T(8,128)(2,1)S(1)} %get-tuple-element.199), channel_id=1, source_target_pairs={{1,0},{2,1},{3,2},{4,3},{5,4},{6,5},{7,6},{8,7},{9,8},{10,9},{11,1... | collective-permute-start | bytes 1327112 | tf_op jit(solution)/shard_map/ppermute | solution.py:20
  1177.1 9.3 copy-start.2
  1212.9 54.9 %copy-start.8 = (bf16[2,4096,96]{1,2,0:T(8,128)(2,1)S(1)}, bf16[2,4096,96]{1,2,0:T(8,128)(2,1)}, u32[]{:S(2)}) copy-start(bf16[2,4096,96]{1,2,0:T(8,128)(2,1)} %get-tuple-element.393) | copy-start | bytes 4718596 | tf_op jit(solution)/shard_map/while
  1279.7 1.2 copy-start.9
  1296.6 9.3 copy-start.2
  1332.5 54.9 %copy-start.8 = (bf16[2,4096,96]{1,2,0:T(8,128)(2,1)S(1)}, bf16[2,4096,96]{1,2,0:T(8,128)(2,1)}, u32[]{:S(2)}) copy-start(bf16[2,4096,96]{1,2,0:T(8,128)(2,1)} %get-tuple-element.393) | copy-start | bytes 4718596 | tf_op jit(solution)/shard_map/while
  1399.2 1.2 copy-start.9
  1400.6 183.5 %copy-start.12 = (pred[16,16,128]{2,1,0:T(8,128)(4,1)S(1)}, pred[16,16,128]{2,1,0:T(8,128)(4,1)}, u32[]{:S(2)}) copy-start(pred[16,16,128]{2,1,0:T(8,128)(4,1)} %copy-done.11) | copy-start | bytes 98308
  (1 other events, 0.5 us)
Sparse Core Ops, SparseCore 0:
  947.5 146.9 all-reduce.6
where the time goes:
time: 1620 us; the launch traced here: 1600 us
  local copies, waits for them, and re-layouts  1120 us (69%)
  waiting for transfers between devices  152 us (9%)
  blocking collectives  126 us (8%)
  other arithmetic  83.8 us (5%)
  matrix products  70.5 us (4%)
  starting transfers between devices  21.7 us (1%)
  between operations  16.6 us (1%)
    reshape x6, local copies, waits for them, and re-layouts, unfold(): jnp.transpose(stacked, (1, 2, 4, 0, 3))  329 us
    dynamic_update_slice x4, local copies, waits for them, and re-layouts, place_bricks(): lax.dynamic_update_slice_in_dim(assembled, brick_piece, slot_ids[slot_ind...  326 us
    transpose x6, local copies, waits for them, and re-layouts, unfold(): jnp.transpose(stacked, (1, 2, 4, 0, 3))  159 us
    psum x1, waiting for transfers between devices, body(): weight_total = lax.psum(weight_local, ('gx', 'gy'))  140 us
    while x176, local copies, waits for them, and re-layouts  136 us
    gather x20, local copies, waits for them, and re-layouts  80.4 us
    psum x1, blocking collectives, body(): lax.psum((jnp.sum(mask_values * preact, axis=(0, 1)), jnp.sum(mask_values...  63.7 us
    psum x1, blocking collectives, body(): lax.psum((jnp.sum(grad_z, axis=(0, 1)), jnp.sum(grad_z * normed, axis=(0,...  62.6 us
  transfers between devices with their start and end apart: 9, of which 3 were waited for; matrix products, arithmetic and copies ran while one was open for 15% of the time, Pallas kernels for 0%

commit v1 on v0

v1 whole, which is shorter than its diff:
```python
import functools

import jax
import jax.numpy as jnp
from jax import lax
from jax.experimental import pallas as pl
from jax.experimental.pallas import tpu as pltpu
from jax.sharding import PartitionSpec as P

B = 16
C = 96
NB = 8
W2 = 512
ROWS = 20 * C
EDGE = C + 16
F32 = jnp.float32
BF16 = jnp.bfloat16
AXES = ("gx", "gy")


def params(mib=56):
    return pltpu.CompilerParams(vmem_limit_bytes=mib * 1024 * 1024)


def vmem():
    return pl.BlockSpec(memory_space=pltpu.VMEM)


def smem():
    return pl.BlockSpec(memory_space=pltpu.SMEM)


def iota(shape, dim):
    return lax.broadcasted_iota(jnp.int32, shape, dim)


def slots(live_ref):
    first = jnp.int32(-1)
    second = jnp.int32(-1)
    for j in reversed(range(NB)):
        on = live_ref[0, 0, j] > 0
        second = jnp.where(on, first, second)
        first = jnp.where(on, jnp.int32(j), first)
    ids = (jnp.maximum(first, 0), jnp.maximum(second, 0))
    return ids, (first >= 0, second >= 0)


def wrap(shift):
    return jnp.bitwise_and(shift + 256, 127)


def pack_tiles(load, ids):
    group = iota((C, 128), 1) // B
    tiles = []
    for s in range(2):
        for h in range(2):
            acc = None
            for j in range(8):
                r = pltpu.roll(load(h * 8 + j), wrap(16 * j - 16 * ids[s]), 1)
                acc = r if j == 0 else jnp.where(group == j, r, acc)
            tiles.append(acc)
    return tiles


def emit_faces(x, tiles, ids, faces):
    x0, x1, y0, y1, c00, c01, c10, c11 = faces
    group = iota((C, 128), 1) // B
    zero = jnp.zeros((C, 128), BF16)

    def side(face, low, high):
        for k in range(4):
            face[0:C, k * 128 : (k + 1) * 128] = tiles[k]
        low[0:C, :] = jnp.where(
            group == 0, tiles[0], jnp.where(group == 1, pltpu.roll(tiles[2], 16, 1), zero)
        )
        high[0:C, :] = jnp.where(
            group == 0,
            pltpu.roll(tiles[1], 16, 1),
            jnp.where(group == 1, pltpu.roll(tiles[3], 32, 1), zero),
        )

    @pl.when(x == 0)
    def _():
        side(x0, c00, c01)
        halves = [
            jnp.full((16, 256), 1.0, F32) * ids[s].astype(F32) for s in range(2)
        ]
        for face in (x0, x1, y0, y1):
            for s in range(2):
                face[C:EDGE, s * 256 : (s + 1) * 256] = halves[s].astype(BF16)
        mixed = jnp.where(
            iota((16, 128), 1) < B, ids[0].astype(F32), ids[1].astype(F32)
        ).astype(BF16)
        for face in (c00, c01, c10, c11):
            face[C:EDGE, :] = mixed

    @pl.when(x == B - 1)
    def _():
        side(x1, c10, c11)

    spot = lax.rem(x, 8)
    half = x // 8
    for face, base, off in ((y0, 0, 0), (y1, 1, 112)):
        for s in range(2):
            r = pltpu.roll(tiles[2 * s + base], wrap(16 * spot - off), 1)
            lanes = pl.ds(pl.multiple_of(s * 256 + half * 128, 128), 128)
            face[0:C, lanes] = jnp.where(group == spot, r, face[0:C, lanes])


FACES = [jax.ShapeDtypeStruct((EDGE, W2), BF16)] * 4 + [
    jax.ShapeDtypeStruct((EDGE, 128), BF16)
] * 4


def pack_features_kernel(live_ref, feat_ref, mask_ref, out_ref, live_out, *faces):
    x = pl.program_id(0)
    ids, valid = slots(live_ref)
    tiles = pack_tiles(lambda y: feat_ref[0, y], ids)
    cells = mask_ref[0].astype(F32)
    pick = iota((8, 128), 1) // B == iota((8, 128), 0)
    for s in range(2):
        keep = valid[s].astype(F32)
        for h in range(2):
            r = pltpu.roll(cells[h * 8 : (h + 1) * 8], wrap(-16 * ids[s]), 1)
            r = pltpu.roll(r, 0, 1, stride=16, stride_axis=0)
            row = jnp.sum(jnp.where(pick, r, 0.0), axis=0, keepdims=True) * keep
            k = 2 * s + h
            live_out[0, :, k * 128 : (k + 1) * 128] = row
            tiles[k] = tiles[k] * row.astype(BF16)
            out_ref[:, k * 128 : (k + 1) * 128] = tiles[k]
    emit_faces(x, tiles, ids, faces)


def whole(shape):
    return pl.BlockSpec(shape, lambda *a: (0,) * len(shape))


def pack_features(live, features, mask):
    return pl.pallas_call(
        pack_features_kernel,
        grid=(B,),
        in_specs=[
            smem(),
            pl.BlockSpec((1, B, C, 128), lambda x: (x, 0, 0, 0)),
            pl.BlockSpec((1, B, 128), lambda x: (x, 0, 0)),
        ],
        out_specs=[
            pl.BlockSpec((C, W2), lambda x: (x + 2, 0)),
            pl.BlockSpec((1, 1, W2), lambda x: (x, 0, 0)),
        ]
        + [whole(f.shape) for f in FACES],
        out_shape=[
            jax.ShapeDtypeStruct((ROWS, W2), BF16),
            jax.ShapeDtypeStruct((B, 1, W2), F32),
        ]
        + FACES,
        compiler_params=params(),
        name="pack_features",
    )(live, features, mask)


def pack_plain_kernel(live_ref, feat_ref, out_ref):
    ids, _ = slots(live_ref)
    tiles = pack_tiles(lambda y: feat_ref[0, y], ids)
    for k in range(4):
        out_ref[:, k * 128 : (k + 1) * 128] = tiles[k]


def pack_plain(live, values):
    return pl.pallas_call(
        pack_plain_kernel,
        grid=(B,),
        in_specs=[smem(), pl.BlockSpec((1, B, C, 128), lambda x: (x, 0, 0, 0))],
        out_specs=pl.BlockSpec((C, W2), lambda x: (x, 0)),
        out_shape=jax.ShapeDtypeStruct((B * C, W2), BF16),
        compiler_params=params(),
        name="pack_cotangent",
    )(live, values)


def exchange(faces):
    nx, ny = lax.axis_size("gx"), lax.axis_size("gy")

    def move(values, dx, dy):
        pairs = [
            (i * ny + j, (i + dx) * ny + j + dy)
            for i in range(nx)
            for j in range(ny)
            if 0 <= i + dx < nx and 0 <= j + dy < ny
        ]
        return lax.ppermute(values, AXES, pairs)

    x0, x1, y0, y1, c00, c01, c10, c11 = faces
    return (
        move(x1, 1, 0),
        move(x0, -1, 0),
        move(y1, 0, 1),
        move(y0, 0, -1),
        move(c11, 1, 1),
        move(c10, 1, -1),
        move(c01, -1, 1),
        move(c00, -1, -1),
    )


def assemble(ids, body, halo, ext, rows_ref):
    xm, xp, ym, yp, cmm, cmp_, cpm, cpp = halo
    group = iota((C, 128), 1) // B
    wide = iota((C, 384), 1)
    deep = jnp.bitwise_and(wide, 15)
    zero = jnp.zeros((C, 128), BF16)

    def matched(ref, s, d):
        total = None
        for t in range(2):
            lanes = slice(t * 256, (t + 1) * 256)
            tag = ref[C : C + 1, lanes].astype(F32)
            hit = jnp.where(tag == (ids[s] + d).astype(F32), 1.0, 0.0).astype(BF16)
            part = ref[0:C, lanes] * hit
            total = part if total is None else total + part
        return total

    def matched_corner(ref, s, d):
        tag = ref[C : C + 1, :].astype(F32)
        hit = jnp.where(tag == (ids[s] + d).astype(F32), 1.0, 0.0).astype(BF16)
        part = ref[0:C, :] * hit
        return jnp.where(group == 0, part + pltpu.roll(part, 112, 1), zero)

    def finish(i, s, planes):
        here, under, over = planes[1], planes[0], planes[2]
        lanes = slice(s * 384, (s + 1) * 384)
        ext[i, 1, :, lanes] = here
        ext[i, 0, :, lanes] = jnp.where(
            deep == 0, pltpu.roll(under, 384 - 15, 1), pltpu.roll(here, 1, 1)
        )
        ext[i, 2, :, lanes] = jnp.where(
            deep == 15, pltpu.roll(over, 15, 1), pltpu.roll(here, 383, 1)
        )

    for s in range(2):
        for way, ref in ((0, ym), (1, yp)):
            for d in (-1, 0, 1):
                rows_ref[s, way, d + 1] = matched(ref, s, d)
        for i, side, low, high in ((0, xm, cmm, cmp_), (17, xp, cpm, cpp)):
            planes = []
            for d in (-1, 0, 1):
                tail = matched_corner(high, s, d) + pltpu.roll(matched_corner(low, s, d), 112, 1)
                planes.append(jnp.concatenate([matched(side, s, d), tail], axis=1))
            finish(i, s, planes)

    after = (ids[1] == ids[0] + 1).astype(F32)

    def plane(x, carry):
        spot = lax.rem(x, 8)
        half = pl.ds(pl.multiple_of((x // 8) * 128, 128), 128)
        rows = pl.ds(pl.multiple_of((x + 2) * C, C), C)
        flag = jnp.full((1, 256), 1.0, F32) * after
        flag = flag.astype(BF16)
        for s in range(2):
            here = body[rows, s * 256 : (s + 1) * 256]
            other = body[rows, (1 - s) * 256 : (2 - s) * 256] * flag
            none = jnp.zeros((C, 256), BF16)
            centre = (none, here, other) if s == 0 else (other, here, none)
            planes = []
            for d in range(3):
                up = pltpu.roll(rows_ref[s, 1, d, :, half], wrap(-16 * spot), 1)
                down = pltpu.roll(rows_ref[s, 0, d, :, half], wrap(112 - 16 * spot), 1)
                tail = jnp.where(group == 0, up, jnp.where(group == 7, down, zero))
                planes.append(jnp.concatenate([centre[d], tail], axis=1))
            finish(x + 1, s, planes)
        return carry

    lax.fori_loop(0, B, plane, 0)


def fill_columns(ext, i, cols):
    for dz in range(3):
        for s in range(2):
            values = ext[i, dz, :, s * 384 : (s + 1) * 384]
            for dy in range(3):
                moved = values if dy == 1 else pltpu.roll(values, 16 if dy == 0 else 368, 1)
                k = dy * 3 + dz
                cols[k * C : (k + 1) * C, s * 256 : (s + 1) * 256] = moved[:, 0:256]


ASSEMBLY = [
    pltpu.VMEM((18, 3, C, 768), BF16),
    pltpu.VMEM((2, 2, 3, C, 256), BF16),
    pltpu.VMEM((9 * C, W2), BF16),
]


def convolve(weight_ref, ext, cols, sums):
    sums[...] = jnp.zeros_like(sums)

    def step(i, carry):
        fill_columns(ext, i, cols)
        part = jnp.dot(weight_ref[...], cols[...], preferred_element_type=F32)
        rows = pl.ds(pl.multiple_of(i * C, C), 3 * C)
        sums[rows, :] += part
        return carry

    lax.fori_loop(0, 18, step, 0)


def fold(values):
    return (values[:, 0:128] + values[:, 128:256]) + (values[:, 256:384] + values[:, 384:512])


def to_row(column_tile):
    column = jnp.sum(column_tile, axis=1, keepdims=True)
    diag = iota((C, 128), 0) == iota((C, 128), 1)
    return jnp.sum(jnp.where(diag, column, 0.0), axis=0, keepdims=True)


def to_column(row):
    diag = iota((C, 128), 0) == iota((C, 128), 1)
    return jnp.sum(jnp.where(diag, row, 0.0), axis=1, keepdims=True)


def forward_kernel(live_ref, body, *refs):
    halo, (weight_ref, mask_ref, pre_ref, stat_ref, ext, rows_ref, cols) = refs[:8], refs[8:]
    ids, _ = slots(live_ref)
    assemble(ids, body, halo, ext, rows_ref)
    convolve(weight_ref, ext, cols, pre_ref)

    def stat(x, carry):
        total, square, count = carry
        rows = pl.ds(pl.multiple_of((x + 2) * C, C), C)
        values = pre_ref[rows, :]
        mask = mask_ref[x]
        held = values * mask
        return total + fold(held), square + fold(held * values), count + mask

    total, square, count = lax.fori_loop(
        0,
        B,
        stat,
        (jnp.zeros((C, 128), F32), jnp.zeros((C, 128), F32), jnp.zeros((1, W2), F32)),
    )
    stat_ref[...] = jnp.zeros_like(stat_ref)
    stat_ref[0:1, :] = to_row(total)
    stat_ref[1:2, :] = to_row(square)
    stat_ref[2:3, :] = jnp.full((1, 128), 1.0, F32) * jnp.sum(count)


def forward(live, body, halo, weight, mask):
    return pl.pallas_call(
        forward_kernel,
        in_specs=[smem()] + [vmem()] * 11,
        out_specs=[vmem()] * 2,
        out_shape=[
            jax.ShapeDtypeStruct((ROWS, W2), F32),
            jax.ShapeDtypeStruct((8, 128), F32),
        ],
        scratch_shapes=ASSEMBLY,
        compiler_params=params(),
        name="forward",
    )(live, body, *halo, weight, mask)


def moments(stat_ref):
    total = jnp.sum(stat_ref[...], axis=0)
    voxels = total[2:3, :]
    mean = total[0:1, :] / voxels
    var = total[1:2, :] / voxels - mean * mean
    return voxels, mean, lax.rsqrt(var + 1e-05)


def slope_kernel(stat_ref, pre_ref, cot_ref, mask_ref, gain_ref, shift_ref, gz_ref, out_ref):
    voxels, mean, inv = moments(stat_ref)
    mean = to_column(mean)
    inv = to_column(inv)
    gain = to_column(gain_ref[...])
    shift = to_column(shift_ref[...])

    def step(x, carry):
        total, cross = carry
        rows = pl.ds(pl.multiple_of((x + 2) * C, C), C)
        own = pl.ds(pl.multiple_of(x * C, C), C)
        normed = (pre_ref[rows, :] - mean) * inv
        zed = gain * normed + shift
        sig = 1.0 / (1.0 + jnp.exp(-zed))
        gz = mask_ref[x] * cot_ref[own, :].astype(F32) * (sig * (1.0 + zed * (1.0 - sig)))
        gz_ref[own, :] = gz
        return total + fold(gz), cross + fold(gz * normed)

    total, cross = lax.fori_loop(
        0, B, step, (jnp.zeros((C, 128), F32), jnp.zeros((C, 128), F32))
    )
    out_ref[...] = jnp.zeros_like(out_ref)
    out_ref[0:1, :] = to_row(total)
    out_ref[1:2, :] = to_row(cross)


def slope(stats, pre, cot, mask, gain, shift):
    return pl.pallas_call(
        slope_kernel,
        in_specs=[vmem()] * 6,
        out_specs=[vmem()] * 2,
        out_shape=[
            jax.ShapeDtypeStruct((B * C, W2), F32),
            jax.ShapeDtypeStruct((8, 128), F32),
        ],
        compiler_params=params(),
        name="slope",
    )(stats, pre, cot, mask, gain, shift)


def pre_grad_kernel(
    live_ref, stat_ref, stat2_ref, pre_ref, gz_ref, mask_ref, gain_ref, out_ref, small_ref, *faces
):
    ids, _ = slots(live_ref)
    voxels, mean, inv = moments(stat_ref)
    total = jnp.sum(stat2_ref[...], axis=0)
    root = 1.0 / jnp.sqrt(voxels)
    small_ref[...] = jnp.zeros_like(small_ref)
    small_ref[0:1, :] = total[1:2, :] * root
    small_ref[1:2, :] = total[0:1, :] * root
    small_ref[2:3, :] = root
    scale = to_column(gain_ref[...] * inv)
    first = to_column(total[0:1, :] / voxels)
    second = to_column(total[1:2, :] / voxels)
    mean = to_column(mean)
    inv = to_column(inv)
    for q in (0, 1, 18, 19):
        out_ref[q * C : (q + 1) * C, :] = jnp.zeros((C, W2), BF16)

    def step(x, carry):
        rows = pl.ds(pl.multiple_of((x + 2) * C, C), C)
        own = pl.ds(pl.multiple_of(x * C, C), C)
        tiles = []
        for k in range(4):
            lanes = slice(k * 128, (k + 1) * 128)
            normed = (pre_ref[rows, lanes] - mean) * inv
            tile = (
                mask_ref[x][:, lanes] * scale * (gz_ref[own, lanes] - first - normed * second)
            ).astype(BF16)
            out_ref[rows, lanes] = tile
            tiles.append(tile)
        emit_faces(x, tiles, ids, faces)
        return carry

    lax.fori_loop(0, B, step, 0)


def pre_grad(live, stats, stats2, pre, gz, mask, gain):
    return pl.pallas_call(
        pre_grad_kernel,
        in_specs=[smem()] + [vmem()] * 6,
        out_specs=[vmem()] * 10,
        out_shape=[
            jax.ShapeDtypeStruct((ROWS, W2), BF16),
            jax.ShapeDtypeStruct((8, 128), F32),
        ]
        + FACES,
        compiler_params=params(),
        name="pre_grad",
    )(live, stats, stats2, pre, gz, mask, gain)


def weight_kernel(live_ref, body, *refs):
    halo, (grad_ref, out_ref, ext, rows_ref, cols, total) = refs[:8], refs[8:]
    ids, _ = slots(live_ref)
    assemble(ids, body, halo, ext, rows_ref)
    total[...] = jnp.zeros_like(total)

    def step(i, carry):
        fill_columns(ext, i, cols)
        rows = pl.ds(pl.multiple_of(i * C, C), 3 * C)
        total[...] += lax.dot_general(
            grad_ref[rows, :], cols[...], (((1,), (1,)), ((), ())), preferred_element_type=F32
        )
        return carry

    lax.fori_loop(0, 18, step, 0)
    for j in range(6):
        out_ref[j * 288 : (j + 1) * 288, :] = total[:, j * 128 : (j + 1) * 128]
    out_ref[6 * 288 : 2048, :] = jnp.zeros((2048 - 6 * 288, 128), F32)
    out_ref[6 * 288 : 7 * 288, 0:96] = total[:, 768:864]


def weight_terms(live, body, halo, grad):
    return pl.pallas_call(
        weight_kernel,
        in_specs=[smem()] + [vmem()] * 10,
        out_specs=vmem(),
        out_shape=jax.ShapeDtypeStruct((2048, 128), F32),
        scratch_shapes=ASSEMBLY + [pltpu.VMEM((3 * C, 9 * C), F32)],
        compiler_params=params(),
        name="weight_terms",
    )(live, body, *halo, grad)


def backward_kernel(live_ref, body, *refs):
    halo, (weight_ref, mask_ref, out_ref, ext, rows_ref, cols, sums) = refs[:8], refs[8:]
    ids, _ = slots(live_ref)
    assemble(ids, body, halo, ext, rows_ref)
    convolve(weight_ref, ext, cols, sums)

    def step(x, carry):
        rows = pl.ds(pl.multiple_of((x + 2) * C, C), C)
        own = pl.ds(pl.multiple_of(x * C, C), C)
        out_ref[own, :] = (sums[rows, :] * mask_ref[x]).astype(BF16)
        return carry

    lax.fori_loop(0, B, step, 0)


def backward(live, body, halo, weight, mask):
    return pl.pallas_call(
        backward_kernel,
        in_specs=[smem()] + [vmem()] * 11,
        out_specs=vmem(),
        out_shape=jax.ShapeDtypeStruct((B * C, W2), BF16),
        scratch_shapes=ASSEMBLY + [pltpu.VMEM((ROWS, W2), F32)],
        compiler_params=params(),
        name="backward",
    )(live, body, *halo, weight, mask)


def unpack_kernel(live_ref, in_ref, out_ref):
    ids, _ = slots(live_ref)
    group = iota((C, 128), 1) // B
    zero = jnp.zeros((C, 128), BF16)
    inside = [group == ids[s] for s in range(2)]
    for y in range(B):
        h, j = y // 8, y % 8
        moved = []
        for s in range(2):
            k = 2 * s + h
            tile = in_ref[:, k * 128 : (k + 1) * 128]
            moved.append(pltpu.roll(tile, wrap(16 * ids[s] - 16 * j), 1))
        out_ref[0, y] = jnp.where(inside[0], moved[0], jnp.where(inside[1], moved[1], zero))


def unpack(live, packed):
    return pl.pallas_call(
        unpack_kernel,
        grid=(B,),
        in_specs=[smem(), pl.BlockSpec((C, W2), lambda x: (x, 0))],
        out_specs=pl.BlockSpec((1, B, C, 128), lambda x: (x, 0, 0, 0)),
        out_shape=jax.ShapeDtypeStruct((B, B, C, 128), BF16),
        compiler_params=params(),
        name="unpack",
    )(live, packed)


def finish_kernel(sum_ref, small_ref, out_ref):
    root = small_ref[2:3, 0:C]
    for a in range(3):
        for k in range(9):
            start = k * C
            pieces = []
            while start < (k + 1) * C:
                j, off = start // 128, start % 128
                stop = min((k + 1) * C, (j + 1) * 128)
                row = j * 288 + (2 - a) * C
                pieces.append(sum_ref[row : row + C, off : off + stop - start].astype(F32))
                start = stop
            block = pieces[0] if len(pieces) == 1 else jnp.concatenate(pieces, axis=1)
            out_ref[9 * a + k] = block.T * root


def finish(sums, small):
    return pl.pallas_call(
        finish_kernel,
        in_specs=[vmem()] * 2,
        out_specs=vmem(),
        out_shape=jax.ShapeDtypeStruct((27, C, C), F32),
        compiler_params=params(),
        name="finish",
    )(sums, small)


def gather_small(values):
    count = lax.axis_size("gx") * lax.axis_size("gy")
    spread = jnp.broadcast_to(values[None], (count,) + values.shape)
    return lax.all_to_all(spread, AXES, 0, 0, tiled=True)


def sum_large(values):
    count = lax.axis_size("gx") * lax.axis_size("gy")
    parts = values.reshape(count, values.shape[0] // count, 128)
    parts = lax.all_to_all(parts, AXES, 0, 0, tiled=True)
    mine = jnp.sum(parts, axis=0)
    spread = jnp.broadcast_to(mine[None], (count,) + mine.shape)
    return lax.all_to_all(spread, AXES, 0, 0, tiled=True).reshape(values.shape)


def body(features, cotangent, weight, bn_gain, bn_shift, voxel_mask, brick_live):
    gain = jnp.pad(bn_gain, (0, 128 - C))[None]
    shift = jnp.pad(bn_shift, (0, 128 - C))[None]
    cube = weight.reshape(3, 3, 3, C, C)
    weight_rows = jnp.transpose(cube[::-1], (0, 4, 1, 2, 3)).reshape(3 * C, 9 * C)
    weight_back = jnp.transpose(cube[:, ::-1, ::-1], (0, 3, 1, 2, 4)).reshape(3 * C, 9 * C)

    packed, mask, *faces = pack_features(brick_live, features, voxel_mask)
    halo = exchange(faces)
    cot = pack_plain(brick_live, cotangent)
    pre, stats = forward(brick_live, packed, halo, weight_rows, mask)
    stats = gather_small(stats)
    gz, stats2 = slope(stats, pre, cot, mask, gain, shift)
    stats2 = gather_small(stats2)
    grad, small, *grad_faces = pre_grad(brick_live, stats, stats2, pre, gz, mask, gain)
    grad_halo = exchange(grad_faces)
    terms = weight_terms(brick_live, packed, halo, grad)
    sums = sum_large(terms)
    back = backward(brick_live, grad, grad_halo, weight_back, mask)
    input_grad = unpack(brick_live, back)
    weight_grad = finish(sums, small)
    return input_grad, weight_grad, small[0, :C], small[1, :C]


def solution(mesh):
    return jax.shard_map(
        body,
        mesh=mesh,
        in_specs=(
            P("gx", "gy", None, None),
            P("gx", "gy", None, None),
            P(),
            P(),
            P(),
            P("gx", "gy", None),
            P("gx", "gy", None),
        ),
        out_specs=(P("gx", "gy", None, None), P(), P(), P()),
        check_vma=False,
    )
```

time: 1620 us -> 262 us (0.16)
  the two profiles are of different devices: /device:TPU:15 before, /device:TPU:7 now
where the time goes in v1:
time: 262 us; the launch traced here: 260 us
  Pallas kernels  120 us (46%)
  starting transfers between devices  65.2 us (25%)
  blocking collectives  46.3 us (18%)
  local copies, waits for them, and re-layouts  17.2 us (7%)
  waiting for transfers between devices  10 us (4%)
    ppermute x16, starting transfers between devices, move(): return lax.ppermute(values, AXES, pairs)  49.8 us
    all_to_all x1, blocking collectives, sum_large(): parts = lax.all_to_all(parts, AXES, 0, 0, tiled=True)  24.4 us
    pallas_call x1, Pallas kernels, forward(): pl.pallas_call(forward_kernel, in_specs=[smem()] + [vmem()] * 11, out_spe...  22.3 us
    all_to_all x1, blocking collectives, gather_small(): return lax.all_to_all(spread, AXES, 0, 0, tiled=True)  21.9 us
    pallas_call x1, Pallas kernels, backward(): pl.pallas_call(backward_kernel, in_specs=[smem()] + [vmem()] * 11, out_sp...  21 us
    pallas_call x1, Pallas kernels, weight_terms(): pl.pallas_call(weight_kernel, in_specs=[smem()] + [vmem()] * 10, out_spec...  20.6 us
    pallas_call x1, Pallas kernels, pack_features(): pl.pallas_call(pack_features_kernel, grid=(B,), in_specs=[smem(), pl.Bloc...  13.5 us
    pallas_call x1, Pallas kernels, pack_plain(): pl.pallas_call(pack_plain_kernel, grid=(B,), in_specs=[smem(), pl.BlockSp...  12.1 us
  transfers between devices with their start and end apart: 18, of which 2 were waited for; matrix products, arithmetic and copies ran while one was open for 4% of the time, Pallas kernels for 17%

profile of v1, /device:TPU:7, one launch (start us, length us, event | category | flops | bytes accessed | tf_op | source)
XLA Modules:
  0.0 259.6 jit_solution(11462295821543743157)
XLA Ops:
  0.6 13.5 %pack_features.1 = (bf16[1920,512]{1,0:T(8,128)(2,1)}, f32[16,1,512]{2,1,0:T(1,128)}, bf16[112,512]{1,0:T(8,128)(2,1)}, bf16[112,512]{1,0:T(8,128)(2,1)}, bf16[1...) custom-call(s32[1,1,8]{2,1,0:T(1,128)} %live_ref.13, ...), custom_call_target="tpu_custom_call" | custom-call | tf_op jit(solution)/shard_map/pack_features/pallas_call | solution.py:139
  14.2 5.0 %collective-permute-start.4 = (bf16[112,128]{1,0:T(8,128)(2,1)}, bf16[112,128]{1,0:T(8,128)(2,1)S(1)}, u32[]{:S(2)}, u32[]{:S(2)}) collective-permute-start(bf16[112,128]{1,0:T(8,128)(2,1)} %get-tuple-element.33), channel_id=1, source_target_pairs={{0,17},{1,18},{2,19},{3,20},{4,21},{5,22},{6,23},{7,24},{8,25},{9,... | collective-permute-start | bytes 86024 | tf_op jit(solution)/shard_map/ppermute | solution.py:191
  19.2 1.9 collective-permute-start.5
  21.1 5.7 %collective-permute-start.6 = (bf16[112,128]{1,0:T(8,128)(2,1)}, bf16[112,128]{1,0:T(8,128)(2,1)S(1)}, u32[]{:S(2)}, u32[]{:S(2)}) collective-permute-start(bf16[112,128]{1,0:T(8,128)(2,1)} %get-tuple-element.35), channel_id=1, source_target_pairs={{16,1},{17,2},{18,3},{19,4},{20,5},{21,6},{22,7},{23,8},{24,9},{25... | collective-permute-start | bytes 86024 | tf_op jit(solution)/shard_map/ppermute | solution.py:191
  26.9 2.8 %collective-permute-start = (bf16[112,512]{1,0:T(8,128)(2,1)}, bf16[112,512]{1,0:T(8,128)(2,1)S(1)}, u32[]{:S(2)}, u32[]{:S(2)}) collective-permute-start(bf16[112,512]{1,0:T(8,128)(2,1)} %get-tuple-element.29), channel_id=1, source_target_pairs={{0,16},{1,17},{2,18},{3,19},{4,20},{5,21},{6,22},{7,23},{8,24},{9,... | collective-permute-start | bytes 344072 | tf_op jit(solution)/shard_map/ppermute | solution.py:191
  29.7 1.9 collective-permute-start.1
  32.3 2.3 collective-permute-start.2
  34.7 3.0 %collective-permute-start.3 = (bf16[112,512]{1,0:T(8,128)(2,1)}, bf16[112,512]{1,0:T(8,128)(2,1)S(1)}, u32[]{:S(2)}, u32[]{:S(2)}) collective-permute-start(bf16[112,512]{1,0:T(8,128)(2,1)} %get-tuple-element.32), channel_id=1, source_target_pairs={{1,0},{2,1},{3,2},{4,3},{5,4},{6,5},{7,6},{8,7},{9,8},{10,9},{11,1... | collective-permute-start | bytes 344072 | tf_op jit(solution)/shard_map/ppermute | solution.py:191
  37.7 1.9 collective-permute-start.7
  41.2 4.9 %collective-permute-done.7.refs_7_ = bf16[112,128]{1,0:T(8,128)(2,1)S(1)} collective-permute-done((bf16[112,128]{1,0:T(8,128)(2,1)}, bf16[112,128]{1,0:T(8,128)(2,1)S(1)}, u32[]{:S(2)}, u32[]{:S(2)}) %collective-permute-start.7) | collective-permute-done | bytes 28704 | tf_op jit(solution)/shard_map/ppermute | solution.py:191
  46.9 22.3 %forward.1 = (f32[1920,512]{1,0:T(8,128)}, f32[8,128]{1,0:T(8,128)}) custom-call(s32[1,1,8]{2,1,0:T(1,128)} %live_ref.13, bf16[1920,512]{1,0:T(8,128)(2,1)} %get-tuple-element.28.body, bf16[112,512]{1,0:T(8,128)(2,1)} %copy-done.3, bf16[112,512]{1,0:T(8,128)(2,1)} %copy-done.4, bf16[112,512]{1,0:T(8,128)(2,1)} %copy-done.5, bf16[112,512]{1,0:T(8,128)(2,1)} %copy-done.6, ...), custom_call_target="tpu_custom_call" | custom-call | tf_op jit(solution)/shard_map/forward/pallas_call | solution.py:348
  70.7 9.7 %all-to-all-start = ((f32[128,8,128]{2,1,0:T(8,128)}), f32[128,8,128]{2,1,0:T(8,128)S(1)}, u32[]{:S(2)}, u32[]{:S(2)}) async-start(f32[128,8,128]{2,1,0:T(8,128)} %broadcast_in_dim.10), calls=%async_computation | async-start | bytes 1048576 | tf_op jit(solution)/shard_map/all_to_all | solution.py:579
  80.5 12.1 %pack_cotangent.1.cot_ref = bf16[1536,512]{1,0:T(8,128)(2,1)} custom-call(s32[1,1,8]{2,1,0:T(1,128)} %live_ref.13, bf16[16,16,96,128]{3,2,1,0:T(8,128)(2,1)} %feat_ref.3), custom_call_target="tpu_custom_call" | custom-call | tf_op jit(solution)/shard_map/pack_cotangent/pallas_call | solution.py:170
  93.8 7.0 %slope.1 = (f32[1536,512]{1,0:T(8,128)}, f32[8,128]{1,0:T(8,128)}) custom-call(f32[128,8,128]{2,1,0:T(8,128)} %copy-done, f32[1920,512]{1,0:T(8,128)} %get-tuple-element.39.pre_ref, bf16[1536,512]{1,0:T(8,128)(2,1)} %pack_cotangent.1.cot_ref, f32[16,1,512]{2,1,0:T(1,128)} %get-tuple-element.37.refs_9_.mask_ref, f32[1,128]{1,0:T(1,128)} %get-tuple-element.55.gain_ref, ...), custom_call_target="tpu_custom_call" | custom-call | tf_op jit(solution)/shard_map/slope/pallas_call | solution.py:397
  101.5 21.9 %all_to_all.20.stat2_ref = f32[128,8,128]{2,1,0:T(8,128)} all-to-all(f32[128,8,128]{2,1,0:T(8,128)S(1)} %broadcast_in_dim.13), channel_id=1, replica_groups=mesh['gx'=8,'gy'=16] {'gx','gy'}, dimensions={0} | all-to-all | bytes 1048576 | tf_op jit(solution)/shard_map/all_to_all | solution.py:579
  123.4 8.1 %pre_grad.1 = (bf16[1920,512]{1,0:T(8,128)(2,1)}, f32[8,128]{1,0:T(8,128)}, bf16[112,512]{1,0:T(8,128)(2,1)}, bf16[112,512]{1,0:T(8,128)(2,1)}, bf16[112,512]{1,...) custom-call(s32[1,1,8]{2,1,0:T(1,128)} %live_ref.13, ...), custom_call_target="tpu_custom_call" | custom-call | tf_op jit(solution)/shard_map/pre_grad/pallas_call | solution.py:448
  131.5 20.6 %weight_terms.1 = f32[2048,128]{1,0:T(8,128)} custom-call(s32[1,1,8]{2,1,0:T(1,128)} %live_ref.13, bf16[1920,512]{1,0:T(8,128)(2,1)} %get-tuple-element.28.body, bf16[112,512]{1,0:T(8,128)(2,1)} %copy-done.3, bf16[112,512]{1,0:T(8,128)(2,1)} %copy-done.4, bf16[112,512]{1,0:T(8,128)(2,1)} %copy-done.5, bf16[112,512]{1,0:T(8,128)(2,1)} %copy-done.6, ...), custom_call_target="tpu_custom_call" | custom-call | tf_op jit(solution)/shard_map/weight_terms/pallas_call | solution.py:484
  152.1 24.4 %all_to_all.21 = f32[128,16,128]{2,1,0:T(8,128)S(1)} all-to-all(f32[128,16,128]{2,1,0:T(8,128)} %bitcast.15), channel_id=1, replica_groups=mesh['gx'=8,'gy'=16] {'gx','gy'}, dimensions={0} | all-to-all | bytes 2097152 | tf_op jit(solution)/shard_map/all_to_all | solution.py:585
  177.7 5.7 %all-to-all-start.3 = ((f32[128,16,128]{2,1,0:T(8,128)}), f32[128,16,128]{2,1,0:T(8,128)S(1)}, u32[]{:S(2)}, u32[]{:S(2)}) async-start(f32[128,16,128]{2,1,0:T(8,128)} %broadcast_in_dim.28), calls=%async_computation.3 | async-start | bytes 2097152 | tf_op jit(solution)/shard_map/all_to_all | solution.py:588
  183.4 4.5 %collective-permute-start.12 = (bf16[112,128]{1,0:T(8,128)(2,1)S(1)}, bf16[112,128]{1,0:T(8,128)(2,1)S(1)}, u32[]{:S(2)}, u32[]{:S(2)}) collective-permute-start(bf16[112,128]{1,0:T(8,128)(2,1)S(1)} %copy-done.28), channel_id=1, source_target_pairs={{0,17},{1,18},{2,19},{3,20},{4,21},{5,22},{6,23},{7,24},{8,25},{9,... | collective-permute-start | bytes 86024 | tf_op jit(solution)/shard_map/ppermute | solution.py:191
  187.9 2.0 collective-permute-start.13
  190.0 5.7 %collective-permute-start.14 = (bf16[112,128]{1,0:T(8,128)(2,1)S(1)}, bf16[112,128]{1,0:T(8,128)(2,1)S(1)}, u32[]{:S(2)}, u32[]{:S(2)}) collective-permute-start(bf16[112,128]{1,0:T(8,128)(2,1)S(1)} %copy-done.26), channel_id=1, source_target_pairs={{16,1},{17,2},{18,3},{19,4},{20,5},{21,6},{22,7},{23,8},{24,9},{25... | collective-permute-start | bytes 86024 | tf_op jit(solution)/shard_map/ppermute | solution.py:191
  196.1 4.2 %rev.7 = bf16[3,3,3,96,96]{4,2,1,3,0:T(4,128)(2,1)S(1)} reverse(bf16[3,3,3,96,96]{4,2,1,3,0:T(4,128)(2,1)S(1)} %copy.14), dimensions={1,2} | reverse | bytes 995328 | tf_op jit(solution)/shard_map/rev | solution.py:596
  201.6 1.9 collective-permute-start.10
  203.5 3.4 %collective-permute-start.11 = (bf16[112,512]{1,0:T(8,128)(2,1)S(1)}, bf16[112,512]{1,0:T(8,128)(2,1)S(1)}, u32[]{:S(2)}, u32[]{:S(2)}) collective-permute-start(bf16[112,512]{1,0:T(8,128)(2,1)S(1)} %copy-done.23), channel_id=1, source_target_pairs={{1,0},{2,1},{3,2},{4,3},{5,4},{6,5},{7,6},{8,7},{9,8},{10,9},{11,1... | collective-permute-start | bytes 344072 | tf_op jit(solution)/shard_map/ppermute | solution.py:191
  206.9 3.7 %collective-permute-start.8 = (bf16[112,512]{1,0:T(8,128)(2,1)S(1)}, bf16[112,512]{1,0:T(8,128)(2,1)S(1)}, u32[]{:S(2)}, u32[]{:S(2)}) collective-permute-start(bf16[112,512]{1,0:T(8,128)(2,1)S(1)} %copy-done.22), channel_id=1, source_target_pairs={{0,16},{1,17},{2,18},{3,19},{4,20},{5,21},{6,22},{7,23},{8,24},{9,... | collective-permute-start | bytes 344072 | tf_op jit(solution)/shard_map/ppermute | solution.py:191
  210.6 1.9 collective-permute-start.9
  212.6 2.1 collective-permute-start.15
  216.0 5.1 %collective-permute-done.15.refs_7_ = bf16[112,128]{1,0:T(8,128)(2,1)S(1)} collective-permute-done((bf16[112,128]{1,0:T(8,128)(2,1)S(1)}, bf16[112,128]{1,0:T(8,128)(2,1)S(1)}, u32[]{:S(2)}, u32[]{:S(2)}) %collective-permute-start.15) | collective-permute-done | bytes 28704 | tf_op jit(solution)/shard_map/ppermute | solution.py:191
  222.5 21.0 %backward.1.in_ref = bf16[1536,512]{1,0:T(8,128)(2,1)} custom-call(s32[1,1,8]{2,1,0:T(1,128)} %live_ref.13, bf16[1920,512]{1,0:T(8,128)(2,1)} %get-tuple-element.42.body.refs_8_, bf16[112,512]{1,0:T(8,128)(2,1)} %copy-done.9, bf16[112,512]{1,0:T(8,128)(2,1)} %copy-done.10, bf16[112,512]{1,0:T(8,128)(2,1)} %copy-done.7, bf16[112,512]{1,0:T(8,128)(2,1)} %copy-done.8, ...), custom_call_target="tpu_custom_call" | custom-call | tf_op jit(solution)/shard_map/backward/pallas_call | solution.py:511
  243.6 12.0 %unpack.1 = bf16[16,16,96,128]{3,2,1,0:T(8,128)(2,1)} custom-call(s32[1,1,8]{2,1,0:T(1,128)} %live_ref.13, bf16[1536,512]{1,0:T(8,128)(2,1)} %backward.1.in_ref), custom_call_target="tpu_custom_call" | custom-call | tf_op jit(solution)/shard_map/unpack/pallas_call | solution.py:538
  256.5 3.1 %finish.1 = f32[27,96,96]{2,1,0:T(8,128)} custom-call(f32[2048,128]{1,0:T(8,128)} %bitcast.14, f32[8,128]{1,0:T(8,128)} %get-tuple-element.51.small_ref), custom_call_target="tpu_custom_call" | custom-call | tf_op jit(solution)/shard_map/finish/pallas_call | solution.py:566
  (85 shorter events, 13.2 us)
Async XLA Ops:
  0.6 31.0 %copy-start.2 = (bf16[27,96,96]{2,1,0:T(8,128)(2,1)S(1)}, bf16[27,96,96]{2,1,0:T(8,128)(2,1)}, u32[]{:S(2)}) copy-start(bf16[27,96,96]{2,1,0:T(8,128)(2,1)} %param.9) | copy-start | bytes 1492996
  14.2 18.2 %collective-permute-start.4 = (bf16[112,128]{1,0:T(8,128)(2,1)}, bf16[112,128]{1,0:T(8,128)(2,1)S(1)}, u32[]{:S(2)}, u32[]{:S(2)}) collective-permute-start(bf16[112,128]{1,0:T(8,128)(2,1)} %get-tuple-element.33), channel_id=1, source_target_pairs={{0,17},{1,18},{2,19},{3,20},{4,21},{5,22},{6,23},{7,24},{8,25},{9,... | collective-permute-start | bytes 86024 | tf_op jit(solution)/shard_map/ppermute | solution.py:191
  19.2 15.5 %collective-permute-start.5 = (bf16[112,128]{1,0:T(8,128)(2,1)}, bf16[112,128]{1,0:T(8,128)(2,1)S(1)}, u32[]{:S(2)}, u32[]{:S(2)}) collective-permute-start(bf16[112,128]{1,0:T(8,128)(2,1)} %get-tuple-element.34), channel_id=1, source_target_pairs={{1,16},{2,17},{3,18},{4,19},{5,20},{6,21},{7,22},{8,23},{9,24},{10... | collective-permute-start | bytes 86024 | tf_op jit(solution)/shard_map/ppermute | solution.py:191
  21.1 16.5 %collective-permute-start.6 = (bf16[112,128]{1,0:T(8,128)(2,1)}, bf16[112,128]{1,0:T(8,128)(2,1)S(1)}, u32[]{:S(2)}, u32[]{:S(2)}) collective-permute-start(bf16[112,128]{1,0:T(8,128)(2,1)} %get-tuple-element.35), channel_id=1, source_target_pairs={{16,1},{17,2},{18,3},{19,4},{20,5},{21,6},{22,7},{23,8},{24,9},{25... | collective-permute-start | bytes 86024 | tf_op jit(solution)/shard_map/ppermute | solution.py:191
  26.9 19.2 %collective-permute-start = (bf16[112,512]{1,0:T(8,128)(2,1)}, bf16[112,512]{1,0:T(8,128)(2,1)S(1)}, u32[]{:S(2)}, u32[]{:S(2)}) collective-permute-start(bf16[112,512]{1,0:T(8,128)(2,1)} %get-tuple-element.29), channel_id=1, source_target_pairs={{0,16},{1,17},{2,18},{3,19},{4,20},{5,21},{6,22},{7,23},{8,24},{9,... | collective-permute-start | bytes 344072 | tf_op jit(solution)/shard_map/ppermute | solution.py:191
  29.7 16.4 %collective-permute-start.1 = (bf16[112,512]{1,0:T(8,128)(2,1)}, bf16[112,512]{1,0:T(8,128)(2,1)S(1)}, u32[]{:S(2)}, u32[]{:S(2)}) collective-permute-start(bf16[112,512]{1,0:T(8,128)(2,1)} %get-tuple-element.30), channel_id=1, source_target_pairs={{16,0},{17,1},{18,2},{19,3},{20,4},{21,5},{22,6},{23,7},{24,8},{25... | collective-permute-start | bytes 344072 | tf_op jit(solution)/shard_map/ppermute | solution.py:191
  32.3 13.8 %copy-start.11 = (bf16[112,128]{1,0:T(8,128)(2,1)}, bf16[112,128]{1,0:T(8,128)(2,1)S(1)}, u32[]{:S(2)}) copy-start(bf16[112,128]{1,0:T(8,128)(2,1)S(1)} %collective-permute-done.4.refs_4_) | copy-start | bytes 86020
  32.3 13.8 %collective-permute-start.2 = (bf16[112,512]{1,0:T(8,128)(2,1)}, bf16[112,512]{1,0:T(8,128)(2,1)S(1)}, u32[]{:S(2)}, u32[]{:S(2)}) collective-permute-start(bf16[112,512]{1,0:T(8,128)(2,1)} %get-tuple-element.31), channel_id=1, source_target_pairs={{0,1},{1,2},{2,3},{3,4},{4,5},{5,6},{6,7},{7,8},{8,9},{9,10},{10,1... | collective-permute-start | bytes 344072 | tf_op jit(solution)/shard_map/ppermute | solution.py:191
  34.7 11.5 %copy-start.12 = (bf16[112,128]{1,0:T(8,128)(2,1)}, bf16[112,128]{1,0:T(8,128)(2,1)S(1)}, u32[]{:S(2)}) copy-start(bf16[112,128]{1,0:T(8,128)(2,1)S(1)} %collective-permute-done.5.refs_5_) | copy-start | bytes 86020
  34.7 11.5 %collective-permute-start.3 = (bf16[112,512]{1,0:T(8,128)(2,1)}, bf16[112,512]{1,0:T(8,128)(2,1)S(1)}, u32[]{:S(2)}, u32[]{:S(2)}) collective-permute-start(bf16[112,512]{1,0:T(8,128)(2,1)} %get-tuple-element.32), channel_id=1, source_target_pairs={{1,0},{2,1},{3,2},{4,3},{5,4},{6,5},{7,6},{8,7},{9,8},{10,9},{11,1... | collective-permute-start | bytes 344072 | tf_op jit(solution)/shard_map/ppermute | solution.py:191
  37.7 8.4 %collective-permute-start.7 = (bf16[112,128]{1,0:T(8,128)(2,1)}, bf16[112,128]{1,0:T(8,128)(2,1)S(1)}, u32[]{:S(2)}, u32[]{:S(2)}) collective-permute-start(bf16[112,128]{1,0:T(8,128)(2,1)} %get-tuple-element.36), channel_id=1, source_target_pairs={{17,0},{18,1},{19,2},{20,3},{21,4},{22,5},{23,6},{24,7},{25,8},{26... | collective-permute-start | bytes 86024 | tf_op jit(solution)/shard_map/ppermute | solution.py:191
  70.7 22.4 %all-to-all-start = ((f32[128,8,128]{2,1,0:T(8,128)}), f32[128,8,128]{2,1,0:T(8,128)S(1)}, u32[]{:S(2)}, u32[]{:S(2)}) async-start(f32[128,8,128]{2,1,0:T(8,128)} %broadcast_in_dim.10), calls=%async_computation | async-start | bytes 1048576 | tf_op jit(solution)/shard_map/all_to_all | solution.py:579
  80.4 12.1 %copy-start.19 = (f32[96]{0:T(128)S(1)}, f32[96]{0:T(128)}, u32[]{:S(2)}) copy-start(f32[96]{0:T(128)} %param.11) | copy-start | bytes 1156
  80.4 12.1 %copy-start.20 = (f32[96]{0:T(128)S(1)}, f32[96]{0:T(128)}, u32[]{:S(2)}) copy-start(f32[96]{0:T(128)} %param.10) | copy-start | bytes 1156
  152.1 31.3 %copy-start.28 = (bf16[112,128]{1,0:T(8,128)(2,1)S(1)}, bf16[112,128]{1,0:T(8,128)(2,1)}, u32[]{:S(2)}) copy-start(bf16[112,128]{1,0:T(8,128)(2,1)} %get-tuple-element.47) | copy-start | bytes 86020
  152.1 35.8 %copy-start.27 = (bf16[112,128]{1,0:T(8,128)(2,1)S(1)}, bf16[112,128]{1,0:T(8,128)(2,1)}, u32[]{:S(2)}) copy-start(bf16[112,128]{1,0:T(8,128)(2,1)} %get-tuple-element.48) | copy-start | bytes 86020
  152.1 37.9 %copy-start.26 = (bf16[112,128]{1,0:T(8,128)(2,1)S(1)}, bf16[112,128]{1,0:T(8,128)(2,1)}, u32[]{:S(2)}) copy-start(bf16[112,128]{1,0:T(8,128)(2,1)} %get-tuple-element.49) | copy-start | bytes 86020
  177.7 23.9 %copy-start.24 = (bf16[112,512]{1,0:T(8,128)(2,1)S(1)}, bf16[112,512]{1,0:T(8,128)(2,1)}, u32[]{:S(2)}) copy-start(bf16[112,512]{1,0:T(8,128)(2,1)} %get-tuple-element.45) | copy-start | bytes 344068
  177.7 25.8 %copy-start.23 = (bf16[112,512]{1,0:T(8,128)(2,1)S(1)}, bf16[112,512]{1,0:T(8,128)(2,1)}, u32[]{:S(2)}) copy-start(bf16[112,512]{1,0:T(8,128)(2,1)} %get-tuple-element.46) | copy-start | bytes 344068
  177.7 29.2 %copy-start.22 = (bf16[112,512]{1,0:T(8,128)(2,1)S(1)}, bf16[112,512]{1,0:T(8,128)(2,1)}, u32[]{:S(2)}) copy-start(bf16[112,512]{1,0:T(8,128)(2,1)} %get-tuple-element.43) | copy-start | bytes 344068
  177.7 32.9 %copy-start.21 = (bf16[112,512]{1,0:T(8,128)(2,1)S(1)}, bf16[112,512]{1,0:T(8,128)(2,1)}, u32[]{:S(2)}) copy-start(bf16[112,512]{1,0:T(8,128)(2,1)} %get-tuple-element.44) | copy-start | bytes 344068
  177.7 34.9 %copy-start.25 = (bf16[112,128]{1,0:T(8,128)(2,1)S(1)}, bf16[112,128]{1,0:T(8,128)(2,1)}, u32[]{:S(2)}) copy-start(bf16[112,128]{1,0:T(8,128)(2,1)} %get-tuple-element.50) | copy-start | bytes 86020
  177.7 77.8 %all-to-all-start.3 = ((f32[128,16,128]{2,1,0:T(8,128)}), f32[128,16,128]{2,1,0:T(8,128)S(1)}, u32[]{:S(2)}, u32[]{:S(2)}) async-start(f32[128,16,128]{2,1,0:T(8,128)} %broadcast_in_dim.28), calls=%async_computation.3 | async-start | bytes 2097152 | tf_op jit(solution)/shard_map/all_to_all | solution.py:588
  183.4 23.5 %collective-permute-start.12 = (bf16[112,128]{1,0:T(8,128)(2,1)S(1)}, bf16[112,128]{1,0:T(8,128)(2,1)S(1)}, u32[]{:S(2)}, u32[]{:S(2)}) collective-permute-start(bf16[112,128]{1,0:T(8,128)(2,1)S(1)} %copy-done.28), channel_id=1, source_target_pairs={{0,17},{1,18},{2,19},{3,20},{4,21},{5,22},{6,23},{7,24},{8,25},{9,... | collective-permute-start | bytes 86024 | tf_op jit(solution)/shard_map/ppermute | solution.py:191
  187.9 22.7 %collective-permute-start.13 = (bf16[112,128]{1,0:T(8,128)(2,1)S(1)}, bf16[112,128]{1,0:T(8,128)(2,1)S(1)}, u32[]{:S(2)}, u32[]{:S(2)}) collective-permute-start(bf16[112,128]{1,0:T(8,128)(2,1)S(1)} %copy-done.27), channel_id=1, source_target_pairs={{1,16},{2,17},{3,18},{4,19},{5,20},{6,21},{7,22},{8,23},{9,24},{10... | collective-permute-start | bytes 86024 | tf_op jit(solution)/shard_map/ppermute | solution.py:191
  190.0 22.6 %collective-permute-start.14 = (bf16[112,128]{1,0:T(8,128)(2,1)S(1)}, bf16[112,128]{1,0:T(8,128)(2,1)S(1)}, u32[]{:S(2)}, u32[]{:S(2)}) collective-permute-start(bf16[112,128]{1,0:T(8,128)(2,1)S(1)} %copy-done.26), channel_id=1, source_target_pairs={{16,1},{17,2},{18,3},{19,4},{20,5},{21,6},{22,7},{23,8},{24,9},{25... | collective-permute-start | bytes 86024 | tf_op jit(solution)/shard_map/ppermute | solution.py:191
  201.6 19.5 %collective-permute-start.10 = (bf16[112,512]{1,0:T(8,128)(2,1)S(1)}, bf16[112,512]{1,0:T(8,128)(2,1)S(1)}, u32[]{:S(2)}, u32[]{:S(2)}) collective-permute-start(bf16[112,512]{1,0:T(8,128)(2,1)S(1)} %copy-done.24), channel_id=1, source_target_pairs={{0,1},{1,2},{2,3},{3,4},{4,5},{5,6},{6,7},{7,8},{8,9},{9,10},{10,1... | collective-permute-start | bytes 344072 | tf_op jit(solution)/shard_map/ppermute | solution.py:191
  203.5 17.6 %collective-permute-start.11 = (bf16[112,512]{1,0:T(8,128)(2,1)S(1)}, bf16[112,512]{1,0:T(8,128)(2,1)S(1)}, u32[]{:S(2)}, u32[]{:S(2)}) collective-permute-start(bf16[112,512]{1,0:T(8,128)(2,1)S(1)} %copy-done.23), channel_id=1, source_target_pairs={{1,0},{2,1},{3,2},{4,3},{5,4},{6,5},{7,6},{8,7},{9,8},{10,9},{11,1... | collective-permute-start | bytes 344072 | tf_op jit(solution)/shard_map/ppermute | solution.py:191
  206.9 14.2 %copy-start.15 = (bf16[112,128]{1,0:T(8,128)(2,1)}, bf16[112,128]{1,0:T(8,128)(2,1)S(1)}, u32[]{:S(2)}) copy-start(bf16[112,128]{1,0:T(8,128)(2,1)S(1)} %collective-permute-done.12.refs_4_) | copy-start | bytes 86020
  206.9 14.2 %collective-permute-start.8 = (bf16[112,512]{1,0:T(8,128)(2,1)S(1)}, bf16[112,512]{1,0:T(8,128)(2,1)S(1)}, u32[]{:S(2)}, u32[]{:S(2)}) collective-permute-start(bf16[112,512]{1,0:T(8,128)(2,1)S(1)} %copy-done.22), channel_id=1, source_target_pairs={{0,16},{1,17},{2,18},{3,19},{4,20},{5,21},{6,22},{7,23},{8,24},{9,... | collective-permute-start | bytes 344072 | tf_op jit(solution)/shard_map/ppermute | solution.py:191
  210.6 10.5 %collective-permute-start.9 = (bf16[112,512]{1,0:T(8,128)(2,1)S(1)}, bf16[112,512]{1,0:T(8,128)(2,1)S(1)}, u32[]{:S(2)}, u32[]{:S(2)}) collective-permute-start(bf16[112,512]{1,0:T(8,128)(2,1)S(1)} %copy-done.21), channel_id=1, source_target_pairs={{16,0},{17,1},{18,2},{19,3},{20,4},{21,5},{22,6},{23,7},{24,8},{25... | collective-permute-start | bytes 344072 | tf_op jit(solution)/shard_map/ppermute | solution.py:191
  212.6 8.5 %collective-permute-start.15 = (bf16[112,128]{1,0:T(8,128)(2,1)S(1)}, bf16[112,128]{1,0:T(8,128)(2,1)S(1)}, u32[]{:S(2)}, u32[]{:S(2)}) collective-permute-start(bf16[112,128]{1,0:T(8,128)(2,1)S(1)} %copy-done.25), channel_id=1, source_target_pairs={{17,0},{18,1},{19,2},{20,3},{21,4},{22,5},{23,6},{24,7},{25,8},{26... | collective-permute-start | bytes 86024 | tf_op jit(solution)/shard_map/ppermute | solution.py:191
  (15 other events, 36.3 us)

commit v2 on v0

v2 whole, which is shorter than its diff:
```python
import functools

import jax
import jax.numpy as jnp
from jax import lax
from jax.experimental import pallas as pl
from jax.experimental.pallas import tpu as pltpu
from jax.sharding import PartitionSpec as P

B = 16
C = 96
NB = 8
W2 = 512
ROWS = 20 * C
EDGE = C + 16
F32 = jnp.float32
BF16 = jnp.bfloat16
AXES = ("gx", "gy")


def params(mib=56):
    return pltpu.CompilerParams(vmem_limit_bytes=mib * 1024 * 1024)


def vmem():
    return pl.BlockSpec(memory_space=pltpu.VMEM)


def smem():
    return pl.BlockSpec(memory_space=pltpu.SMEM)


def iota(shape, dim):
    return lax.broadcasted_iota(jnp.int32, shape, dim)


def slots(live_ref):
    first = jnp.int32(-1)
    second = jnp.int32(-1)
    for j in reversed(range(NB)):
        on = live_ref[0, 0, j] > 0
        second = jnp.where(on, first, second)
        first = jnp.where(on, jnp.int32(j), first)
    first = jnp.maximum(first, 0)
    spare = jnp.bitwise_and(first + 1, NB - 1)
    return first, jnp.where(second >= 0, second, spare)


def wrap(shift):
    return jnp.bitwise_and(shift + 256, 127)


def lane_parts(shape):
    lane = iota(shape, 1)
    return lane >> 6, (lane >> 4) & 3, lane & 15


def scaled(tile, row):
    return (tile.reshape(C // 16, 16, 128) * row[None]).reshape(C, 128)


def flags(cond):
    return jnp.where(cond, 1.0, 0.0).astype(BF16)


def by_slot(first, second, shape=(16, 128)):
    return jnp.where(lane_parts(shape)[0] == 0, first, second)


def fill_selector(sel_ref, ids):
    row = iota((512, 128), 0)
    slot, group, deep = lane_parts((512, 128))
    start = jnp.where(slot == 0, ids[0], ids[1]) * B
    sel_ref[...] = flags(((row >> 7) == group) & ((row & 127) == start + deep))


def emit_sides(x, tiles, ids, sides):
    xa, xb, ya, yb = sides
    odd_x = lax.axis_index("gx") % 2
    odd_y = lax.axis_index("gy") % 2
    group = lane_parts((C, 128))[1]

    @pl.when(x == 0)
    def _():
        tag = by_slot(ids[0], ids[1]).astype(F32).astype(BF16)
        for face in sides:
            for k in range(4):
                face[C:EDGE, k * 128 : (k + 1) * 128] = tag

    for face, where in ((xa, jnp.where(odd_x == 1, 0, B - 1)), (xb, jnp.where(odd_x == 1, B - 1, 0))):

        @pl.when(x == where)
        def _(face=face):
            for k in range(4):
                face[0:C, k * 128 : (k + 1) * 128] = tiles[k]

    spot = x // 4
    lanes = pl.ds(pl.multiple_of(lax.rem(x, 4) * 128, 128), 128)
    low = pltpu.roll(tiles[0], wrap(16 * spot), 1)
    high = pltpu.roll(tiles[3], wrap(16 * spot - 48), 1)
    for face, flip in ((ya, 1), (yb, 0)):
        moved = jnp.where(odd_y == flip, low, high)
        face[0:C, lanes] = jnp.where(group == spot, moved, face[0:C, lanes])


SIDES = [jax.ShapeDtypeStruct((EDGE, W2), BF16)] * 4


PACE = 4


def paced():
    return pl.BlockSpec((PACE * C, W2), lambda t: (t, 0))


def paced_mask():
    return pl.BlockSpec((PACE, 1, W2), lambda t: (t, 0, 0))


def whole(shape):
    return pl.BlockSpec(shape, lambda *a: (0,) * len(shape))


def pack_features_kernel(live_ref, feat_ref, mask_ref, out_ref, live_out, *refs):
    sides, (sel_ref, lhs_ref) = refs[:4], refs[4:]
    t = pl.program_id(0)
    ids = slots(live_ref)

    @pl.when(t == 0)
    def _():
        fill_selector(sel_ref, ids)

    brick = iota((B, 128), 1) >> 4
    column = jnp.zeros((B, 128), F32)
    for j in range(NB):
        column = jnp.where(brick == j, live_ref[0, 0, j].astype(F32), column)
    for u in range(PACE):
        cells = mask_ref[u].astype(F32) * column
        for y in range(B):
            row = jnp.broadcast_to(cells[y : y + 1, :], (16, 128)).astype(BF16)
            base, lanes = (4 * u + y % 4) * EDGE, slice((y // 4) * 128, (y // 4 + 1) * 128)
            lhs_ref[base : base + C, lanes] = scaled(feat_ref[u, y], row)
            lhs_ref[base + C : base + EDGE, lanes] = row
    moved = jnp.dot(lhs_ref[...], sel_ref[...], preferred_element_type=F32)
    for u in range(PACE):
        tiles = []
        for m in range(4):
            lanes = slice(m * 128, (m + 1) * 128)
            base = (4 * u + m) * EDGE
            tile = moved[base : base + C].astype(BF16)
            out_ref[u * C : (u + 1) * C, lanes] = tile
            live_out[u, :, lanes] = moved[base + C : base + C + 1]
            tiles.append(tile)
        emit_sides(PACE * t + u, tiles, ids, sides)


def pack_features(live, features, mask):
    return pl.pallas_call(
        pack_features_kernel,
        grid=(B // PACE,),
        in_specs=[
            smem(),
            pl.BlockSpec((PACE, B, C, 128), lambda t: (t, 0, 0, 0)),
            pl.BlockSpec((PACE, B, 128), lambda t: (t, 0, 0)),
        ],
        out_specs=[paced(), paced_mask()]
        + [whole(f.shape) for f in SIDES],
        out_shape=[
            jax.ShapeDtypeStruct((B * C, W2), BF16),
            jax.ShapeDtypeStruct((B, 1, W2), F32),
        ]
        + SIDES,
        scratch_shapes=[pltpu.VMEM((512, 128), BF16), pltpu.VMEM((PACE * 4 * EDGE, 512), BF16)],
        compiler_params=params(),
        name="pack_features",
    )(live, features, mask)


def pack_plain_kernel(live_ref, feat_ref, out_ref, sel_ref, lhs_ref):
    ids = slots(live_ref)

    @pl.when(pl.program_id(0) == 0)
    def _():
        fill_selector(sel_ref, ids)

    for u in range(PACE):
        for y in range(B):
            base, lanes = (4 * u + y % 4) * C, slice((y // 4) * 128, (y // 4 + 1) * 128)
            lhs_ref[base : base + C, lanes] = feat_ref[u, y]
    moved = jnp.dot(lhs_ref[...], sel_ref[...], preferred_element_type=F32)
    for u in range(PACE):
        for m in range(4):
            base = (4 * u + m) * C
            out_ref[u * C : (u + 1) * C, m * 128 : (m + 1) * 128] = moved[base : base + C].astype(
                BF16
            )


def pack_plain(live, values):
    return pl.pallas_call(
        pack_plain_kernel,
        grid=(B // PACE,),
        in_specs=[smem(), pl.BlockSpec((PACE, B, C, 128), lambda t: (t, 0, 0, 0))],
        out_specs=paced(),
        out_shape=jax.ShapeDtypeStruct((B * C, W2), BF16),
        scratch_shapes=[pltpu.VMEM((512, 128), BF16), pltpu.VMEM((PACE * 4 * C, 512), BF16)],
        compiler_params=params(),
        name="pack_cotangent",
    )(live, values)


def pick(odd, first, second):
    return jnp.where(odd == 1, first, second), jnp.where(odd == 1, second, first)


def relay_kernel(xa, xb, ya, yb, ya_out, yb_out):
    odd_x = lax.axis_index("gx") % 2
    odd_y = lax.axis_index("gy") % 2
    group = lane_parts((EDGE, 128))[1]
    zero = jnp.zeros((EDGE, 128), BF16)
    edges = []
    for tile, turn in ((0, 0), (3, 80)):
        lanes = slice(tile * 128, (tile + 1) * 128)
        below, above = pick(odd_x, xa[:, lanes], xb[:, lanes])
        if turn:
            below = pltpu.roll(below, turn, 1)
        above = pltpu.roll(above, (turn + 16) % 128, 1)
        edges.append(jnp.where(group == 0, below, jnp.where(group == 1, above, zero)))
    high_first = jnp.where(odd_y == 1, edges[0], edges[1])
    low_first = jnp.where(odd_y == 1, edges[1], edges[0])
    ya_out[:, 0:W2] = ya[...]
    yb_out[:, 0:W2] = yb[...]
    ya_out[:, W2:640] = high_first
    yb_out[:, W2:640] = low_first


def relay(xa, xb, ya, yb):
    return pl.pallas_call(
        relay_kernel,
        in_specs=[vmem()] * 4,
        out_specs=[vmem()] * 2,
        out_shape=[jax.ShapeDtypeStruct((EDGE, 640), BF16)] * 2,
        compiler_params=params(),
        name="relay",
    )(xa, xb, ya, yb)


def swap(values, axis, first):
    count = lax.axis_size(axis)
    pairs = []
    for i in range(count):
        j = i ^ 1 if first else ((i + 1) ^ 1) - 1
        if 0 <= j < count:
            pairs.append((i, j))
    return lax.ppermute(values, axis, pairs)


def exchange(sides, beside):
    xa, xb, ya, yb = sides
    xa = swap(xa, "gx", True)
    xb = swap(xb, "gx", False)
    xa, xb, beside = lax.optimization_barrier((xa, xb, beside))
    ya, yb = relay(xa, xb, ya, yb)
    return (xa, xb, swap(ya, "gy", True), swap(yb, "gy", False)), beside


HALO = [(EDGE, W2), (EDGE, W2), (EDGE, 640), (EDGE, 640)]


class Columns:
    def __init__(self, ids, halo, edge_ref, rows_ref):
        self.halo, self.edge_ref, self.rows_ref = halo, edge_ref, rows_ref
        self.ids = ids
        slot, group, deep = lane_parts((16, 128))
        after = (ids[1] == ids[0] + 1) & (ids[1] > 0)
        near = jnp.where(after, 1, 0)
        self.keep_low = flags(deep > 0)
        self.keep_high = flags(deep < 15)
        self.at_low = flags(deep == 0)
        self.at_high = flags(deep == 15)
        self.from_next = flags((deep == 15) & (slot < near))
        self.from_last = flags((deep == 0) & (slot + near == 2))
        self.first = flags(group == 0)
        self.not_first = flags(group > 0)
        self.last = flags(group == 3)
        self.not_last = flags(group < 3)

    def prepare(self):
        xa, xb, ya, yb = self.halo
        odd_x = lax.axis_index("gx") % 2
        odd_y = lax.axis_index("gy") % 2
        mine = by_slot(self.ids[0], self.ids[1]).astype(F32)

        def shifted(cells):
            tag = cells[C:EDGE].astype(F32)
            turned = pltpu.roll(tag, 64, 1)
            body = cells[0:C]
            other = pltpu.roll(body, 64, 1)
            under, here, over = [
                scaled(body, flags(tag == mine + d)) + scaled(other, flags(turned == mine + d))
                for d in (-1.0, 0.0, 1.0)
            ]
            return (
                scaled(pltpu.roll(here, 1, 1), self.keep_low)
                + scaled(pltpu.roll(under, 113, 1), self.at_low),
                here,
                scaled(pltpu.roll(here, 127, 1), self.keep_high)
                + scaled(pltpu.roll(over, 15, 1), self.at_high),
            )

        def lanes(k):
            return slice(k * 128, (k + 1) * 128)

        for k in range(5):
            for way, cells in enumerate(pick(odd_y, ya[:, lanes(k)], yb[:, lanes(k)])):
                for dz, tile in enumerate(shifted(cells)):
                    self.rows_ref[way, dz, :, lanes(k)] = tile
        for k in range(4):
            for way, cells in enumerate(pick(odd_x, xa[:, lanes(k)], xb[:, lanes(k)])):
                for dz, tile in enumerate(shifted(cells)):
                    self.edge_ref[way, dz, :, lanes(k)] = tile

    def store(self, cols, dz, tiles, below, above):
        head = scaled(pltpu.roll(tiles[3], 16, 1), self.not_first) + scaled(below, self.first)
        tail = scaled(pltpu.roll(tiles[0], 112, 1), self.not_last) + scaled(above, self.last)
        line = [head] + list(tiles) + [tail]
        for dy in range(3):
            k = dy * 3 + dz
            for m in range(4):
                cols[k * C : (k + 1) * C, m * 128 : (m + 1) * 128] = line[dy + m]

    def edge(self, way, cols):
        for dz in range(3):
            tiles = [self.edge_ref[way, dz, :, m * 128 : (m + 1) * 128] for m in range(4)]
            low = self.rows_ref[0, dz, :, W2:640]
            high = self.rows_ref[1, dz, :, W2:640]
            self.store(
                cols,
                dz,
                tiles,
                pltpu.roll(low, 112, 1) if way else low,
                pltpu.roll(high, 32 if way else 48, 1),
            )

    def inner(self, x, body, cols):
        here = [body[:, m * 128 : (m + 1) * 128] for m in range(4)]
        spot = x // 4
        lanes = pl.ds(pl.multiple_of(lax.rem(x, 4) * 128, 128), 128)
        for dz in range(3):
            if dz == 0:
                tiles = [
                    scaled(pltpu.roll(t, 1, 1), self.keep_low)
                    + scaled(pltpu.roll(t, 49, 1), self.from_last)
                    for t in here
                ]
            elif dz == 1:
                tiles = here
            else:
                tiles = [
                    scaled(pltpu.roll(t, 127, 1), self.keep_high)
                    + scaled(pltpu.roll(t, 79, 1), self.from_next)
                    for t in here
                ]
            below = pltpu.roll(self.rows_ref[0, dz, :, lanes], wrap(-16 * spot), 1)
            above = pltpu.roll(self.rows_ref[1, dz, :, lanes], wrap(48 - 16 * spot), 1)
            self.store(cols, dz, tiles, below, above)


ASSEMBLY = [
    pltpu.VMEM((2, 3, C, W2), BF16),
    pltpu.VMEM((2, 3, C, 640), BF16),
    pltpu.VMEM((2, 9 * C, W2), BF16),
]
STEPS = B // 2 + 1


def run_planes(live_ref, body_ref, halo, edge_ref, rows_ref, cols_ref, use):
    t = pl.program_id(0)
    ids = slots(live_ref)
    columns = Columns(ids, halo, edge_ref, rows_ref)
    even, odd = cols_ref.at[0], cols_ref.at[1]

    @pl.when(t == 0)
    def _():
        columns.prepare()
        columns.edge(0, even)

    @pl.when(t < STEPS - 1)
    def _():
        columns.inner(2 * t, body_ref[0:C, :], odd)
        use(2 * t, even)
        columns.inner(2 * t + 1, body_ref[C : 2 * C, :], even)
        use(2 * t + 1, odd)

    @pl.when(t == STEPS - 1)
    def _():
        columns.edge(1, odd)
        use(2 * t, even)
        use(2 * t + 1, odd)


def plane_block():
    return pl.BlockSpec((2 * C, W2), lambda t: (jnp.minimum(t, B // 2 - 1), 0))


def late_block():
    return pl.BlockSpec((2 * C, W2), lambda t: (jnp.maximum(t - 1, 0), 0))


def fold(values):
    return (values[:, 0:128] + values[:, 128:256]) + (values[:, 256:384] + values[:, 384:512])


def to_row(column_tile):
    column = jnp.sum(column_tile, axis=1, keepdims=True)
    diag = iota((C, 128), 0) == iota((C, 128), 1)
    return jnp.sum(jnp.where(diag, column, 0.0), axis=0, keepdims=True)


def to_column(row):
    diag = iota((C, 128), 0) == iota((C, 128), 1)
    return jnp.sum(jnp.where(diag, row, 0.0), axis=1, keepdims=True)


def add_product(weight_ref, sums):
    def use(i, cols):
        part = jnp.dot(weight_ref[...], cols[...], preferred_element_type=F32)
        rows = pl.ds(pl.multiple_of(i * C, C), 3 * C)
        sums[rows, :] += part

    return use


def forward_kernel(live_ref, body_ref, *refs):
    halo, (weight_ref, mask_ref, pre_ref, stat_ref) = refs[:4], refs[4:8]
    edge_ref, rows_ref, cols_ref, sums, acc = refs[8:]
    t = pl.program_id(0)

    @pl.when(t == 0)
    def _():
        sums[...] = jnp.zeros_like(sums)
        acc[...] = jnp.zeros_like(acc)

    run_planes(
        live_ref, body_ref, halo, edge_ref, rows_ref, cols_ref, add_product(weight_ref, sums)
    )

    @pl.when(t > 0)
    def _():
        for u in range(2):
            values = sums[pl.ds(pl.multiple_of((2 * t + u) * C, C), C), :]
            mask = mask_ref[2 * t - 2 + u]
            held = values * mask
            pre_ref[u * C : (u + 1) * C, :] = values
            acc[0] += fold(held)
            acc[1] += fold(held * values)
            acc[2, 0:1, :] += fold(mask)

    @pl.when(t == STEPS - 1)
    def _():
        stat_ref[...] = jnp.zeros_like(stat_ref)
        stat_ref[0:1, :] = to_row(acc[0])
        stat_ref[1:2, :] = to_row(acc[1])
        stat_ref[2:3, :] = jnp.full((1, 128), 1.0, F32) * jnp.sum(acc[2, 0:1, :])


def forward(live, body, halo, weight, mask):
    return pl.pallas_call(
        forward_kernel,
        grid=(STEPS,),
        in_specs=[smem(), plane_block()]
        + [whole(h) for h in HALO]
        + [whole(weight.shape), whole(mask.shape)],
        out_specs=[late_block(), whole((8, 128))],
        out_shape=[
            jax.ShapeDtypeStruct((B * C, W2), F32),
            jax.ShapeDtypeStruct((8, 128), F32),
        ],
        scratch_shapes=ASSEMBLY + [pltpu.VMEM((ROWS, W2), F32), pltpu.VMEM((3, C, 128), F32)],
        compiler_params=params(),
        name="forward",
    )(live, body, *halo, weight, mask)


def moments(stat_ref):
    total = jnp.sum(stat_ref[...], axis=0)
    voxels = total[2:3, :]
    mean = total[0:1, :] / voxels
    var = total[1:2, :] / voxels - mean * mean
    return voxels, mean, lax.rsqrt(var + 1e-05)


def slope_kernel(
    stat_ref, pre_ref, cot_ref, mask_ref, gain_ref, shift_ref, gz_ref, out_ref, col_ref, acc
):
    t = pl.program_id(0)

    @pl.when(t == 0)
    def _():
        voxels, mean, inv = moments(stat_ref)
        for k, row in enumerate((mean, inv, gain_ref[...], shift_ref[...])):
            col_ref[k] = jnp.broadcast_to(to_column(row), (C, 128))
        acc[...] = jnp.zeros_like(acc)

    mean, inv, gain, shift = [col_ref[k] for k in range(4)]
    total = acc[0]
    cross = acc[1]
    for u in range(PACE):
        rows = slice(u * C, (u + 1) * C)
        for k in range(4):
            lanes = slice(k * 128, (k + 1) * 128)
            normed = (pre_ref[rows, lanes] - mean) * inv
            zed = gain * normed + shift
            sig = 0.5 + 0.5 * jnp.tanh(0.5 * zed)
            gz = (
                mask_ref[u][:, lanes]
                * cot_ref[rows, lanes].astype(F32)
                * (sig * (1.0 + zed * (1.0 - sig)))
            )
            gz_ref[rows, lanes] = gz
            total += gz
            cross += gz * normed
    acc[0] = total
    acc[1] = cross

    @pl.when(t == B // PACE - 1)
    def _():
        out_ref[...] = jnp.zeros_like(out_ref)
        out_ref[0:1, :] = to_row(acc[0])
        out_ref[1:2, :] = to_row(acc[1])


def slope(stats, pre, cot, mask, gain, shift):
    return pl.pallas_call(
        slope_kernel,
        grid=(B // PACE,),
        in_specs=[
            whole(stats.shape),
            paced(),
            paced(),
            paced_mask(),
            whole((1, 128)),
            whole((1, 128)),
        ],
        out_specs=[paced(), whole((8, 128))],
        out_shape=[
            jax.ShapeDtypeStruct((B * C, W2), F32),
            jax.ShapeDtypeStruct((8, 128), F32),
        ],
        scratch_shapes=[pltpu.VMEM((4, C, 128), F32), pltpu.VMEM((2, C, 128), F32)],
        compiler_params=params(),
        name="slope",
    )(stats, pre, cot, mask, gain, shift)


def pre_grad_kernel(
    live_ref, stat_ref, stat2_ref, pre_ref, gz_ref, mask_ref, gain_ref, out_ref, small_ref, *refs
):
    sides, (col_ref,) = refs[:4], refs[4:]
    t = pl.program_id(0)
    ids = slots(live_ref)

    @pl.when(t == 0)
    def _():
        voxels, mean, inv = moments(stat_ref)
        total = jnp.sum(stat2_ref[...], axis=0)
        root = 1.0 / jnp.sqrt(voxels)
        small_ref[...] = jnp.zeros_like(small_ref)
        small_ref[0:1, :] = total[1:2, :] * root
        small_ref[1:2, :] = total[0:1, :] * root
        small_ref[2:3, :] = root
        rows = (mean, inv, gain_ref[...] * inv, total[0:1, :] / voxels, total[1:2, :] / voxels)
        for k, row in enumerate(rows):
            col_ref[k] = jnp.broadcast_to(to_column(row), (C, 128))

    mean, inv, scale, first, second = [col_ref[k] for k in range(5)]
    for u in range(PACE):
        rows = slice(u * C, (u + 1) * C)
        tiles = []
        for k in range(4):
            lanes = slice(k * 128, (k + 1) * 128)
            normed = (pre_ref[rows, lanes] - mean) * inv
            tile = (
                mask_ref[u][:, lanes] * scale * (gz_ref[rows, lanes] - first - normed * second)
            ).astype(BF16)
            out_ref[rows, lanes] = tile
            tiles.append(tile)
        emit_sides(PACE * t + u, tiles, ids, sides)


def pre_grad(live, stats, stats2, pre, gz, mask, gain):
    return pl.pallas_call(
        pre_grad_kernel,
        grid=(B // PACE,),
        in_specs=[
            smem(),
            whole(stats.shape),
            whole(stats2.shape),
            paced(),
            paced(),
            paced_mask(),
            whole((1, 128)),
        ],
        out_specs=[paced(), whole((8, 128))] + [whole(f.shape) for f in SIDES],
        out_shape=[
            jax.ShapeDtypeStruct((B * C, W2), BF16),
            jax.ShapeDtypeStruct((8, 128), F32),
        ]
        + SIDES,
        scratch_shapes=[pltpu.VMEM((5, C, 128), F32)],
        compiler_params=params(),
        name="pre_grad",
    )(live, stats, stats2, pre, gz, mask, gain)


def weight_kernel(live_ref, body_ref, *refs):
    halo, (grad_ref, out_ref) = refs[:4], refs[4:6]
    edge_ref, rows_ref, cols_ref, padded, total = refs[6:]
    t = pl.program_id(0)

    @pl.when(t == 0)
    def _():
        padded[0 : 2 * C, :] = jnp.zeros((2 * C, W2), BF16)
        padded[2 * C : 18 * C, :] = grad_ref[...]
        padded[18 * C : ROWS, :] = jnp.zeros((2 * C, W2), BF16)
        total[...] = jnp.zeros_like(total)

    def use(i, cols):
        rows = pl.ds(pl.multiple_of(i * C, C), 3 * C)
        total[...] += lax.dot_general(
            padded[rows, :], cols[...], (((1,), (1,)), ((), ())), preferred_element_type=F32
        )

    run_planes(live_ref, body_ref, halo, edge_ref, rows_ref, cols_ref, use)

    @pl.when(t == STEPS - 1)
    def _():
        for j in range(6):
            out_ref[j * 288 : (j + 1) * 288, :] = total[:, j * 128 : (j + 1) * 128]
        out_ref[6 * 288 : 2048, :] = jnp.zeros((2048 - 6 * 288, 128), F32)
        out_ref[6 * 288 : 7 * 288, 0:96] = total[:, 768:864]


def weight_terms(live, body, halo, grad):
    return pl.pallas_call(
        weight_kernel,
        grid=(STEPS,),
        in_specs=[smem(), plane_block()] + [whole(h) for h in HALO] + [whole(grad.shape)],
        out_specs=whole((2048, 128)),
        out_shape=jax.ShapeDtypeStruct((2048, 128), F32),
        scratch_shapes=ASSEMBLY
        + [pltpu.VMEM((ROWS, W2), BF16), pltpu.VMEM((3 * C, 9 * C), F32)],
        compiler_params=params(),
        name="weight_terms",
    )(live, body, *halo, grad)


def backward_kernel(live_ref, body_ref, *refs):
    halo, (weight_ref, mask_ref, out_ref) = refs[:4], refs[4:7]
    edge_ref, rows_ref, cols_ref, sums, spread = refs[7:]
    t = pl.program_id(0)

    @pl.when(t == 0)
    def _():
        sums[...] = jnp.zeros_like(sums)
        ids = slots(live_ref)
        row, lane = iota((128, W2), 0), iota((128, W2), 1)
        start = jnp.where((row >> 6) == 0, ids[0], ids[1]) * B
        spread[...] = flags(
            (((row >> 4) & 3) == (lane >> 7)) & ((lane & 127) == start + (row & 15))
        )

    run_planes(
        live_ref, body_ref, halo, edge_ref, rows_ref, cols_ref, add_product(weight_ref, sums)
    )

    @pl.when(t > 0)
    def _():
        for u in range(2):
            rows = pl.ds(pl.multiple_of((2 * t + u) * C, C), C)
            mask = mask_ref[2 * t - 2 + u]
            for m in range(4):
                lanes = slice(m * 128, (m + 1) * 128)
                tile = (sums[rows, lanes] * mask[:, lanes]).astype(BF16)
                moved = jnp.dot(tile, spread[...], preferred_element_type=F32)
                for g in range(4):
                    out_ref[u, 4 * g + m] = moved[:, g * 128 : (g + 1) * 128].astype(BF16)


def backward(live, body, halo, weight, mask):
    return pl.pallas_call(
        backward_kernel,
        grid=(STEPS,),
        in_specs=[smem(), plane_block()]
        + [whole(h) for h in HALO]
        + [whole(weight.shape), whole(mask.shape)],
        out_specs=pl.BlockSpec((2, B, C, 128), lambda t: (jnp.maximum(t - 1, 0), 0, 0, 0)),
        out_shape=jax.ShapeDtypeStruct((B, B, C, 128), BF16),
        scratch_shapes=ASSEMBLY + [pltpu.VMEM((ROWS, W2), F32), pltpu.VMEM((128, W2), BF16)],
        compiler_params=params(),
        name="backward",
    )(live, body, *halo, weight, mask)


def finish_kernel(sum_ref, small_ref, out_ref):
    root = small_ref[2:3, 0:C]
    for a in range(3):
        for k in range(9):
            start = k * C
            pieces = []
            while start < (k + 1) * C:
                j, off = start // 128, start % 128
                stop = min((k + 1) * C, (j + 1) * 128)
                row = j * 288 + (2 - a) * C
                pieces.append(sum_ref[row : row + C, off : off + stop - start].astype(F32))
                start = stop
            block = pieces[0] if len(pieces) == 1 else jnp.concatenate(pieces, axis=1)
            out_ref[9 * a + k] = block.T * root


def finish(sums, small):
    return pl.pallas_call(
        finish_kernel,
        in_specs=[vmem()] * 2,
        out_specs=vmem(),
        out_shape=jax.ShapeDtypeStruct((27, C, C), F32),
        compiler_params=params(),
        name="finish",
    )(sums, small)


def arrange_kernel(weight_ref, fwd_ref, back_ref):
    for a in range(3):
        for k in range(9):
            block = weight_ref[9 * a + k]
            fwd_ref[(2 - a) * C : (3 - a) * C, k * C : (k + 1) * C] = block.T
            back_ref[a * C : (a + 1) * C, (8 - k) * C : (9 - k) * C] = block


def arrange(weight):
    return pl.pallas_call(
        arrange_kernel,
        in_specs=[vmem()],
        out_specs=[vmem()] * 2,
        out_shape=[jax.ShapeDtypeStruct((3 * C, 9 * C), BF16)] * 2,
        compiler_params=params(),
        name="arrange",
    )(weight)


def gather_small(values):
    count = lax.axis_size("gx") * lax.axis_size("gy")
    spread = jnp.broadcast_to(values[None], (count,) + values.shape)
    return lax.all_to_all(spread, AXES, 0, 0, tiled=True)


def scatter_large(values):
    count = lax.axis_size("gx") * lax.axis_size("gy")
    parts = values.reshape(count, values.shape[0] // count, 128)
    return lax.all_to_all(parts, AXES, 0, 0, tiled=True)


def gather_large(parts):
    mine = jnp.sum(parts, axis=0)
    spread = jnp.broadcast_to(mine[None], parts.shape)
    return lax.all_to_all(spread, AXES, 0, 0, tiled=True).reshape(-1, 128)


def body(features, cotangent, weight, bn_gain, bn_shift, voxel_mask, brick_live):
    gain = jnp.pad(bn_gain, (0, 128 - C))[None]
    shift = jnp.pad(bn_shift, (0, 128 - C))[None]
    packed, mask, *sides = pack_features(brick_live, features, voxel_mask)
    weight_rows, weight_back = arrange(weight)
    halo, (weight_rows, weight_back) = exchange(sides, (weight_rows, weight_back))
    pre, stats = forward(brick_live, packed, halo, weight_rows, mask)
    cotangent, stats = lax.optimization_barrier((cotangent, stats))
    stats = gather_small(stats)
    cot = pack_plain(brick_live, cotangent)
    gz, stats2 = slope(stats, pre, cot, mask, gain, shift)
    stats2 = gather_small(stats2)
    grad, small, *grad_sides = pre_grad(brick_live, stats, stats2, pre, gz, mask, gain)
    terms = weight_terms(brick_live, packed, halo, grad)
    grad_halo, terms = exchange(grad_sides, terms)
    parts = scatter_large(terms)
    parts, grad_halo = lax.optimization_barrier((parts, grad_halo))
    sums = gather_large(parts)
    input_grad = backward(brick_live, grad, grad_halo, weight_back, mask)
    weight_grad = finish(sums, small)
    return input_grad, weight_grad, small[0, :C], small[1, :C]


def solution(mesh):
    return jax.shard_map(
        body,
        mesh=mesh,
        in_specs=(
            P("gx", "gy", None, None),
            P("gx", "gy", None, None),
            P(),
            P(),
            P(),
            P("gx", "gy", None),
            P("gx", "gy", None),
        ),
        out_specs=(P("gx", "gy", None, None), P(), P(), P()),
        check_vma=False,
    )
```

time: 1620 us -> 172 us (0.11)
  the two profiles are of different devices: /device:TPU:15 before, /device:TPU:7 now
where the time goes in v2:
time: 172 us; the launch traced here: 169 us
  Pallas kernels  77 us (45%)
  starting transfers between devices  41.2 us (24%)
  waiting for transfers between devices  23.8 us (14%)
  blocking collectives  18.3 us (11%)
  local copies, waits for them, and re-layouts  8.18 us (5%)
    all_to_all x1, blocking collectives, gather_small(): return lax.all_to_all(spread, AXES, 0, 0, tiled=True)  18.3 us
    ppermute x8, starting transfers between devices, swap(): return lax.ppermute(values, axis, pairs)  16 us
    pallas_call x1, Pallas kernels, backward(): pl.pallas_call(backward_kernel, grid=(STEPS,), in_specs=[smem(), plane_bl...  15.4 us
    ppermute x8, waiting for transfers between devices, swap(): return lax.ppermute(values, axis, pairs)  14.8 us
    pallas_call x1, Pallas kernels, forward(): pl.pallas_call(forward_kernel, grid=(STEPS,), in_specs=[smem(), plane_blo...  13.4 us
    pallas_call x1, Pallas kernels, weight_terms(): pl.pallas_call(weight_kernel, grid=(STEPS,), in_specs=[smem(), plane_bloc...  13.2 us
    all_to_all x1, starting transfers between devices, gather_small(): return lax.all_to_all(spread, AXES, 0, 0, tiled=True)  11.9 us
    all_to_all x1, starting transfers between devices, gather_large(): return lax.all_to_all(spread, AXES, 0, 0, tiled=True).reshape(-1, 128)  7.37 us
  transfers between devices with their start and end apart: 11, of which 7 were waited for; matrix products, arithmetic and copies ran while one was open for 1% of the time, Pallas kernels for 23%

profile of v2, /device:TPU:7, one launch (start us, length us, event | category | flops | bytes accessed | tf_op | source)
XLA Modules:
  0.0 169.3 jit_solution(5941170911707125301)
XLA Ops:
  0.6 7.1 %pack_features.1 = (bf16[1536,512]{1,0:T(8,128)(2,1)}, f32[16,1,512]{2,1,0:T(1,128)}, bf16[112,512]{1,0:T(8,128)(2,1)}, bf16[112,512]{1,0:T(8,128)(2,1)}, bf16[1...) custom-call(s32[1,1,8]{2,1,0:T(1,128)} %live_ref.11, bf16[16,16,96,128]{3,2,1,0:T(8,128)(2,1)} %feat_ref.1, ...), custom_call_target="tpu_custom_call" | custom-call | tf_op jit(solution)/shard_map/pack_features/pallas_call | solution.py:158
  7.8 0.8 collective-permute-start
  8.6 3.1 %collective-permute-start.1 = (bf16[112,512]{1,0:T(8,128)(2,1)}, bf16[112,512]{1,0:T(8,128)(2,1)S(1)}, u32[]{:S(2)}, u32[]{:S(2)}) collective-permute-start(bf16[112,512]{1,0:T(8,128)(2,1)} %get-tuple-element.42), channel_id=1, source_target_pairs={{16,32},{32,16},{48,64},{64,48},{80,96},{96,80},{17,33},{33,17},{4... | collective-permute-start | bytes 344072 | tf_op jit(solution)/shard_map/ppermute | solution.py:255
  11.7 2.7 %arrange.1 = (bf16[288,864]{1,0:T(8,128)(2,1)}, bf16[288,864]{1,0:T(8,128)(2,1)}) custom-call(bf16[27,96,96]{2,1,0:T(8,128)(2,1)} %weight_ref.1), custom_call_target="tpu_custom_call" | custom-call | tf_op jit(solution)/shard_map/arrange/pallas_call | solution.py:741
  15.5 1.9 %relay.2 = (bf16[112,640]{1,0:T(8,128)(2,1)}, bf16[112,640]{1,0:T(8,128)(2,1)}) custom-call(bf16[112,512]{1,0:T(8,128)(2,1)} %copy-done.2, bf16[112,512]{1,0:T(8,128)(2,1)} %copy-done.3, bf16[112,512]{1,0:T(8,128)(2,1)} %get-tuple-element.47.ya, bf16[112,512]{1,0:T(8,128)(2,1)} %get-tuple-element.48.yb), custom_call_target="tpu_custom_call" | custom-call | tf_op jit(solution)/shard_map/relay/pallas_call | solution.py:238
  18.0 4.1 %collective-permute-start.3 = (bf16[112,640]{1,0:T(8,128)(2,1)}, bf16[112,640]{1,0:T(8,128)(2,1)S(1)}, u32[]{:S(2)}, u32[]{:S(2)}) collective-permute-start(bf16[112,640]{1,0:T(8,128)(2,1)} %get-tuple-element.50), channel_id=1, source_target_pairs={{1,2},{2,1},{3,4},{4,3},{5,6},{6,5},{7,8},{8,7},{9,10},{10,9},{11,... | collective-permute-start | bytes 430088 | tf_op jit(solution)/shard_map/ppermute | solution.py:255
  22.1 4.0 %collective-permute-done.3.refs_3_ = bf16[112,640]{1,0:T(8,128)(2,1)S(1)} collective-permute-done((bf16[112,640]{1,0:T(8,128)(2,1)}, bf16[112,640]{1,0:T(8,128)(2,1)S(1)}, u32[]{:S(2)}, u32[]{:S(2)}) %collective-permute-start.3) | collective-permute-done | bytes 143392 | tf_op jit(solution)/shard_map/ppermute | solution.py:255
  26.8 13.4 %forward.1 = (f32[1536,512]{1,0:T(8,128)}, f32[8,128]{1,0:T(8,128)}) custom-call(s32[1,1,8]{2,1,0:T(1,128)} %live_ref.11, bf16[1536,512]{1,0:T(8,128)(2,1)} %get-tuple-element.40.body_ref, bf16[112,512]{1,0:T(8,128)(2,1)} %copy-done.2, bf16[112,512]{1,0:T(8,128)(2,1)} %copy-done.3, bf16[112,640]{1,0:T(8,128)(2,1)} %copy-done.4, bf16[112,640]{1,0:T(8,128)(2,1)} %copy-done.5, ...), custom_call_target="tpu_custom_call" | custom-call | tf_op jit(solution)/shard_map/forward/pallas_call | solution.py:468
  40.2 1.5 broadcast_in_dim.10
  41.7 11.9 %all-to-all-start = ((f32[128,8,128]{2,1,0:T(8,128)}), f32[128,8,128]{2,1,0:T(8,128)S(1)}, u32[]{:S(2)}, u32[]{:S(2)}) async-start(f32[128,8,128]{2,1,0:T(8,128)} %broadcast_in_dim.10), calls=%async_computation | async-start | bytes 1048576 | tf_op jit(solution)/shard_map/all_to_all | solution.py:754
  54.2 5.8 %pack_cotangent.1.cot_ref = bf16[1536,512]{1,0:T(8,128)(2,1)} custom-call(s32[1,1,8]{2,1,0:T(1,128)} %live_ref.11, bf16[16,16,96,128]{3,2,1,0:T(8,128)(2,1)} %feat_ref.2), custom_call_target="tpu_custom_call" | custom-call | tf_op jit(solution)/shard_map/pack_cotangent/pallas_call | solution.py:200
  60.0 5.9 %all-to-all-done.stat_ref = f32[128,8,128]{2,1,0:T(8,128)S(1)} async-done(((f32[128,8,128]{2,1,0:T(8,128)}), f32[128,8,128]{2,1,0:T(8,128)S(1)}, u32[]{:S(2)}, u32[]{:S(2)}) %all-to-all-start) | async-done | bytes 524320 | tf_op jit(solution)/shard_map/all_to_all | solution.py:754
  65.9 0.8 copy-done
  66.7 6.1 %slope.1 = (f32[1536,512]{1,0:T(8,128)}, f32[8,128]{1,0:T(8,128)}) custom-call(f32[128,8,128]{2,1,0:T(8,128)} %copy-done, f32[1536,512]{1,0:T(8,128)} %get-tuple-element.55.pre_ref, bf16[1536,512]{1,0:T(8,128)(2,1)} %pack_cotangent.1.cot_ref, f32[16,1,512]{2,1,0:T(1,128)} %get-tuple-element.52.refs_5_.mask_ref, f32[1,128]{1,0:T(1,128)} %get-tuple-element.79.gain_ref, ...), custom_call_target="tpu_custom_call" | custom-call | tf_op jit(solution)/shard_map/slope/pallas_call | solution.py:534
  73.5 18.3 %all_to_all.20.stat2_ref = f32[128,8,128]{2,1,0:T(8,128)} all-to-all(f32[128,8,128]{2,1,0:T(8,128)S(1)} %broadcast_in_dim.13), channel_id=1, replica_groups=mesh['gx'=8,'gy'=16] {'gx','gy'}, dimensions={0} | all-to-all | bytes 1048576 | tf_op jit(solution)/shard_map/all_to_all | solution.py:754
  91.8 6.4 %pre_grad.1 = (bf16[1536,512]{1,0:T(8,128)(2,1)}, f32[8,128]{1,0:T(8,128)}, bf16[112,512]{1,0:T(8,128)(2,1)}, bf16[112,512]{1,0:T(8,128)(2,1)}, bf16[112,512]{1,0:T(8,128)(2,1)}, /*index=5*/bf16[112,512]{1,0:T(8,128)(2,1)}) custom-call(s32[1,1,8]{2,1,0:T(1,128)} %live_ref.11, f32[128,8,128]{2,1,0:T(8,128)} %copy-done, f32[128,8,128]{2,1,0:T(8,128)} %all_to_all.20.stat2_ref, ...), custom_call_target="tpu_custom_call" | custom-call | tf_op jit(solution)/shard_map/pre_grad/pallas_call | solution.py:592
  98.2 0.8 collective-permute-start.4
  98.9 2.3 %collective-permute-start.5 = (bf16[112,512]{1,0:T(8,128)(2,1)}, bf16[112,512]{1,0:T(8,128)(2,1)S(1)}, u32[]{:S(2)}, u32[]{:S(2)}) collective-permute-start(bf16[112,512]{1,0:T(8,128)(2,1)} %get-tuple-element.61), channel_id=1, source_target_pairs={{16,32},{32,16},{48,64},{64,48},{80,96},{96,80},{17,33},{33,17},{4... | collective-permute-start | bytes 344072 | tf_op jit(solution)/shard_map/ppermute | solution.py:255
  101.3 13.2 %weight_terms.1 = f32[2048,128]{1,0:T(8,128)} custom-call(s32[1,1,8]{2,1,0:T(1,128)} %live_ref.11, bf16[1536,512]{1,0:T(8,128)(2,1)} %get-tuple-element.40.body_ref, bf16[112,512]{1,0:T(8,128)(2,1)} %copy-done.2, bf16[112,512]{1,0:T(8,128)(2,1)} %copy-done.3, bf16[112,640]{1,0:T(8,128)(2,1)} %copy-done.4, bf16[112,640]{1,0:T(8,128)(2,1)} %copy-done.5, ...), custom_call_target="tpu_custom_call" | custom-call | tf_op jit(solution)/shard_map/weight_terms/pallas_call | solution.py:645
  114.5 5.8 %all-to-all-start.2 = ((f32[128,16,128]{2,1,0:T(8,128)}), f32[128,16,128]{2,1,0:T(8,128)S(1)}, u32[]{:S(2)}, u32[]{:S(2)}) async-start(f32[128,16,128]{2,1,0:T(8,128)} %bitcast.10), calls=%async_computation.2 | async-start | bytes 2097152 | tf_op jit(solution)/shard_map/all_to_all | solution.py:760
  120.4 1.9 %relay.3 = (bf16[112,640]{1,0:T(8,128)(2,1)}, bf16[112,640]{1,0:T(8,128)(2,1)}) custom-call(bf16[112,512]{1,0:T(8,128)(2,1)} %copy-done.6, bf16[112,512]{1,0:T(8,128)(2,1)} %copy-done.7, bf16[112,512]{1,0:T(8,128)(2,1)} %get-tuple-element.65.ya, bf16[112,512]{1,0:T(8,128)(2,1)} %get-tuple-element.66.yb), custom_call_target="tpu_custom_call" | custom-call | tf_op jit(solution)/shard_map/relay/pallas_call | solution.py:238
  122.8 3.8 %collective-permute-start.7 = (bf16[112,640]{1,0:T(8,128)(2,1)}, bf16[112,640]{1,0:T(8,128)(2,1)S(1)}, u32[]{:S(2)}, u32[]{:S(2)}) collective-permute-start(bf16[112,640]{1,0:T(8,128)(2,1)} %get-tuple-element.68), channel_id=1, source_target_pairs={{1,2},{2,1},{3,4},{4,3},{5,6},{6,5},{7,8},{8,7},{9,10},{10,9},{11,... | collective-permute-start | bytes 430088 | tf_op jit(solution)/shard_map/ppermute | solution.py:255
  126.6 8.7 %collective-permute-done.6.refs_2_ = bf16[112,640]{1,0:T(8,128)(2,1)S(1)} collective-permute-done((bf16[112,640]{1,0:T(8,128)(2,1)}, bf16[112,640]{1,0:T(8,128)(2,1)S(1)}, u32[]{:S(2)}, u32[]{:S(2)}) %collective-permute-start.6) | collective-permute-done | bytes 143392 | tf_op jit(solution)/shard_map/ppermute | solution.py:255
  135.3 1.7 collective-permute-done.7.refs_3_
  137.0 1.6 all-to-all-done.2
  138.8 1.0 broadcast_in_dim.28
  139.8 7.4 %all-to-all-start.3 = ((f32[128,16,128]{2,1,0:T(8,128)}), f32[128,16,128]{2,1,0:T(8,128)S(1)}, u32[]{:S(2)}, u32[]{:S(2)}) async-start(f32[128,16,128]{2,1,0:T(8,128)} %broadcast_in_dim.28), calls=%async_computation.3 | async-start | bytes 2097152 | tf_op jit(solution)/shard_map/all_to_all | solution.py:766
  147.2 1.3 slice_bitcast_fusion
  148.5 15.4 %backward.1 = bf16[16,16,96,128]{3,2,1,0:T(8,128)(2,1)} custom-call(s32[1,1,8]{2,1,0:T(1,128)} %live_ref.11, bf16[1536,512]{1,0:T(8,128)(2,1)} %get-tuple-element.59.refs_4_.body_ref, bf16[112,512]{1,0:T(8,128)(2,1)} %copy-done.6, bf16[112,512]{1,0:T(8,128)(2,1)} %copy-done.7, bf16[112,640]{1,0:T(8,128)(2,1)} %copy-done.8, bf16[112,640]{1,0:T(8,128)(2,1)} %copy-done.9, ...), custom_call_target="tpu_custom_call" | custom-call | tf_op jit(solution)/shard_map/backward/pallas_call | solution.py:691
  163.9 1.4 all-to-all-done.3
  165.3 1.0 copy-done.1
  166.2 3.1 %finish.1 = f32[27,96,96]{2,1,0:T(8,128)} custom-call(f32[2048,128]{1,0:T(8,128)} %bitcast.11, f32[8,128]{1,0:T(8,128)} %get-tuple-element.75.small_ref), custom_call_target="tpu_custom_call" | custom-call | tf_op jit(solution)/shard_map/finish/pallas_call | solution.py:722
  (32 shorter events, 4.3 us)
Async XLA Ops:
  7.8 45.8 %copy-start.10 = (f32[96]{0:T(128)S(1)}, f32[96]{0:T(128)}, u32[]{:S(2)}) copy-start(f32[96]{0:T(128)} %param.11) | copy-start | bytes 1156
  7.8 45.8 %copy-start.11 = (f32[96]{0:T(128)S(1)}, f32[96]{0:T(128)}, u32[]{:S(2)}) copy-start(f32[96]{0:T(128)} %param.10) | copy-start | bytes 1156
  7.8 6.6 %collective-permute-start = (bf16[112,512]{1,0:T(8,128)(2,1)}, bf16[112,512]{1,0:T(8,128)(2,1)S(1)}, u32[]{:S(2)}, u32[]{:S(2)}) collective-permute-start(bf16[112,512]{1,0:T(8,128)(2,1)} %get-tuple-element.41), channel_id=1, source_target_pairs={{0,16},{16,0},{32,48},{48,32},{64,80},{80,64},{96,112},{112,96},{1... | collective-permute-start | bytes 344072 | tf_op jit(solution)/shard_map/ppermute | solution.py:255
  8.6 6.3 %collective-permute-start.1 = (bf16[112,512]{1,0:T(8,128)(2,1)}, bf16[112,512]{1,0:T(8,128)(2,1)S(1)}, u32[]{:S(2)}, u32[]{:S(2)}) collective-permute-start(bf16[112,512]{1,0:T(8,128)(2,1)} %get-tuple-element.42), channel_id=1, source_target_pairs={{16,32},{32,16},{48,64},{64,48},{80,96},{96,80},{17,33},{33,17},{4... | collective-permute-start | bytes 344072 | tf_op jit(solution)/shard_map/ppermute | solution.py:255
  14.4 0.6 copy-start.2
  14.9 0.7 copy-start.3
  17.4 4.7 %collective-permute-start.2 = (bf16[112,640]{1,0:T(8,128)(2,1)}, bf16[112,640]{1,0:T(8,128)(2,1)S(1)}, u32[]{:S(2)}, u32[]{:S(2)}) collective-permute-start(bf16[112,640]{1,0:T(8,128)(2,1)} %get-tuple-element.49), channel_id=1, source_target_pairs={{0,1},{1,0},{2,3},{3,2},{4,5},{5,4},{6,7},{7,6},{8,9},{9,8},{10,11... | collective-permute-start | bytes 430088 | tf_op jit(solution)/shard_map/ppermute | solution.py:255
  18.0 8.2 %collective-permute-start.3 = (bf16[112,640]{1,0:T(8,128)(2,1)}, bf16[112,640]{1,0:T(8,128)(2,1)S(1)}, u32[]{:S(2)}, u32[]{:S(2)}) collective-permute-start(bf16[112,640]{1,0:T(8,128)(2,1)} %get-tuple-element.50), channel_id=1, source_target_pairs={{1,2},{2,1},{3,4},{4,3},{5,6},{6,5},{7,8},{8,7},{9,10},{10,9},{11,... | collective-permute-start | bytes 430088 | tf_op jit(solution)/shard_map/ppermute | solution.py:255
  22.1 4.0 %copy-start.4 = (bf16[112,640]{1,0:T(8,128)(2,1)}, bf16[112,640]{1,0:T(8,128)(2,1)S(1)}, u32[]{:S(2)}) copy-start(bf16[112,640]{1,0:T(8,128)(2,1)S(1)} %collective-permute-done.2.refs_2_) | copy-start | bytes 430084
  26.1 0.7 copy-start.5
  41.7 24.2 %all-to-all-start = ((f32[128,8,128]{2,1,0:T(8,128)}), f32[128,8,128]{2,1,0:T(8,128)S(1)}, u32[]{:S(2)}, u32[]{:S(2)}) async-start(f32[128,8,128]{2,1,0:T(8,128)} %broadcast_in_dim.10), calls=%async_computation | async-start | bytes 1048576 | tf_op jit(solution)/shard_map/all_to_all | solution.py:754
  65.9 0.8 copy-start
  98.2 16.3 %collective-permute-start.4 = (bf16[112,512]{1,0:T(8,128)(2,1)}, bf16[112,512]{1,0:T(8,128)(2,1)S(1)}, u32[]{:S(2)}, u32[]{:S(2)}) collective-permute-start(bf16[112,512]{1,0:T(8,128)(2,1)} %get-tuple-element.60), channel_id=1, source_target_pairs={{0,16},{16,0},{32,48},{48,32},{64,80},{80,64},{96,112},{112,96},{1... | collective-permute-start | bytes 344072 | tf_op jit(solution)/shard_map/ppermute | solution.py:255
  98.9 15.5 %collective-permute-start.5 = (bf16[112,512]{1,0:T(8,128)(2,1)}, bf16[112,512]{1,0:T(8,128)(2,1)S(1)}, u32[]{:S(2)}, u32[]{:S(2)}) collective-permute-start(bf16[112,512]{1,0:T(8,128)(2,1)} %get-tuple-element.61), channel_id=1, source_target_pairs={{16,32},{32,16},{48,64},{64,48},{80,96},{96,80},{17,33},{33,17},{4... | collective-permute-start | bytes 344072 | tf_op jit(solution)/shard_map/ppermute | solution.py:255
  114.5 5.9 %copy-start.6 = (bf16[112,512]{1,0:T(8,128)(2,1)}, bf16[112,512]{1,0:T(8,128)(2,1)S(1)}, u32[]{:S(2)}) copy-start(bf16[112,512]{1,0:T(8,128)(2,1)S(1)} %collective-permute-done.4.xa.refs_0_) | copy-start | bytes 344068
  114.5 5.9 %copy-start.7 = (bf16[112,512]{1,0:T(8,128)(2,1)}, bf16[112,512]{1,0:T(8,128)(2,1)S(1)}, u32[]{:S(2)}) copy-start(bf16[112,512]{1,0:T(8,128)(2,1)S(1)} %collective-permute-done.5.xb.refs_1_) | copy-start | bytes 344068
  114.5 24.2 %all-to-all-start.2 = ((f32[128,16,128]{2,1,0:T(8,128)}), f32[128,16,128]{2,1,0:T(8,128)S(1)}, u32[]{:S(2)}, u32[]{:S(2)}) async-start(f32[128,16,128]{2,1,0:T(8,128)} %bitcast.10), calls=%async_computation.2 | async-start | bytes 2097152 | tf_op jit(solution)/shard_map/all_to_all | solution.py:760
  122.2 13.1 %collective-permute-start.6 = (bf16[112,640]{1,0:T(8,128)(2,1)}, bf16[112,640]{1,0:T(8,128)(2,1)S(1)}, u32[]{:S(2)}, u32[]{:S(2)}) collective-permute-start(bf16[112,640]{1,0:T(8,128)(2,1)} %get-tuple-element.67), channel_id=1, source_target_pairs={{0,1},{1,0},{2,3},{3,2},{4,5},{5,4},{6,7},{7,6},{8,9},{9,8},{10,11... | collective-permute-start | bytes 430088 | tf_op jit(solution)/shard_map/ppermute | solution.py:255
  122.8 14.2 %collective-permute-start.7 = (bf16[112,640]{1,0:T(8,128)(2,1)}, bf16[112,640]{1,0:T(8,128)(2,1)S(1)}, u32[]{:S(2)}, u32[]{:S(2)}) collective-permute-start(bf16[112,640]{1,0:T(8,128)(2,1)} %get-tuple-element.68), channel_id=1, source_target_pairs={{1,2},{2,1},{3,4},{4,3},{5,6},{6,5},{7,8},{8,7},{9,10},{10,9},{11,... | collective-permute-start | bytes 430088 | tf_op jit(solution)/shard_map/ppermute | solution.py:255
  135.3 13.1 %copy-start.8 = (bf16[112,640]{1,0:T(8,128)(2,1)}, bf16[112,640]{1,0:T(8,128)(2,1)S(1)}, u32[]{:S(2)}) copy-start(bf16[112,640]{1,0:T(8,128)(2,1)S(1)} %collective-permute-done.6.refs_2_) | copy-start | bytes 430084
  137.0 11.5 %copy-start.9 = (bf16[112,640]{1,0:T(8,128)(2,1)}, bf16[112,640]{1,0:T(8,128)(2,1)S(1)}, u32[]{:S(2)}) copy-start(bf16[112,640]{1,0:T(8,128)(2,1)S(1)} %collective-permute-done.7.refs_3_) | copy-start | bytes 430084
  139.8 25.4 %all-to-all-start.3 = ((f32[128,16,128]{2,1,0:T(8,128)}), f32[128,16,128]{2,1,0:T(8,128)S(1)}, u32[]{:S(2)}, u32[]{:S(2)}) async-start(f32[128,16,128]{2,1,0:T(8,128)} %broadcast_in_dim.28), calls=%async_computation.3 | async-start | bytes 2097152 | tf_op jit(solution)/shard_map/all_to_all | solution.py:766
  165.3 1.0 copy-start.1

commit v3 on v2

--- a/solution.py
+++ b/solution.py
@@ -106,7 +106,7 @@
 SIDES = [jax.ShapeDtypeStruct((EDGE, W2), BF16)] * 4
 
 
-PACE = 4
+PACE = 8
 
 
 def paced():
@@ -371,40 +371,45 @@
     pltpu.VMEM((2, 3, C, 640), BF16),
     pltpu.VMEM((2, 9 * C, W2), BF16),
 ]
-STEPS = B // 2 + 1
 
 
 def run_planes(live_ref, body_ref, halo, edge_ref, rows_ref, cols_ref, use):
     t = pl.program_id(0)
-    ids = slots(live_ref)
-    columns = Columns(ids, halo, edge_ref, rows_ref)
-    even, odd = cols_ref.at[0], cols_ref.at[1]
+    columns = Columns(slots(live_ref), halo, edge_ref, rows_ref)
+    bufs = [cols_ref.at[k] for k in range(2)]
+
+    def build(i, buf):
+        if isinstance(i, int) and i in (0, 17):
+            columns.edge(i // 17, buf)
+        else:
+            rows = (i - 1) * C
+            if not isinstance(i, int):
+                rows = pl.multiple_of(rows, C)
+            columns.inner(i - 1, body_ref[pl.ds(rows, C), :], buf)
+
+    def pass_over(base, count):
+        for j in range(count):
+            if not isinstance(base, int) or base + j < 17:
+                build(base + j + 1, bufs[(j + 1) % 2])
+            use(base + j, bufs[j % 2])
 
     @pl.when(t == 0)
     def _():
         columns.prepare()
-        columns.edge(0, even)
-
-    @pl.when(t < STEPS - 1)
-    def _():
-        columns.inner(2 * t, body_ref[0:C, :], odd)
-        use(2 * t, even)
-        columns.inner(2 * t + 1, body_ref[C : 2 * C, :], even)
-        use(2 * t + 1, odd)
-
-    @pl.when(t == STEPS - 1)
-    def _():
-        columns.edge(1, odd)
-        use(2 * t, even)
-        use(2 * t + 1, odd)
-
-
-def plane_block():
-    return pl.BlockSpec((2 * C, W2), lambda t: (jnp.minimum(t, B // 2 - 1), 0))
-
-
-def late_block():
-    return pl.BlockSpec((2 * C, W2), lambda t: (jnp.maximum(t - 1, 0), 0))
+        build(0, bufs[0])
+        pass_over(0, 6)
+
+    @pl.when((t > 0) & (t < 3))
+    def _():
+        pass_over(2 + 4 * t, 4)
+
+    @pl.when(t == 3)
+    def _():
+        pass_over(14, 4)
+
+
+def four_planes():
+    return pl.BlockSpec((4 * C, W2), lambda t: (t, 0))
 
 
 def fold(values):
@@ -425,8 +430,9 @@
 def add_product(weight_ref, sums):
     def use(i, cols):
         part = jnp.dot(weight_ref[...], cols[...], preferred_element_type=F32)
-        rows = pl.ds(pl.multiple_of(i * C, C), 3 * C)
-        sums[rows, :] += part
+        rows = i * C if isinstance(i, int) else pl.multiple_of(i * C, C)
+        sums[pl.ds(rows, 2 * C), :] += part[0 : 2 * C]
+        sums[pl.ds(rows + 2 * C, C), :] = part[2 * C : 3 * C]
 
     return use
 
@@ -438,43 +444,44 @@
 
     @pl.when(t == 0)
     def _():
-        sums[...] = jnp.zeros_like(sums)
         acc[...] = jnp.zeros_like(acc)
 
     run_planes(
         live_ref, body_ref, halo, edge_ref, rows_ref, cols_ref, add_product(weight_ref, sums)
     )
-
-    @pl.when(t > 0)
-    def _():
-        for u in range(2):
-            values = sums[pl.ds(pl.multiple_of((2 * t + u) * C, C), C), :]
-            mask = mask_ref[2 * t - 2 + u]
-            held = values * mask
-            pre_ref[u * C : (u + 1) * C, :] = values
-            acc[0] += fold(held)
-            acc[1] += fold(held * values)
-            acc[2, 0:1, :] += fold(mask)
-
-    @pl.when(t == STEPS - 1)
-    def _():
-        stat_ref[...] = jnp.zeros_like(stat_ref)
-        stat_ref[0:1, :] = to_row(acc[0])
-        stat_ref[1:2, :] = to_row(acc[1])
-        stat_ref[2:3, :] = jnp.full((1, 128), 1.0, F32) * jnp.sum(acc[2, 0:1, :])
+    for u in range(4):
+        values = sums[pl.ds(pl.multiple_of((4 * t + 2 + u) * C, C), C), :]
+        mask = mask_ref[4 * t + u]
+        held = values * mask
+        pre_ref[u * C : (u + 1) * C, :] = values
+        acc[0] += fold(held)
+        acc[1] += fold(held * values)
+        acc[2, 0:1, :] += fold(mask)
+
+    @pl.when(t == 3)
+    def _():
+        lane = iota((1, 128), 1)
+        total = jnp.where(lane == C, jnp.sum(acc[2, 0:1, :]), to_row(acc[0]))
+        rows = jnp.concatenate([total, to_row(acc[1])], axis=0)
+        stat_ref[...] = jnp.broadcast_to(rows[None], stat_ref.shape)
+
+
+def devices():
+    return lax.axis_size("gx") * lax.axis_size("gy")
 
 
 def forward(live, body, halo, weight, mask):
+    spread = (devices(), 2, 128)
     return pl.pallas_call(
         forward_kernel,
-        grid=(STEPS,),
-        in_specs=[smem(), plane_block()]
+        grid=(4,),
+        in_specs=[smem(), whole(body.shape)]
         + [whole(h) for h in HALO]
         + [whole(weight.shape), whole(mask.shape)],
-        out_specs=[late_block(), whole((8, 128))],
+        out_specs=[four_planes(), whole(spread)],
         out_shape=[
             jax.ShapeDtypeStruct((B * C, W2), F32),
-            jax.ShapeDtypeStruct((8, 128), F32),
+            jax.ShapeDtypeStruct(spread, F32),
         ],
         scratch_shapes=ASSEMBLY + [pltpu.VMEM((ROWS, W2), F32), pltpu.VMEM((3, C, 128), F32)],
         compiler_params=params(),
@@ -484,14 +491,27 @@
 
 def moments(stat_ref):
     total = jnp.sum(stat_ref[...], axis=0)
-    voxels = total[2:3, :]
+    lane = iota((1, 128), 1)
+    voxels = jnp.sum(jnp.where(lane == C, total[0:1, :], 0.0), axis=1, keepdims=True)
+    voxels = jnp.broadcast_to(voxels, (1, 128))
     mean = total[0:1, :] / voxels
     var = total[1:2, :] / voxels - mean * mean
     return voxels, mean, lax.rsqrt(var + 1e-05)
 
 
+def slope_tile(refs, u, k, terms):
+    pre_ref, cot_ref, mask_ref = refs
+    mean, inv, gain, shift = terms
+    rows, lanes = slice(u * C, (u + 1) * C), slice(k * 128, (k + 1) * 128)
+    normed = (pre_ref[rows, lanes] - mean) * inv
+    zed = gain * normed + shift
+    sig = 0.5 + 0.5 * jnp.tanh(0.5 * zed)
+    held = mask_ref[u][:, lanes] * cot_ref[rows, lanes].astype(F32)
+    return normed, held * (sig * (1.0 + zed * (1.0 - sig)))
+
+
 def slope_kernel(
-    stat_ref, pre_ref, cot_ref, mask_ref, gain_ref, shift_ref, gz_ref, out_ref, col_ref, acc
+    stat_ref, pre_ref, cot_ref, mask_ref, gain_ref, shift_ref, out_ref, col_ref, acc
 ):
     t = pl.program_id(0)
 
@@ -502,22 +522,12 @@
             col_ref[k] = jnp.broadcast_to(to_column(row), (C, 128))
         acc[...] = jnp.zeros_like(acc)
 
-    mean, inv, gain, shift = [col_ref[k] for k in range(4)]
+    terms = [col_ref[k] for k in range(4)]
     total = acc[0]
     cross = acc[1]
     for u in range(PACE):
-        rows = slice(u * C, (u + 1) * C)
         for k in range(4):
-            lanes = slice(k * 128, (k + 1) * 128)
-            normed = (pre_ref[rows, lanes] - mean) * inv
-            zed = gain * normed + shift
-            sig = 0.5 + 0.5 * jnp.tanh(0.5 * zed)
-            gz = (
-                mask_ref[u][:, lanes]
-                * cot_ref[rows, lanes].astype(F32)
-                * (sig * (1.0 + zed * (1.0 - sig)))
-            )
-            gz_ref[rows, lanes] = gz
+            normed, gz = slope_tile((pre_ref, cot_ref, mask_ref), u, k, terms)
             total += gz
             cross += gz * normed
     acc[0] = total
@@ -525,9 +535,8 @@
 
     @pl.when(t == B // PACE - 1)
     def _():
-        out_ref[...] = jnp.zeros_like(out_ref)
-        out_ref[0:1, :] = to_row(acc[0])
-        out_ref[1:2, :] = to_row(acc[1])
+        rows = jnp.concatenate([to_row(acc[0]), to_row(acc[1])], axis=0)
+        out_ref[...] = jnp.broadcast_to(rows[None], out_ref.shape)
 
 
 def slope(stats, pre, cot, mask, gain, shift):
@@ -542,21 +551,17 @@
             whole((1, 128)),
             whole((1, 128)),
         ],
-        out_specs=[paced(), whole((8, 128))],
-        out_shape=[
-            jax.ShapeDtypeStruct((B * C, W2), F32),
-            jax.ShapeDtypeStruct((8, 128), F32),
-        ],
+        out_specs=whole(stats.shape),
+        out_shape=jax.ShapeDtypeStruct(stats.shape, F32),
         scratch_shapes=[pltpu.VMEM((4, C, 128), F32), pltpu.VMEM((2, C, 128), F32)],
         compiler_params=params(),
         name="slope",
     )(stats, pre, cot, mask, gain, shift)
 
 
-def pre_grad_kernel(
-    live_ref, stat_ref, stat2_ref, pre_ref, gz_ref, mask_ref, gain_ref, out_ref, small_ref, *refs
-):
-    sides, (col_ref,) = refs[:4], refs[4:]
+def pre_grad_kernel(live_ref, stat_ref, stat2_ref, pre_ref, cot_ref, mask_ref, *refs):
+    gain_ref, shift_ref, out_ref, small_ref = refs[:4]
+    sides, (col_ref,) = refs[4:8], refs[8:]
     t = pl.program_id(0)
     ids = slots(live_ref)
 
@@ -569,26 +574,27 @@
         small_ref[0:1, :] = total[1:2, :] * root
         small_ref[1:2, :] = total[0:1, :] * root
         small_ref[2:3, :] = root
-        rows = (mean, inv, gain_ref[...] * inv, total[0:1, :] / voxels, total[1:2, :] / voxels)
+        gain = gain_ref[...]
+        rows = (mean, inv, gain, shift_ref[...], gain * inv)
+        rows = rows + (total[0:1, :] / voxels, total[1:2, :] / voxels)
         for k, row in enumerate(rows):
             col_ref[k] = jnp.broadcast_to(to_column(row), (C, 128))
 
-    mean, inv, scale, first, second = [col_ref[k] for k in range(5)]
+    terms = [col_ref[k] for k in range(4)]
+    scale, first, second = [col_ref[k] for k in range(4, 7)]
     for u in range(PACE):
         rows = slice(u * C, (u + 1) * C)
         tiles = []
         for k in range(4):
             lanes = slice(k * 128, (k + 1) * 128)
-            normed = (pre_ref[rows, lanes] - mean) * inv
-            tile = (
-                mask_ref[u][:, lanes] * scale * (gz_ref[rows, lanes] - first - normed * second)
-            ).astype(BF16)
+            normed, gz = slope_tile((pre_ref, cot_ref, mask_ref), u, k, terms)
+            tile = (mask_ref[u][:, lanes] * scale * (gz - first - normed * second)).astype(BF16)
             out_ref[rows, lanes] = tile
             tiles.append(tile)
         emit_sides(PACE * t + u, tiles, ids, sides)
 
 
-def pre_grad(live, stats, stats2, pre, gz, mask, gain):
+def pre_grad(live, stats, stats2, pre, cot, mask, gain, shift):
     return pl.pallas_call(
         pre_grad_kernel,
         grid=(B // PACE,),
@@ -600,6 +606,7 @@
             paced(),
             paced_mask(),
             whole((1, 128)),
+            whole((1, 128)),
         ],
         out_specs=[paced(), whole((8, 128))] + [whole(f.shape) for f in SIDES],
         out_shape=[
@@ -607,10 +614,10 @@
             jax.ShapeDtypeStruct((8, 128), F32),
         ]
         + SIDES,
-        scratch_shapes=[pltpu.VMEM((5, C, 128), F32)],
+        scratch_shapes=[pltpu.VMEM((7, C, 128), F32)],
         compiler_params=params(),
         name="pre_grad",
-    )(live, stats, stats2, pre, gz, mask, gain)
+    )(live, stats, stats2, pre, cot, mask, gain, shift)
 
 
 def weight_kernel(live_ref, body_ref, *refs):
@@ -626,14 +633,14 @@
         total[...] = jnp.zeros_like(total)
 
     def use(i, cols):
-        rows = pl.ds(pl.multiple_of(i * C, C), 3 * C)
+        rows = pl.ds(i * C if isinstance(i, int) else pl.multiple_of(i * C, C), 3 * C)
         total[...] += lax.dot_general(
             padded[rows, :], cols[...], (((1,), (1,)), ((), ())), preferred_element_type=F32
         )
 
     run_planes(live_ref, body_ref, halo, edge_ref, rows_ref, cols_ref, use)
 
-    @pl.when(t == STEPS - 1)
+    @pl.when(t == 3)
     def _():
         for j in range(6):
             out_ref[j * 288 : (j + 1) * 288, :] = total[:, j * 128 : (j + 1) * 128]
@@ -644,8 +651,8 @@
 def weight_terms(live, body, halo, grad):
     return pl.pallas_call(
         weight_kernel,
-        grid=(STEPS,),
-        in_specs=[smem(), plane_block()] + [whole(h) for h in HALO] + [whole(grad.shape)],
+        grid=(4,),
+        in_specs=[smem(), whole(body.shape)] + [whole(h) for h in HALO] + [whole(grad.shape)],
         out_specs=whole((2048, 128)),
         out_shape=jax.ShapeDtypeStruct((2048, 128), F32),
         scratch_shapes=ASSEMBLY
@@ -662,7 +669,6 @@
 
     @pl.when(t == 0)
     def _():
-        sums[...] = jnp.zeros_like(sums)
         ids = slots(live_ref)
         row, lane = iota((128, W2), 0), iota((128, W2), 1)
         start = jnp.where((row >> 6) == 0, ids[0], ids[1]) * B
@@ -673,28 +679,25 @@
     run_planes(
         live_ref, body_ref, halo, edge_ref, rows_ref, cols_ref, add_product(weight_ref, sums)
     )
-
-    @pl.when(t > 0)
-    def _():
-        for u in range(2):
-            rows = pl.ds(pl.multiple_of((2 * t + u) * C, C), C)
-            mask = mask_ref[2 * t - 2 + u]
-            for m in range(4):
-                lanes = slice(m * 128, (m + 1) * 128)
-                tile = (sums[rows, lanes] * mask[:, lanes]).astype(BF16)
-                moved = jnp.dot(tile, spread[...], preferred_element_type=F32)
-                for g in range(4):
-                    out_ref[u, 4 * g + m] = moved[:, g * 128 : (g + 1) * 128].astype(BF16)
+    for u in range(4):
+        rows = pl.ds(pl.multiple_of((4 * t + 2 + u) * C, C), C)
+        mask = mask_ref[4 * t + u]
+        for m in range(4):
+            lanes = slice(m * 128, (m + 1) * 128)
+            tile = (sums[rows, lanes] * mask[:, lanes]).astype(BF16)
+            moved = jnp.dot(tile, spread[...], preferred_element_type=F32)
+            for g in range(4):
+                out_ref[u, 4 * g + m] = moved[:, g * 128 : (g + 1) * 128].astype(BF16)
 
 
 def backward(live, body, halo, weight, mask):
     return pl.pallas_call(
         backward_kernel,
-        grid=(STEPS,),
-        in_specs=[smem(), plane_block()]
+        grid=(4,),
+        in_specs=[smem(), whole(body.shape)]
         + [whole(h) for h in HALO]
         + [whole(weight.shape), whole(mask.shape)],
-        out_specs=pl.BlockSpec((2, B, C, 128), lambda t: (jnp.maximum(t - 1, 0), 0, 0, 0)),
+        out_specs=pl.BlockSpec((4, B, C, 128), lambda t: (t, 0, 0, 0)),
         out_shape=jax.ShapeDtypeStruct((B, B, C, 128), BF16),
         scratch_shapes=ASSEMBLY + [pltpu.VMEM((ROWS, W2), F32), pltpu.VMEM((128, W2), BF16)],
         compiler_params=params(),
@@ -703,26 +706,27 @@
 
 
 def finish_kernel(sum_ref, small_ref, out_ref):
+    base = pl.multiple_of((2 - pl.program_id(0)) * C, C)
     root = small_ref[2:3, 0:C]
-    for a in range(3):
-        for k in range(9):
-            start = k * C
-            pieces = []
-            while start < (k + 1) * C:
-                j, off = start // 128, start % 128
-                stop = min((k + 1) * C, (j + 1) * 128)
-                row = j * 288 + (2 - a) * C
-                pieces.append(sum_ref[row : row + C, off : off + stop - start].astype(F32))
-                start = stop
-            block = pieces[0] if len(pieces) == 1 else jnp.concatenate(pieces, axis=1)
-            out_ref[9 * a + k] = block.T * root
+    for k in range(9):
+        start = k * C
+        pieces = []
+        while start < (k + 1) * C:
+            j, off = start // 128, start % 128
+            stop = min((k + 1) * C, (j + 1) * 128)
+            rows = pl.ds(base + j * 288, C)
+            pieces.append(sum_ref[rows, off : off + stop - start].astype(F32))
+            start = stop
+        block = pieces[0] if len(pieces) == 1 else jnp.concatenate(pieces, axis=1)
+        out_ref[k] = block.T * root
 
 
 def finish(sums, small):
     return pl.pallas_call(
         finish_kernel,
-        in_specs=[vmem()] * 2,
-        out_specs=vmem(),
+        grid=(3,),
+        in_specs=[whole(sums.shape), whole(small.shape)],
+        out_specs=pl.BlockSpec((9, C, C), lambda a: (a, 0, 0)),
         out_shape=jax.ShapeDtypeStruct((27, C, C), F32),
         compiler_params=params(),
         name="finish",
@@ -748,9 +752,7 @@
     )(weight)
 
 
-def gather_small(values):
-    count = lax.axis_size("gx") * lax.axis_size("gy")
-    spread = jnp.broadcast_to(values[None], (count,) + values.shape)
+def swap_all(spread):
     return lax.all_to_all(spread, AXES, 0, 0, tiled=True)
 
 
@@ -774,11 +776,13 @@
     halo, (weight_rows, weight_back) = exchange(sides, (weight_rows, weight_back))
     pre, stats = forward(brick_live, packed, halo, weight_rows, mask)
     cotangent, stats = lax.optimization_barrier((cotangent, stats))
-    stats = gather_small(stats)
+    stats = swap_all(stats)
     cot = pack_plain(brick_live, cotangent)
-    gz, stats2 = slope(stats, pre, cot, mask, gain, shift)
-    stats2 = gather_small(stats2)
-    grad, small, *grad_sides = pre_grad(brick_live, stats, stats2, pre, gz, mask, gain)
+    stats2 = slope(stats, pre, cot, mask, gain, shift)
+    stats2 = swap_all(stats2)
+    grad, small, *grad_sides = pre_grad(
+        brick_live, stats, stats2, pre, cot, mask, gain, shift
+    )
     terms = weight_terms(brick_live, packed, halo, grad)
     grad_halo, terms = exchange(grad_sides, terms)
     parts = scatter_large(terms)

time: 172 us -> 161 us (0.936)
  Pallas kernels: 77 us -> 72.9 us
  blocking collectives: 18.3 us -> 15.7 us
  waiting for transfers between devices: 23.8 us -> 21.3 us
  local copies, waits for them, and re-layouts: 8.18 us -> 5.8 us
    all_to_all x1, waiting for transfers between devices: 5.92 us -> 2.64 us  [swap_all(): return lax.all_to_all(spread, AXES, 0, 0, tiled=True)]
    all_to_all x1, blocking collectives: 18.3 us -> 15.7 us  [swap_all(): return lax.all_to_all(spread, AXES, 0, 0, tiled=True)]
    broadcast_in_dim x2 -> x0, local copies, waits for them, and re-layouts: 2.23 us -> none  [gather_small(): spread = jnp.broadcast_to(values[None], (count,) + values.shape)]
    pallas_call x4, Pallas kernels: 45.1 us -> 43.2 us  [the longest x1 14.5 us: backward(): pl.pallas_call(backward_kernel, grid=(4,), in_specs=[smem(), whole(body.s...]
where the time goes in v3:
time: 161 us; the launch traced here: 158 us
  Pallas kernels  72.9 us (45%)
  starting transfers between devices  41.4 us (26%)
  waiting for transfers between devices  21.3 us (13%)
  blocking collectives  15.7 us (10%)
  local copies, waits for them, and re-layouts  5.8 us (4%)
    ppermute x8, starting transfers between devices, swap(): return lax.ppermute(values, axis, pairs)  15.9 us
    all_to_all x1, blocking collectives, swap_all(): return lax.all_to_all(spread, AXES, 0, 0, tiled=True)  15.7 us
    ppermute x8, waiting for transfers between devices, swap(): return lax.ppermute(values, axis, pairs)  14.8 us
    pallas_call x1, Pallas kernels, backward(): pl.pallas_call(backward_kernel, grid=(4,), in_specs=[smem(), whole(body.s...  14.5 us
    pallas_call x1, Pallas kernels, forward(): pl.pallas_call(forward_kernel, grid=(4,), in_specs=[smem(), whole(body.sh...  13 us
    pallas_call x1, Pallas kernels, weight_terms(): pl.pallas_call(weight_kernel, grid=(4,), in_specs=[smem(), whole(body.sha...  12.3 us
    all_to_all x1, starting transfers between devices, swap_all(): return lax.all_to_all(spread, AXES, 0, 0, tiled=True)  11.9 us
    all_to_all x1, starting transfers between devices, gather_large(): return lax.all_to_all(spread, AXES, 0, 0, tiled=True).reshape(-1, 128)  7.37 us
  transfers between devices with their start and end apart: 11, of which 7 were waited for; matrix products, arithmetic and copies ran while one was open for 1% of the time, Pallas kernels for 23%

profile of v3, /device:TPU:7, one launch (start us, length us, event | category | flops | bytes accessed | tf_op | source)
XLA Modules:
  0.0 158.0 jit_solution(5916010188321948440)
XLA Ops:
  0.6 6.8 %pack_features.1 = (bf16[1536,512]{1,0:T(8,128)(2,1)}, f32[16,1,512]{2,1,0:T(1,128)}, bf16[112,512]{1,0:T(8,128)(2,1)}, bf16[112,512]{1,0:T(8,128)(2,1)}, bf16[1...) custom-call(s32[1,1,8]{2,1,0:T(1,128)} %live_ref.11, bf16[16,16,96,128]{3,2,1,0:T(8,128)(2,1)} %feat_ref.1, ...), custom_call_target="tpu_custom_call" | custom-call | tf_op jit(solution)/shard_map/pack_features/pallas_call | solution.py:158
  7.5 0.8 collective-permute-start
  8.3 3.1 %collective-permute-start.1 = (bf16[112,512]{1,0:T(8,128)(2,1)}, bf16[112,512]{1,0:T(8,128)(2,1)S(1)}, u32[]{:S(2)}, u32[]{:S(2)}) collective-permute-start(bf16[112,512]{1,0:T(8,128)(2,1)} %get-tuple-element.40), channel_id=1, source_target_pairs={{16,32},{32,16},{48,64},{64,48},{80,96},{96,80},{17,33},{33,17},{4... | collective-permute-start | bytes 344072 | tf_op jit(solution)/shard_map/ppermute | solution.py:255
  11.4 2.7 %arrange.1 = (bf16[288,864]{1,0:T(8,128)(2,1)}, bf16[288,864]{1,0:T(8,128)(2,1)}) custom-call(bf16[27,96,96]{2,1,0:T(8,128)(2,1)} %weight_ref.1), custom_call_target="tpu_custom_call" | custom-call | tf_op jit(solution)/shard_map/arrange/pallas_call | solution.py:745
  15.2 1.9 %relay.2 = (bf16[112,640]{1,0:T(8,128)(2,1)}, bf16[112,640]{1,0:T(8,128)(2,1)}) custom-call(bf16[112,512]{1,0:T(8,128)(2,1)} %copy-done.2, bf16[112,512]{1,0:T(8,128)(2,1)} %copy-done.3, bf16[112,512]{1,0:T(8,128)(2,1)} %get-tuple-element.45.ya, bf16[112,512]{1,0:T(8,128)(2,1)} %get-tuple-element.46.yb), custom_call_target="tpu_custom_call" | custom-call | tf_op jit(solution)/shard_map/relay/pallas_call | solution.py:238
  17.6 4.1 %collective-permute-start.3 = (bf16[112,640]{1,0:T(8,128)(2,1)}, bf16[112,640]{1,0:T(8,128)(2,1)S(1)}, u32[]{:S(2)}, u32[]{:S(2)}) collective-permute-start(bf16[112,640]{1,0:T(8,128)(2,1)} %get-tuple-element.48), channel_id=1, source_target_pairs={{1,2},{2,1},{3,4},{4,3},{5,6},{6,5},{7,8},{8,7},{9,10},{10,9},{11,... | collective-permute-start | bytes 430088 | tf_op jit(solution)/shard_map/ppermute | solution.py:255
  21.8 4.0 %collective-permute-done.3.refs_3_ = bf16[112,640]{1,0:T(8,128)(2,1)S(1)} collective-permute-done((bf16[112,640]{1,0:T(8,128)(2,1)}, bf16[112,640]{1,0:T(8,128)(2,1)S(1)}, u32[]{:S(2)}, u32[]{:S(2)}) %collective-permute-start.3) | collective-permute-done | bytes 143392 | tf_op jit(solution)/shard_map/ppermute | solution.py:255
  25.8 0.7 copy-done.5
  26.5 13.0 %forward.1 = (f32[1536,512]{1,0:T(8,128)}, f32[128,2,128]{2,1,0:T(2,128)}) custom-call(s32[1,1,8]{2,1,0:T(1,128)} %live_ref.11, bf16[1536,512]{1,0:T(8,128)(2,1)} %get-tuple-element.38.body_ref, bf16[112,512]{1,0:T(8,128)(2,1)} %copy-done.2, bf16[112,512]{1,0:T(8,128)(2,1)} %copy-done.3, bf16[112,640]{1,0:T(8,128)(2,1)} %copy-done.4, ...), custom_call_target="tpu_custom_call" | custom-call | tf_op jit(solution)/shard_map/forward/pallas_call | solution.py:475
  39.5 11.9 %all-to-all-start = ((f32[128,2,128]{2,1,0:T(2,128)}), f32[128,2,128]{2,1,0:T(2,128)S(1)}, u32[]{:S(2)}, u32[]{:S(2)}) async-start(f32[128,2,128]{2,1,0:T(2,128)} %get-tuple-element.52), calls=%async_computation | async-start | bytes 262144 | tf_op jit(solution)/shard_map/all_to_all | solution.py:756
  51.9 5.0 %pack_cotangent.1.cot_ref = bf16[1536,512]{1,0:T(8,128)(2,1)} custom-call(s32[1,1,8]{2,1,0:T(1,128)} %live_ref.11, bf16[16,16,96,128]{3,2,1,0:T(8,128)(2,1)} %feat_ref.2), custom_call_target="tpu_custom_call" | custom-call | tf_op jit(solution)/shard_map/pack_cotangent/pallas_call | solution.py:200
  56.9 2.6 %all-to-all-done.stat_ref = f32[128,2,128]{2,1,0:T(2,128)S(1)} async-done(((f32[128,2,128]{2,1,0:T(2,128)}), f32[128,2,128]{2,1,0:T(2,128)S(1)}, u32[]{:S(2)}, u32[]{:S(2)}) %all-to-all-start) | async-done | bytes 131104 | tf_op jit(solution)/shard_map/all_to_all | solution.py:756
  59.6 0.7 copy-done.1
  60.2 5.1 %slope.1 = f32[128,2,128]{2,1,0:T(2,128)} custom-call(f32[128,2,128]{2,1,0:T(2,128)} %copy-done.1, f32[1536,512]{1,0:T(8,128)} %get-tuple-element.53.pre_ref, bf16[1536,512]{1,0:T(8,128)(2,1)} %pack_cotangent.1.cot_ref, f32[16,1,512]{2,1,0:T(1,128)} %get-tuple-element.50.refs_5_.mask_ref, f32[1,128]{1,0:T(1,128)} %get-tuple-element.75.gain_ref.refs_0_, ...), custom_call_target="tpu_custom_call" | custom-call | tf_op jit(solution)/shard_map/slope/pallas_call | solution.py:543
  65.3 15.7 %all_to_all.20.stat2_ref = f32[128,2,128]{2,1,0:T(2,128)} all-to-all(f32[128,2,128]{2,1,0:T(2,128)} %slope.1), channel_id=1, replica_groups=mesh['gx'=8,'gy'=16] {'gx','gy'}, dimensions={0} | all-to-all | bytes 262144 | tf_op jit(solution)/shard_map/all_to_all | solution.py:756
  81.0 6.2 %pre_grad.1 = (bf16[1536,512]{1,0:T(8,128)(2,1)}, f32[8,128]{1,0:T(8,128)}, bf16[112,512]{1,0:T(8,128)(2,1)}, bf16[112,512]{1,0:T(8,128)(2,1)}, bf16[112,512]{1,0:T(8,128)(2,1)}, /*index=5*/bf16[112,512]{1,0:T(8,128)(2,1)}) custom-call(s32[1,1,8]{2,1,0:T(1,128)} %live_ref.11, f32[128,2,128]{2,1,0:T(2,128)} %copy-done.1, ...), custom_call_target="tpu_custom_call" | custom-call | tf_op jit(solution)/shard_map/pre_grad/pallas_call | solution.py:598
  87.2 0.9 collective-permute-start.4
  88.1 2.1 %collective-permute-start.5 = (bf16[112,512]{1,0:T(8,128)(2,1)}, bf16[112,512]{1,0:T(8,128)(2,1)S(1)}, u32[]{:S(2)}, u32[]{:S(2)}) collective-permute-start(bf16[112,512]{1,0:T(8,128)(2,1)} %get-tuple-element.57), channel_id=1, source_target_pairs={{16,32},{32,16},{48,64},{64,48},{80,96},{96,80},{17,33},{33,17},{4... | collective-permute-start | bytes 344072 | tf_op jit(solution)/shard_map/ppermute | solution.py:255
  90.2 12.3 %weight_terms.1 = f32[2048,128]{1,0:T(8,128)} custom-call(s32[1,1,8]{2,1,0:T(1,128)} %live_ref.11, bf16[1536,512]{1,0:T(8,128)(2,1)} %get-tuple-element.38.body_ref, bf16[112,512]{1,0:T(8,128)(2,1)} %copy-done.2, bf16[112,512]{1,0:T(8,128)(2,1)} %copy-done.3, bf16[112,640]{1,0:T(8,128)(2,1)} %copy-done.4, bf16[112,640]{1,0:T(8,128)(2,1)} %copy-done.5, ...), custom_call_target="tpu_custom_call" | custom-call | tf_op jit(solution)/shard_map/weight_terms/pallas_call | solution.py:652
  102.6 6.1 %all-to-all-start.2 = ((f32[128,16,128]{2,1,0:T(8,128)}), f32[128,16,128]{2,1,0:T(8,128)S(1)}, u32[]{:S(2)}, u32[]{:S(2)}) async-start(f32[128,16,128]{2,1,0:T(8,128)} %bitcast.10), calls=%async_computation.2 | async-start | bytes 2097152 | tf_op jit(solution)/shard_map/all_to_all | solution.py:762
  108.7 1.9 %relay.3 = (bf16[112,640]{1,0:T(8,128)(2,1)}, bf16[112,640]{1,0:T(8,128)(2,1)}) custom-call(bf16[112,512]{1,0:T(8,128)(2,1)} %copy-done.6, bf16[112,512]{1,0:T(8,128)(2,1)} %copy-done.7, bf16[112,512]{1,0:T(8,128)(2,1)} %get-tuple-element.61.ya, bf16[112,512]{1,0:T(8,128)(2,1)} %get-tuple-element.62.yb), custom_call_target="tpu_custom_call" | custom-call | tf_op jit(solution)/shard_map/relay/pallas_call | solution.py:238
  111.2 3.8 %collective-permute-start.7 = (bf16[112,640]{1,0:T(8,128)(2,1)}, bf16[112,640]{1,0:T(8,128)(2,1)S(1)}, u32[]{:S(2)}, u32[]{:S(2)}) collective-permute-start(bf16[112,640]{1,0:T(8,128)(2,1)} %get-tuple-element.64), channel_id=1, source_target_pairs={{1,2},{2,1},{3,4},{4,3},{5,6},{6,5},{7,8},{8,7},{9,10},{10,9},{11,... | collective-permute-start | bytes 430088 | tf_op jit(solution)/shard_map/ppermute | solution.py:255
  115.0 8.7 %collective-permute-done.6.refs_2_ = bf16[112,640]{1,0:T(8,128)(2,1)S(1)} collective-permute-done((bf16[112,640]{1,0:T(8,128)(2,1)}, bf16[112,640]{1,0:T(8,128)(2,1)S(1)}, u32[]{:S(2)}, u32[]{:S(2)}) %collective-permute-start.6) | collective-permute-done | bytes 143392 | tf_op jit(solution)/shard_map/ppermute | solution.py:255
  123.7 1.7 %collective-permute-done.7.refs_3_ = bf16[112,640]{1,0:T(8,128)(2,1)S(1)} collective-permute-done((bf16[112,640]{1,0:T(8,128)(2,1)}, bf16[112,640]{1,0:T(8,128)(2,1)S(1)}, u32[]{:S(2)}, u32[]{:S(2)}) %collective-permute-start.7) | collective-permute-done | bytes 143392 | tf_op jit(solution)/shard_map/ppermute | solution.py:255
  125.4 1.6 %all-to-all-done.2 = f32[128,16,128]{2,1,0:T(8,128)S(1)} async-done(((f32[128,16,128]{2,1,0:T(8,128)}), f32[128,16,128]{2,1,0:T(8,128)S(1)}, u32[]{:S(2)}, u32[]{:S(2)}) %all-to-all-start.2) | async-done | bytes 1048608 | tf_op jit(solution)/shard_map/all_to_all | solution.py:762
  127.1 1.0 broadcast_in_dim.14
  128.2 7.4 %all-to-all-start.3 = ((f32[128,16,128]{2,1,0:T(8,128)}), f32[128,16,128]{2,1,0:T(8,128)S(1)}, u32[]{:S(2)}, u32[]{:S(2)}) async-start(f32[128,16,128]{2,1,0:T(8,128)} %broadcast_in_dim.14), calls=%async_computation.3 | async-start | bytes 2097152 | tf_op jit(solution)/shard_map/all_to_all | solution.py:768
  135.5 1.3 slice_bitcast_fusion
  136.8 14.5 %backward.1 = bf16[16,16,96,128]{3,2,1,0:T(8,128)(2,1)} custom-call(s32[1,1,8]{2,1,0:T(1,128)} %live_ref.11, bf16[1536,512]{1,0:T(8,128)(2,1)} %get-tuple-element.55.refs_4_.body_ref, bf16[112,512]{1,0:T(8,128)(2,1)} %copy-done.6, bf16[112,512]{1,0:T(8,128)(2,1)} %copy-done.7, bf16[112,640]{1,0:T(8,128)(2,1)} %copy-done.8, bf16[112,640]{1,0:T(8,128)(2,1)} %copy-done.9, ...), custom_call_target="tpu_custom_call" | custom-call | tf_op jit(solution)/shard_map/backward/pallas_call | solution.py:694
  151.4 2.2 %all-to-all-done.3 = f32[128,16,128]{2,1,0:T(8,128)S(1)} async-done(((f32[128,16,128]{2,1,0:T(8,128)}), f32[128,16,128]{2,1,0:T(8,128)S(1)}, u32[]{:S(2)}, u32[]{:S(2)}) %all-to-all-start.3) | async-done | bytes 1048608 | tf_op jit(solution)/shard_map/all_to_all | solution.py:768
  153.6 1.0 copy-done
  154.6 3.4 %finish.1 = f32[27,96,96]{2,1,0:T(8,128)} custom-call(f32[2048,128]{1,0:T(8,128)} %bitcast.11, f32[8,128]{1,0:T(8,128)} %get-tuple-element.71.small_ref), custom_call_target="tpu_custom_call" | custom-call | tf_op jit(solution)/shard_map/finish/pallas_call | solution.py:725
  (30 shorter events, 2.9 us)
Async XLA Ops:
  7.5 43.9 %copy-start.10 = (f32[96]{0:T(128)S(1)}, f32[96]{0:T(128)}, u32[]{:S(2)}) copy-start(f32[96]{0:T(128)} %param.11) | copy-start | bytes 1156
  7.5 43.9 %copy-start.11 = (f32[96]{0:T(128)S(1)}, f32[96]{0:T(128)}, u32[]{:S(2)}) copy-start(f32[96]{0:T(128)} %param.10) | copy-start | bytes 1156
  7.5 6.6 %collective-permute-start = (bf16[112,512]{1,0:T(8,128)(2,1)}, bf16[112,512]{1,0:T(8,128)(2,1)S(1)}, u32[]{:S(2)}, u32[]{:S(2)}) collective-permute-start(bf16[112,512]{1,0:T(8,128)(2,1)} %get-tuple-element.39), channel_id=1, source_target_pairs={{0,16},{16,0},{32,48},{48,32},{64,80},{80,64},{96,112},{112,96},{1... | collective-permute-start | bytes 344072 | tf_op jit(solution)/shard_map/ppermute | solution.py:255
  8.3 6.3 %collective-permute-start.1 = (bf16[112,512]{1,0:T(8,128)(2,1)}, bf16[112,512]{1,0:T(8,128)(2,1)S(1)}, u32[]{:S(2)}, u32[]{:S(2)}) collective-permute-start(bf16[112,512]{1,0:T(8,128)(2,1)} %get-tuple-element.40), channel_id=1, source_target_pairs={{16,32},{32,16},{48,64},{64,48},{80,96},{96,80},{17,33},{33,17},{4... | collective-permute-start | bytes 344072 | tf_op jit(solution)/shard_map/ppermute | solution.py:255
  14.1 0.6 copy-start.2
  14.6 0.6 copy-start.3
  17.1 4.7 %collective-permute-start.2 = (bf16[112,640]{1,0:T(8,128)(2,1)}, bf16[112,640]{1,0:T(8,128)(2,1)S(1)}, u32[]{:S(2)}, u32[]{:S(2)}) collective-permute-start(bf16[112,640]{1,0:T(8,128)(2,1)} %get-tuple-element.47), channel_id=1, source_target_pairs={{0,1},{1,0},{2,3},{3,2},{4,5},{5,4},{6,7},{7,6},{8,9},{9,8},{10,11... | collective-permute-start | bytes 430088 | tf_op jit(solution)/shard_map/ppermute | solution.py:255
  17.6 8.2 %collective-permute-start.3 = (bf16[112,640]{1,0:T(8,128)(2,1)}, bf16[112,640]{1,0:T(8,128)(2,1)S(1)}, u32[]{:S(2)}, u32[]{:S(2)}) collective-permute-start(bf16[112,640]{1,0:T(8,128)(2,1)} %get-tuple-element.48), channel_id=1, source_target_pairs={{1,2},{2,1},{3,4},{4,3},{5,6},{6,5},{7,8},{8,7},{9,10},{10,9},{11,... | collective-permute-start | bytes 430088 | tf_op jit(solution)/shard_map/ppermute | solution.py:255
  21.8 4.0 %copy-start.4 = (bf16[112,640]{1,0:T(8,128)(2,1)}, bf16[112,640]{1,0:T(8,128)(2,1)S(1)}, u32[]{:S(2)}) copy-start(bf16[112,640]{1,0:T(8,128)(2,1)S(1)} %collective-permute-done.2.refs_2_) | copy-start | bytes 430084
  25.8 0.7 copy-start.5
  39.5 20.1 %all-to-all-start = ((f32[128,2,128]{2,1,0:T(2,128)}), f32[128,2,128]{2,1,0:T(2,128)S(1)}, u32[]{:S(2)}, u32[]{:S(2)}) async-start(f32[128,2,128]{2,1,0:T(2,128)} %get-tuple-element.52), calls=%async_computation | async-start | bytes 262144 | tf_op jit(solution)/shard_map/all_to_all | solution.py:756
  59.6 0.7 copy-start.1
  87.2 15.3 %collective-permute-start.4 = (bf16[112,512]{1,0:T(8,128)(2,1)}, bf16[112,512]{1,0:T(8,128)(2,1)S(1)}, u32[]{:S(2)}, u32[]{:S(2)}) collective-permute-start(bf16[112,512]{1,0:T(8,128)(2,1)} %get-tuple-element.56), channel_id=1, source_target_pairs={{0,16},{16,0},{32,48},{48,32},{64,80},{80,64},{96,112},{112,96},{1... | collective-permute-start | bytes 344072 | tf_op jit(solution)/shard_map/ppermute | solution.py:255
  88.1 14.4 %collective-permute-start.5 = (bf16[112,512]{1,0:T(8,128)(2,1)}, bf16[112,512]{1,0:T(8,128)(2,1)S(1)}, u32[]{:S(2)}, u32[]{:S(2)}) collective-permute-start(bf16[112,512]{1,0:T(8,128)(2,1)} %get-tuple-element.57), channel_id=1, source_target_pairs={{16,32},{32,16},{48,64},{64,48},{80,96},{96,80},{17,33},{33,17},{4... | collective-permute-start | bytes 344072 | tf_op jit(solution)/shard_map/ppermute | solution.py:255
  102.5 6.2 %copy-start.6 = (bf16[112,512]{1,0:T(8,128)(2,1)}, bf16[112,512]{1,0:T(8,128)(2,1)S(1)}, u32[]{:S(2)}) copy-start(bf16[112,512]{1,0:T(8,128)(2,1)S(1)} %collective-permute-done.4.xa.refs_0_) | copy-start | bytes 344068
  102.5 6.2 %copy-start.7 = (bf16[112,512]{1,0:T(8,128)(2,1)}, bf16[112,512]{1,0:T(8,128)(2,1)S(1)}, u32[]{:S(2)}) copy-start(bf16[112,512]{1,0:T(8,128)(2,1)S(1)} %collective-permute-done.5.xb.refs_1_) | copy-start | bytes 344068
  102.6 24.4 %all-to-all-start.2 = ((f32[128,16,128]{2,1,0:T(8,128)}), f32[128,16,128]{2,1,0:T(8,128)S(1)}, u32[]{:S(2)}, u32[]{:S(2)}) async-start(f32[128,16,128]{2,1,0:T(8,128)} %bitcast.10), calls=%async_computation.2 | async-start | bytes 2097152 | tf_op jit(solution)/shard_map/all_to_all | solution.py:762
  110.6 13.1 %collective-permute-start.6 = (bf16[112,640]{1,0:T(8,128)(2,1)}, bf16[112,640]{1,0:T(8,128)(2,1)S(1)}, u32[]{:S(2)}, u32[]{:S(2)}) collective-permute-start(bf16[112,640]{1,0:T(8,128)(2,1)} %get-tuple-element.63), channel_id=1, source_target_pairs={{0,1},{1,0},{2,3},{3,2},{4,5},{5,4},{6,7},{7,6},{8,9},{9,8},{10,11... | collective-permute-start | bytes 430088 | tf_op jit(solution)/shard_map/ppermute | solution.py:255
  111.2 14.2 %collective-permute-start.7 = (bf16[112,640]{1,0:T(8,128)(2,1)}, bf16[112,640]{1,0:T(8,128)(2,1)S(1)}, u32[]{:S(2)}, u32[]{:S(2)}) collective-permute-start(bf16[112,640]{1,0:T(8,128)(2,1)} %get-tuple-element.64), channel_id=1, source_target_pairs={{1,2},{2,1},{3,4},{4,3},{5,6},{6,5},{7,8},{8,7},{9,10},{10,9},{11,... | collective-permute-start | bytes 430088 | tf_op jit(solution)/shard_map/ppermute | solution.py:255
  123.7 13.1 %copy-start.8 = (bf16[112,640]{1,0:T(8,128)(2,1)}, bf16[112,640]{1,0:T(8,128)(2,1)S(1)}, u32[]{:S(2)}) copy-start(bf16[112,640]{1,0:T(8,128)(2,1)S(1)} %collective-permute-done.6.refs_2_) | copy-start | bytes 430084
  125.4 11.5 %copy-start.9 = (bf16[112,640]{1,0:T(8,128)(2,1)}, bf16[112,640]{1,0:T(8,128)(2,1)S(1)}, u32[]{:S(2)}) copy-start(bf16[112,640]{1,0:T(8,128)(2,1)S(1)} %collective-permute-done.7.refs_3_) | copy-start | bytes 430084
  128.2 25.4 %all-to-all-start.3 = ((f32[128,16,128]{2,1,0:T(8,128)}), f32[128,16,128]{2,1,0:T(8,128)S(1)}, u32[]{:S(2)}, u32[]{:S(2)}) async-start(f32[128,16,128]{2,1,0:T(8,128)} %broadcast_in_dim.14), calls=%async_computation.3 | async-start | bytes 2097152 | tf_op jit(solution)/shard_map/all_to_all | solution.py:768
  153.6 1.0 copy-start

commit v4 on v3

--- a/solution.py
+++ b/solution.py
@@ -255,13 +255,17 @@
     return lax.ppermute(values, axis, pairs)
 
 
-def exchange(sides, beside):
+def exchange(sides, beside, then):
     xa, xb, ya, yb = sides
     xa = swap(xa, "gx", True)
     xb = swap(xb, "gx", False)
     xa, xb, beside = lax.optimization_barrier((xa, xb, beside))
     ya, yb = relay(xa, xb, ya, yb)
-    return (xa, xb, swap(ya, "gy", True), swap(yb, "gy", False)), beside
+    made = then(beside)
+    ya = swap(ya, "gy", True)
+    yb = swap(yb, "gy", False)
+    ya, yb, made = lax.optimization_barrier((ya, yb, made))
+    return (xa, xb, ya, yb), made
 
 
 HALO = [(EDGE, W2), (EDGE, W2), (EDGE, 640), (EDGE, 640)]
@@ -620,9 +624,9 @@
     )(live, stats, stats2, pre, cot, mask, gain, shift)
 
 
-def weight_kernel(live_ref, body_ref, *refs):
-    halo, (grad_ref, out_ref) = refs[:4], refs[4:6]
-    edge_ref, rows_ref, cols_ref, padded, total = refs[6:]
+def weight_kernel(pairs, live_ref, body_ref, *refs):
+    halo, (grad_ref, mine_ref, other_ref) = refs[:4], refs[4:7]
+    edge_ref, rows_ref, cols_ref, padded, total, line = refs[7:]
     t = pl.program_id(0)
 
     @pl.when(t == 0)
@@ -643,20 +647,26 @@
     @pl.when(t == 3)
     def _():
         for j in range(6):
-            out_ref[j * 288 : (j + 1) * 288, :] = total[:, j * 128 : (j + 1) * 128]
-        out_ref[6 * 288 : 2048, :] = jnp.zeros((2048 - 6 * 288, 128), F32)
-        out_ref[6 * 288 : 7 * 288, 0:96] = total[:, 768:864]
+            line[j * 288 : (j + 1) * 288, :] = total[:, j * 128 : (j + 1) * 128]
+        line[6 * 288 : 2048, :] = jnp.zeros((2048 - 6 * 288, 128), F32)
+        line[6 * 288 : 7 * 288, 0:96] = total[:, 768:864]
+        odd = lax.axis_index("gx") % 2
+        span = mine_ref.shape[0] // pairs
+        for a in range(pairs):
+            for ref, k in ((mine_ref, odd), (other_ref, 1 - odd)):
+                rows = pl.ds(pl.multiple_of((2 * a + k) * span, span), span)
+                ref[a * span : (a + 1) * span, :] = line[rows, :]
 
 
 def weight_terms(live, body, halo, grad):
     return pl.pallas_call(
-        weight_kernel,
+        functools.partial(weight_kernel, lax.axis_size("gx") // 2),
         grid=(4,),
         in_specs=[smem(), whole(body.shape)] + [whole(h) for h in HALO] + [whole(grad.shape)],
-        out_specs=whole((2048, 128)),
-        out_shape=jax.ShapeDtypeStruct((2048, 128), F32),
+        out_specs=[whole((1024, 128))] * 2,
+        out_shape=[jax.ShapeDtypeStruct((1024, 128), F32)] * 2,
         scratch_shapes=ASSEMBLY
-        + [pltpu.VMEM((ROWS, W2), BF16), pltpu.VMEM((3 * C, 9 * C), F32)],
+        + [pltpu.VMEM((ROWS, W2), BF16), pltpu.VMEM((3 * C, 9 * C), F32), pltpu.VMEM((2048, 128), F32)],
         compiler_params=params(),
         name="weight_terms",
     )(live, body, *halo, grad)
@@ -705,7 +715,9 @@
     )(live, body, *halo, weight, mask)
 
 
-def finish_kernel(sum_ref, small_ref, out_ref):
+def finish_kernel(sum_ref, small_ref, out_ref, gain_out, shift_out):
+    gain_out[...] = small_ref[0:1, 0:C]
+    shift_out[...] = small_ref[1:2, 0:C]
     base = pl.multiple_of((2 - pl.program_id(0)) * C, C)
     root = small_ref[2:3, 0:C]
     for k in range(9):
@@ -726,8 +738,9 @@
         finish_kernel,
         grid=(3,),
         in_specs=[whole(sums.shape), whole(small.shape)],
-        out_specs=pl.BlockSpec((9, C, C), lambda a: (a, 0, 0)),
-        out_shape=jax.ShapeDtypeStruct((27, C, C), F32),
+        out_specs=[pl.BlockSpec((9, C, C), lambda a: (a, 0, 0)), whole((1, C)), whole((1, C))],
+        out_shape=[jax.ShapeDtypeStruct((27, C, C), F32)]
+        + [jax.ShapeDtypeStruct((1, C), F32)] * 2,
         compiler_params=params(),
         name="finish",
     )(sums, small)
@@ -756,15 +769,22 @@
     return lax.all_to_all(spread, AXES, 0, 0, tiled=True)
 
 
-def scatter_large(values):
-    count = lax.axis_size("gx") * lax.axis_size("gy")
-    parts = values.reshape(count, values.shape[0] // count, 128)
-    return lax.all_to_all(parts, AXES, 0, 0, tiled=True)
+def sum_pair(terms):
+    mine, other = terms
+    return scatter_large(mine + swap(other, "gx", True))
+
+
+def scatter_large(mine):
+    nx, ny = lax.axis_size("gx"), lax.axis_size("gy")
+    groups = [[i * ny + j for i in range(c, nx, 2) for j in range(ny)] for c in range(2)]
+    count = nx * ny // 2
+    parts = mine.reshape(count, mine.shape[0] // count, 128)
+    return lax.all_to_all(parts, AXES, 0, 0, tiled=True, axis_index_groups=groups)
 
 
 def gather_large(parts):
-    mine = jnp.sum(parts, axis=0)
-    spread = jnp.broadcast_to(mine[None], parts.shape)
+    mine = jnp.sum(parts, axis=0).astype(BF16)
+    spread = jnp.broadcast_to(mine[None], (devices(),) + mine.shape)
     return lax.all_to_all(spread, AXES, 0, 0, tiled=True).reshape(-1, 128)
 
 
@@ -773,24 +793,23 @@
     shift = jnp.pad(bn_shift, (0, 128 - C))[None]
     packed, mask, *sides = pack_features(brick_live, features, voxel_mask)
     weight_rows, weight_back = arrange(weight)
-    halo, (weight_rows, weight_back) = exchange(sides, (weight_rows, weight_back))
+    cot = pack_plain(brick_live, cotangent)
+    halo, ((weight_rows, weight_back), cot) = exchange(
+        sides, (weight_rows, weight_back), lambda beside: (beside, cot)
+    )
     pre, stats = forward(brick_live, packed, halo, weight_rows, mask)
-    cotangent, stats = lax.optimization_barrier((cotangent, stats))
     stats = swap_all(stats)
-    cot = pack_plain(brick_live, cotangent)
     stats2 = slope(stats, pre, cot, mask, gain, shift)
     stats2 = swap_all(stats2)
     grad, small, *grad_sides = pre_grad(
         brick_live, stats, stats2, pre, cot, mask, gain, shift
     )
     terms = weight_terms(brick_live, packed, halo, grad)
-    grad_halo, terms = exchange(grad_sides, terms)
-    parts = scatter_large(terms)
-    parts, grad_halo = lax.optimization_barrier((parts, grad_halo))
+    grad_halo, parts = exchange(grad_sides, terms, sum_pair)
     sums = gather_large(parts)
     input_grad = backward(brick_live, grad, grad_halo, weight_back, mask)
-    weight_grad = finish(sums, small)
-    return input_grad, weight_grad, small[0, :C], small[1, :C]
+    weight_grad, gain_grad, shift_grad = finish(sums, small)
+    return input_grad, weight_grad, gain_grad.reshape(C), shift_grad.reshape(C)
 
 
 def solution(mesh):

time: 161 us -> 156 us (0.969)
  waiting for transfers between devices: 21.3 us -> 15.2 us
  starting transfers between devices: 41.4 us -> 44 us
  other arithmetic: 0.14 us -> 1.98 us
    ppermute x8 -> x9, waiting for transfers between devices: 14.8 us -> 7.54 us  [swap(): return lax.ppermute(values, axis, pairs)]
    all_to_all x1, waiting for transfers between devices: 2.64 us -> 7.63 us  [swap_all(): return lax.all_to_all(spread, AXES, 0, 0, tiled=True)]
    all_to_all x1, starting transfers between devices: 7.37 us -> 10.6 us  [gather_large(): return lax.all_to_all(spread, AXES, 0, 0, tiled=True).reshape(-1, 128)]
    all_to_all x1, waiting for transfers between devices: 2.24 us -> 0.01 us  [gather_large(): return lax.all_to_all(spread, AXES, 0, 0, tiled=True).reshape(-1, 128)]
    add x0 -> x1, other arithmetic: none -> 1.91 us  [sum_pair(): return scatter_large(mine + swap(other, 'gx', True))]
    all_to_all x1, waiting for transfers between devices: 1.63 us -> 0.01 us  [scatter_large(): lax.all_to_all(parts, AXES, 0, 0, tiled=True, axis_index_groups=groups)]
    ppermute x8 -> x9, starting transfers between devices: 15.9 us -> 16 us  [swap(): return lax.ppermute(values, axis, pairs)]
  transfers between devices with their start and end apart: 11 -> 12, of which waited for: 7 -> 5; matrix products, arithmetic and copies ran while one was open for 1% -> 0% of each run, Pallas kernels for 23% -> 24%
where the time goes in v4:
time: 156 us; the launch traced here: 154 us
  Pallas kernels  72.7 us (47%)
  starting transfers between devices  44 us (28%)
  blocking collectives  15.3 us (10%)
  waiting for transfers between devices  15.2 us (10%)
  local copies, waits for them, and re-layouts  4.19 us (3%)
  other arithmetic  1.98 us (1%)
    ppermute x9, starting transfers between devices, swap(): return lax.ppermute(values, axis, pairs)  16 us
    all_to_all x1, blocking collectives, swap_all(): return lax.all_to_all(spread, AXES, 0, 0, tiled=True)  15.3 us
    pallas_call x1, Pallas kernels, backward(): pl.pallas_call(backward_kernel, grid=(4,), in_specs=[smem(), whole(body.s...  14.6 us
    pallas_call x1, Pallas kernels, forward(): pl.pallas_call(forward_kernel, grid=(4,), in_specs=[smem(), whole(body.sh...  13 us
    pallas_call x1, Pallas kernels, weight_terms(): pl.pallas_call(functools.partial(weight_kernel, lax.axis_size('gx') // 2)...  12.4 us
    all_to_all x1, starting transfers between devices, swap_all(): return lax.all_to_all(spread, AXES, 0, 0, tiled=True)  10.9 us
    all_to_all x1, starting transfers between devices, gather_large(): return lax.all_to_all(spread, AXES, 0, 0, tiled=True).reshape(-1, 128)  10.6 us
    all_to_all x1, waiting for transfers between devices, swap_all(): return lax.all_to_all(spread, AXES, 0, 0, tiled=True)  7.63 us
  transfers between devices with their start and end apart: 12, of which 5 were waited for; matrix products, arithmetic and copies ran while one was open for 0% of the time, Pallas kernels for 24%

profile of v4, /device:TPU:7, one launch (start us, length us, event | category | flops | bytes accessed | tf_op | source)
XLA Modules:
  0.0 154.3 jit_solution(9302647884398280206)
XLA Ops:
  0.6 6.8 %pack_features.1 = (bf16[1536,512]{1,0:T(8,128)(2,1)}, f32[16,1,512]{2,1,0:T(1,128)}, bf16[112,512]{1,0:T(8,128)(2,1)}, bf16[112,512]{1,0:T(8,128)(2,1)}, bf16[1...) custom-call(s32[1,1,8]{2,1,0:T(1,128)} %live_ref.11, bf16[16,16,96,128]{3,2,1,0:T(8,128)(2,1)} %feat_ref.2, ...), custom_call_target="tpu_custom_call" | custom-call | tf_op jit(solution)/shard_map/pack_features/pallas_call | solution.py:158
  7.5 0.8 collective-permute-start
  8.2 3.1 %collective-permute-start.1 = (bf16[112,512]{1,0:T(8,128)(2,1)}, bf16[112,512]{1,0:T(8,128)(2,1)S(1)}, u32[]{:S(2)}, u32[]{:S(2)}) collective-permute-start(bf16[112,512]{1,0:T(8,128)(2,1)} %get-tuple-element.47), channel_id=1, source_target_pairs={{16,32},{32,16},{48,64},{64,48},{80,96},{96,80},{17,33},{33,17},{4... | collective-permute-start | bytes 344072 | tf_op jit(solution)/shard_map/ppermute | solution.py:255
  11.3 2.7 %arrange.1 = (bf16[288,864]{1,0:T(8,128)(2,1)}, bf16[288,864]{1,0:T(8,128)(2,1)}) custom-call(bf16[27,96,96]{2,1,0:T(8,128)(2,1)} %weight_ref.1), custom_call_target="tpu_custom_call" | custom-call | tf_op jit(solution)/shard_map/arrange/pallas_call | solution.py:758
  15.2 1.9 %relay.2 = (bf16[112,640]{1,0:T(8,128)(2,1)}, bf16[112,640]{1,0:T(8,128)(2,1)}) custom-call(bf16[112,512]{1,0:T(8,128)(2,1)} %copy-done.2, bf16[112,512]{1,0:T(8,128)(2,1)} %copy-done.3, bf16[112,512]{1,0:T(8,128)(2,1)} %get-tuple-element.52.ya, bf16[112,512]{1,0:T(8,128)(2,1)} %get-tuple-element.53.yb), custom_call_target="tpu_custom_call" | custom-call | tf_op jit(solution)/shard_map/relay/pallas_call | solution.py:238
  17.1 0.5 collective-permute-start.2
  17.6 4.2 %collective-permute-start.3 = (bf16[112,640]{1,0:T(8,128)(2,1)}, bf16[112,640]{1,0:T(8,128)(2,1)S(1)}, u32[]{:S(2)}, u32[]{:S(2)}) collective-permute-start(bf16[112,640]{1,0:T(8,128)(2,1)} %get-tuple-element.55), channel_id=1, source_target_pairs={{1,2},{2,1},{3,4},{4,3},{5,6},{6,5},{7,8},{8,7},{9,10},{10,9},{11,... | collective-permute-start | bytes 430088 | tf_op jit(solution)/shard_map/ppermute | solution.py:255
  21.9 5.0 %pack_cotangent.1.cot_ref = bf16[1536,512]{1,0:T(8,128)(2,1)} custom-call(s32[1,1,8]{2,1,0:T(1,128)} %live_ref.11, bf16[16,16,96,128]{3,2,1,0:T(8,128)(2,1)} %feat_ref.3), custom_call_target="tpu_custom_call" | custom-call | tf_op jit(solution)/shard_map/pack_cotangent/pallas_call | solution.py:200
  26.9 0.7 copy-done.4
  27.6 13.0 %forward.1 = (f32[1536,512]{1,0:T(8,128)}, f32[128,2,128]{2,1,0:T(2,128)}) custom-call(s32[1,1,8]{2,1,0:T(1,128)} %live_ref.11, bf16[1536,512]{1,0:T(8,128)(2,1)} %get-tuple-element.45.body_ref, bf16[112,512]{1,0:T(8,128)(2,1)} %copy-done.2, bf16[112,512]{1,0:T(8,128)(2,1)} %copy-done.3, bf16[112,640]{1,0:T(8,128)(2,1)} %copy-done.4, ...), custom_call_target="tpu_custom_call" | custom-call | tf_op jit(solution)/shard_map/forward/pallas_call | solution.py:479
  40.6 10.9 %all-to-all-start = ((f32[128,2,128]{2,1,0:T(2,128)}), f32[128,2,128]{2,1,0:T(2,128)S(1)}, u32[]{:S(2)}, u32[]{:S(2)}) async-start(f32[128,2,128]{2,1,0:T(2,128)} %get-tuple-element.62), calls=%async_computation | async-start | bytes 262144 | tf_op jit(solution)/shard_map/all_to_all | solution.py:769
  52.1 7.6 %all-to-all-done.stat_ref = f32[128,2,128]{2,1,0:T(2,128)S(1)} async-done(((f32[128,2,128]{2,1,0:T(2,128)}), f32[128,2,128]{2,1,0:T(2,128)S(1)}, u32[]{:S(2)}, u32[]{:S(2)}) %all-to-all-start) | async-done | bytes 131104 | tf_op jit(solution)/shard_map/all_to_all | solution.py:769
  59.7 0.7 copy-done.1
  60.3 5.1 %slope.1 = f32[128,2,128]{2,1,0:T(2,128)} custom-call(f32[128,2,128]{2,1,0:T(2,128)} %copy-done.1, f32[1536,512]{1,0:T(8,128)} %get-tuple-element.63.pre_ref, bf16[1536,512]{1,0:T(8,128)(2,1)} %pack_cotangent.1.cot_ref, f32[16,1,512]{2,1,0:T(1,128)} %get-tuple-element.61.refs_5_.mask_ref, f32[1,128]{1,0:T(1,128)} %get-tuple-element.87.gain_ref.refs_0_, ...), custom_call_target="tpu_custom_call" | custom-call | tf_op jit(solution)/shard_map/slope/pallas_call | solution.py:547
  65.4 15.3 %all_to_all.20.stat2_ref = f32[128,2,128]{2,1,0:T(2,128)} all-to-all(f32[128,2,128]{2,1,0:T(2,128)} %slope.1), channel_id=1, replica_groups=mesh['gx'=8,'gy'=16] {'gx','gy'}, dimensions={0} | all-to-all | bytes 262144 | tf_op jit(solution)/shard_map/all_to_all | solution.py:769
  80.8 6.2 %pre_grad.1 = (bf16[1536,512]{1,0:T(8,128)(2,1)}, f32[8,128]{1,0:T(8,128)}, bf16[112,512]{1,0:T(8,128)(2,1)}, bf16[112,512]{1,0:T(8,128)(2,1)}, bf16[112,512]{1,0:T(8,128)(2,1)}, /*index=5*/bf16[112,512]{1,0:T(8,128)(2,1)}) custom-call(s32[1,1,8]{2,1,0:T(1,128)} %live_ref.11, f32[128,2,128]{2,1,0:T(2,128)} %copy-done.1, ...), custom_call_target="tpu_custom_call" | custom-call | tf_op jit(solution)/shard_map/pre_grad/pallas_call | solution.py:602
  87.0 0.9 collective-permute-start.4
  87.9 2.2 %collective-permute-start.5 = (bf16[112,512]{1,0:T(8,128)(2,1)}, bf16[112,512]{1,0:T(8,128)(2,1)S(1)}, u32[]{:S(2)}, u32[]{:S(2)}) collective-permute-start(bf16[112,512]{1,0:T(8,128)(2,1)} %get-tuple-element.67), channel_id=1, source_target_pairs={{16,32},{32,16},{48,64},{64,48},{80,96},{96,80},{17,33},{33,17},{4... | collective-permute-start | bytes 344072 | tf_op jit(solution)/shard_map/ppermute | solution.py:255
  90.1 12.4 %weight_terms.1 = (f32[1024,128]{1,0:T(8,128)}, f32[1024,128]{1,0:T(8,128)}) custom-call(s32[1,1,8]{2,1,0:T(1,128)} %live_ref.11, bf16[1536,512]{1,0:T(8,128)(2,1)} %get-tuple-element.45.body_ref, bf16[112,512]{1,0:T(8,128)(2,1)} %copy-done.2, bf16[112,512]{1,0:T(8,128)(2,1)} %copy-done.3, bf16[112,640]{1,0:T(8,128)(2,1)} %copy-done.4, ...), custom_call_target="tpu_custom_call" | custom-call | tf_op jit(solution)/shard_map/weight_terms/pallas_call | solution.py:662
  102.6 2.1 %collective-permute-done.8 = f32[1024,128]{1,0:T(8,128)S(1)} collective-permute-done((f32[1024,128]{1,0:T(8,128)}, f32[1024,128]{1,0:T(8,128)S(1)}, u32[]{:S(2)}, u32[]{:S(2)}) %collective-permute-start.8) | collective-permute-done | bytes 524320 | tf_op jit(solution)/shard_map/ppermute | solution.py:255
  104.7 1.9 %add.7 = f32[1024,128]{1,0:T(8,128)} add(f32[1024,128]{1,0:T(8,128)} %get-tuple-element.76, f32[1024,128]{1,0:T(8,128)S(1)} %collective-permute-done.8) | non-fusion elementwise | flops 131072 | bytes 1572864 | tf_op jit(solution)/shard_map/add | solution.py:774
  106.6 6.5 %all-to-all-start.2 = ((f32[64,16,128]{2,1,0:T(8,128)}), f32[64,16,128]{2,1,0:T(8,128)S(1)}, u32[]{:S(2)}, u32[]{:S(2)}) async-start(f32[64,16,128]{2,1,0:T(8,128)} %bitcast.2), calls=%async_computation.2 | async-start | bytes 1048576 | tf_op jit(solution)/shard_map/all_to_all | solution.py:782
  113.2 1.9 %relay.3 = (bf16[112,640]{1,0:T(8,128)(2,1)}, bf16[112,640]{1,0:T(8,128)(2,1)}) custom-call(bf16[112,512]{1,0:T(8,128)(2,1)} %copy-done.6, bf16[112,512]{1,0:T(8,128)(2,1)} %copy-done.7, bf16[112,512]{1,0:T(8,128)(2,1)} %get-tuple-element.72.ya, bf16[112,512]{1,0:T(8,128)(2,1)} %get-tuple-element.73.yb), custom_call_target="tpu_custom_call" | custom-call | tf_op jit(solution)/shard_map/relay/pallas_call | solution.py:238
  115.0 0.6 collective-permute-start.6
  115.6 3.7 %collective-permute-start.7 = (bf16[112,640]{1,0:T(8,128)(2,1)}, bf16[112,640]{1,0:T(8,128)(2,1)S(1)}, u32[]{:S(2)}, u32[]{:S(2)}) collective-permute-start(bf16[112,640]{1,0:T(8,128)(2,1)} %get-tuple-element.75), channel_id=1, source_target_pairs={{1,2},{2,1},{3,4},{4,3},{5,6},{6,5},{7,8},{8,7},{9,10},{10,9},{11,... | collective-permute-start | bytes 430088 | tf_op jit(solution)/shard_map/ppermute | solution.py:255
  119.3 3.1 %collective-permute-done.6.refs_2_ = bf16[112,640]{1,0:T(8,128)(2,1)S(1)} collective-permute-done((bf16[112,640]{1,0:T(8,128)(2,1)}, bf16[112,640]{1,0:T(8,128)(2,1)S(1)}, u32[]{:S(2)}, u32[]{:S(2)}) %collective-permute-start.6) | collective-permute-done | bytes 143392 | tf_op jit(solution)/shard_map/ppermute | solution.py:255
  122.4 1.9 %collective-permute-done.7.refs_3_ = bf16[112,640]{1,0:T(8,128)(2,1)S(1)} collective-permute-done((bf16[112,640]{1,0:T(8,128)(2,1)}, bf16[112,640]{1,0:T(8,128)(2,1)S(1)}, u32[]{:S(2)}, u32[]{:S(2)}) %collective-permute-start.7) | collective-permute-done | bytes 143392 | tf_op jit(solution)/shard_map/ppermute | solution.py:255
  124.4 0.9 broadcast_in_dim.14
  125.2 10.6 %all-to-all-start.3 = ((bf16[128,16,128]{2,1,0:T(8,128)(2,1)}), bf16[128,16,128]{2,1,0:T(8,128)(2,1)S(1)}, u32[]{:S(2)}, u32[]{:S(2)}) async-start(bf16[128,16,128]{2,1,0:T(8,128)(2,1)} %broadcast_in_dim.14), calls=%async_computation.3 | async-start | bytes 1048576 | tf_op jit(solution)/shard_map/all_to_all | solution.py:788
  135.8 14.6 %backward.1 = bf16[16,16,96,128]{3,2,1,0:T(8,128)(2,1)} custom-call(s32[1,1,8]{2,1,0:T(1,128)} %live_ref.11, bf16[1536,512]{1,0:T(8,128)(2,1)} %get-tuple-element.65.refs_4_.body_ref, bf16[112,512]{1,0:T(8,128)(2,1)} %copy-done.6, bf16[112,512]{1,0:T(8,128)(2,1)} %copy-done.7, bf16[112,640]{1,0:T(8,128)(2,1)} %copy-done.8, bf16[112,640]{1,0:T(8,128)(2,1)} %copy-done.9, ...), custom_call_target="tpu_custom_call" | custom-call | tf_op jit(solution)/shard_map/backward/pallas_call | solution.py:704
  150.4 0.8 copy-done
  151.2 3.1 %finish.1 = (f32[27,96,96]{2,1,0:T(8,128)}, f32[1,96]{1,0:T(1,128)}, f32[1,96]{1,0:T(1,128)}) custom-call(bf16[2048,128]{1,0:T(8,128)(2,1)} %bitcast.8, f32[8,128]{1,0:T(8,128)} %get-tuple-element.82.small_ref), custom_call_target="tpu_custom_call" | custom-call | tf_op jit(solution)/shard_map/finish/pallas_call | solution.py:737
  (32 shorter events, 1.9 us)
Async XLA Ops:
  7.5 6.6 %collective-permute-start = (bf16[112,512]{1,0:T(8,128)(2,1)}, bf16[112,512]{1,0:T(8,128)(2,1)S(1)}, u32[]{:S(2)}, u32[]{:S(2)}) collective-permute-start(bf16[112,512]{1,0:T(8,128)(2,1)} %get-tuple-element.46), channel_id=1, source_target_pairs={{0,16},{16,0},{32,48},{48,32},{64,80},{80,64},{96,112},{112,96},{1... | collective-permute-start | bytes 344072 | tf_op jit(solution)/shard_map/ppermute | solution.py:255
  8.2 6.3 %collective-permute-start.1 = (bf16[112,512]{1,0:T(8,128)(2,1)}, bf16[112,512]{1,0:T(8,128)(2,1)S(1)}, u32[]{:S(2)}, u32[]{:S(2)}) collective-permute-start(bf16[112,512]{1,0:T(8,128)(2,1)} %get-tuple-element.47), channel_id=1, source_target_pairs={{16,32},{32,16},{48,64},{64,48},{80,96},{96,80},{17,33},{33,17},{4... | collective-permute-start | bytes 344072 | tf_op jit(solution)/shard_map/ppermute | solution.py:255
  14.1 0.7 copy-start.2
  14.5 0.6 copy-start.3
  17.1 9.8 %collective-permute-start.2 = (bf16[112,640]{1,0:T(8,128)(2,1)}, bf16[112,640]{1,0:T(8,128)(2,1)S(1)}, u32[]{:S(2)}, u32[]{:S(2)}) collective-permute-start(bf16[112,640]{1,0:T(8,128)(2,1)} %get-tuple-element.54), channel_id=1, source_target_pairs={{0,1},{1,0},{2,3},{3,2},{4,5},{5,4},{6,7},{7,6},{8,9},{9,8},{10,11... | collective-permute-start | bytes 430088 | tf_op jit(solution)/shard_map/ppermute | solution.py:255
  17.6 33.9 %copy-start.10 = (f32[96]{0:T(128)S(1)}, f32[96]{0:T(128)}, u32[]{:S(2)}) copy-start(f32[96]{0:T(128)} %param.11) | copy-start | bytes 1156
  17.6 33.9 %copy-start.11 = (f32[96]{0:T(128)S(1)}, f32[96]{0:T(128)}, u32[]{:S(2)}) copy-start(f32[96]{0:T(128)} %param.10) | copy-start | bytes 1156
  17.6 9.3 %collective-permute-start.3 = (bf16[112,640]{1,0:T(8,128)(2,1)}, bf16[112,640]{1,0:T(8,128)(2,1)S(1)}, u32[]{:S(2)}, u32[]{:S(2)}) collective-permute-start(bf16[112,640]{1,0:T(8,128)(2,1)} %get-tuple-element.55), channel_id=1, source_target_pairs={{1,2},{2,1},{3,4},{4,3},{5,6},{6,5},{7,8},{8,7},{9,10},{10,9},{11,... | collective-permute-start | bytes 430088 | tf_op jit(solution)/shard_map/ppermute | solution.py:255
  26.9 0.7 copy-start.4
  26.9 0.7 copy-start.5
  40.6 19.1 %all-to-all-start = ((f32[128,2,128]{2,1,0:T(2,128)}), f32[128,2,128]{2,1,0:T(2,128)S(1)}, u32[]{:S(2)}, u32[]{:S(2)}) async-start(f32[128,2,128]{2,1,0:T(2,128)} %get-tuple-element.62), calls=%async_computation | async-start | bytes 262144 | tf_op jit(solution)/shard_map/all_to_all | solution.py:769
  59.7 0.7 copy-start.1
  87.0 15.5 %collective-permute-start.4 = (bf16[112,512]{1,0:T(8,128)(2,1)}, bf16[112,512]{1,0:T(8,128)(2,1)S(1)}, u32[]{:S(2)}, u32[]{:S(2)}) collective-permute-start(bf16[112,512]{1,0:T(8,128)(2,1)} %get-tuple-element.66), channel_id=1, source_target_pairs={{0,16},{16,0},{32,48},{48,32},{64,80},{80,64},{96,112},{112,96},{1... | collective-permute-start | bytes 344072 | tf_op jit(solution)/shard_map/ppermute | solution.py:255
  87.9 14.6 %collective-permute-start.5 = (bf16[112,512]{1,0:T(8,128)(2,1)}, bf16[112,512]{1,0:T(8,128)(2,1)S(1)}, u32[]{:S(2)}, u32[]{:S(2)}) collective-permute-start(bf16[112,512]{1,0:T(8,128)(2,1)} %get-tuple-element.67), channel_id=1, source_target_pairs={{16,32},{32,16},{48,64},{64,48},{80,96},{96,80},{17,33},{33,17},{4... | collective-permute-start | bytes 344072 | tf_op jit(solution)/shard_map/ppermute | solution.py:255
  102.5 10.7 %copy-start.6 = (bf16[112,512]{1,0:T(8,128)(2,1)}, bf16[112,512]{1,0:T(8,128)(2,1)S(1)}, u32[]{:S(2)}) copy-start(bf16[112,512]{1,0:T(8,128)(2,1)S(1)} %collective-permute-done.4.xa.refs_0_) | copy-start | bytes 344068
  102.5 10.6 %copy-start.7 = (bf16[112,512]{1,0:T(8,128)(2,1)}, bf16[112,512]{1,0:T(8,128)(2,1)S(1)}, u32[]{:S(2)}) copy-start(bf16[112,512]{1,0:T(8,128)(2,1)S(1)} %collective-permute-done.5.xb.refs_1_) | copy-start | bytes 344068
  102.5 2.2 %collective-permute-start.8 = (f32[1024,128]{1,0:T(8,128)}, f32[1024,128]{1,0:T(8,128)S(1)}, u32[]{:S(2)}, u32[]{:S(2)}) collective-permute-start(f32[1024,128]{1,0:T(8,128)} %get-tuple-element.77), channel_id=1, source_target_pairs={{0,16},{16,0},{32,48},{48,32},{64,80},{80,64},{96,112},{112,96},{1... | collective-permute-start | bytes 1572872 | tf_op jit(solution)/shard_map/ppermute | solution.py:255
  106.6 17.6 %all-to-all-start.2 = ((f32[64,16,128]{2,1,0:T(8,128)}), f32[64,16,128]{2,1,0:T(8,128)S(1)}, u32[]{:S(2)}, u32[]{:S(2)}) async-start(f32[64,16,128]{2,1,0:T(8,128)} %bitcast.2), calls=%async_computation.2 | async-start | bytes 1048576 | tf_op jit(solution)/shard_map/all_to_all | solution.py:782
  115.0 7.3 %collective-permute-start.6 = (bf16[112,640]{1,0:T(8,128)(2,1)}, bf16[112,640]{1,0:T(8,128)(2,1)S(1)}, u32[]{:S(2)}, u32[]{:S(2)}) collective-permute-start(bf16[112,640]{1,0:T(8,128)(2,1)} %get-tuple-element.74), channel_id=1, source_target_pairs={{0,1},{1,0},{2,3},{3,2},{4,5},{5,4},{6,7},{7,6},{8,9},{9,8},{10,11... | collective-permute-start | bytes 430088 | tf_op jit(solution)/shard_map/ppermute | solution.py:255
  115.6 8.7 %collective-permute-start.7 = (bf16[112,640]{1,0:T(8,128)(2,1)}, bf16[112,640]{1,0:T(8,128)(2,1)S(1)}, u32[]{:S(2)}, u32[]{:S(2)}) collective-permute-start(bf16[112,640]{1,0:T(8,128)(2,1)} %get-tuple-element.75), channel_id=1, source_target_pairs={{1,2},{2,1},{3,4},{4,3},{5,6},{6,5},{7,8},{8,7},{9,10},{10,9},{11,... | collective-permute-start | bytes 430088 | tf_op jit(solution)/shard_map/ppermute | solution.py:255
  122.4 13.4 %copy-start.8 = (bf16[112,640]{1,0:T(8,128)(2,1)}, bf16[112,640]{1,0:T(8,128)(2,1)S(1)}, u32[]{:S(2)}) copy-start(bf16[112,640]{1,0:T(8,128)(2,1)S(1)} %collective-permute-done.6.refs_2_) | copy-start | bytes 430084
  124.3 11.5 %copy-start.9 = (bf16[112,640]{1,0:T(8,128)(2,1)}, bf16[112,640]{1,0:T(8,128)(2,1)S(1)}, u32[]{:S(2)}) copy-start(bf16[112,640]{1,0:T(8,128)(2,1)S(1)} %collective-permute-done.7.refs_3_) | copy-start | bytes 430084
  125.2 25.2 %all-to-all-start.3 = ((bf16[128,16,128]{2,1,0:T(8,128)(2,1)}), bf16[128,16,128]{2,1,0:T(8,128)(2,1)S(1)}, u32[]{:S(2)}, u32[]{:S(2)}) async-start(bf16[128,16,128]{2,1,0:T(8,128)(2,1)} %broadcast_in_dim.14), calls=%async_computation.3 | async-start | bytes 1048576 | tf_op jit(solution)/shard_map/all_to_all | solution.py:788
  150.4 0.8 copy-start
